TPU v7x, 256 devices: a whole 4x4x8 slice. The times are simulated.
256 devices in a mesh: row: 8 (over y, core), col: 16 (over z_lo, x), dp: 2 (over z_hi).
Axes of the slice: x: 4, y: 4, z: 8 (z_hi: 2, z_lo: 4; z = z_hi * 4 + z_lo), core: 2. Of those that a mesh axis runs over, the one named last changes fastest.
Arguments:
- tokens: bfloat16 [640, 12288], P(('row', 'dp'), 'col'), may hold values from -6 to 6
- w_in: bfloat16 [12288, 24576], P('col', ('row', 'dp')), may hold values from -0.0546875 to 0.0546875
- w_out: bfloat16 [24576, 12288], P(('row', 'dp'), 'col'), may hold values from -0.0390625 to 0.0390625
- grad_out: bfloat16 [640, 12288], P(('row', 'dp'), 'col'), may hold values from -6 to 6
Outputs:
- output: float32 [640, 12288], P(('row', 'dp'), 'col')
- grad_tokens: float32 [640, 12288], P(('row', 'dp'), 'col')
- grad_w_in: bfloat16 [12288, 24576], P('col', ('row', 'dp'))
- grad_w_out: bfloat16 [24576, 12288], P(('row', 'dp'), 'col')
All inputs are finite; a program needn't handle non-finite values.
Results may differ from a plain program's by a relative error of at most 0.0049.
Values may be sent and summed in bfloat16 or wider, within the bound.
No kernel may reach another device: no remote copies, remote signals or barrier semaphores. Data moves between devices by JAX's collectives and lax.ppermute only.
A program may use at most 128 MiB of HBM per device.

v0:
```python
import math

import jax
import jax.numpy as jnp
from jax import lax
from jax.sharding import PartitionSpec as P

gelu_scale = math.sqrt(2.0 / math.pi)
cubic_coef = 0.044715


def gelu_parts(pre_act):
    inner_arg = gelu_scale * (pre_act + cubic_coef * pre_act * pre_act * pre_act)
    tanh_part = jnp.tanh(inner_arg)
    values = 0.5 * pre_act * (1.0 + tanh_part)
    slopes = 0.5 * (1.0 + tanh_part) + 0.5 * pre_act * (
        1.0 - tanh_part * tanh_part
    ) * gelu_scale * (1.0 + 3.0 * cubic_coef * pre_act * pre_act)
    return (values, slopes)


def product(left_side, right_side, left_dim, right_dim):
    return lax.dot_general(
        left_side,
        right_side,
        (((left_dim,), (right_dim,)), ((), ())),
        preferred_element_type=jnp.float32,
    )


def reduce_width(source, weight, contract):
    return lax.psum(product(source, weight, 1, contract), "col")


def reduce_tokens(source, weight, contract):
    return lax.psum_scatter(
        product(source, weight, 1, contract), ("row", "dp"), scatter_dimension=0, tiled=True
    )


def shards(tokens, w_in, w_out, grad_out):
    gathered, gathered_grad = (
        lax.all_gather(tokens, ("row", "dp"), axis=0, tiled=True),
        lax.all_gather(grad_out, ("row", "dp"), axis=0, tiled=True),
    )
    first_block, second_block = (w_in, w_out)
    pre_act = reduce_width(gathered, first_block, 0)
    values, slopes = gelu_parts(pre_act)
    activation = values.astype(jnp.bfloat16)
    output = tokens.astype(jnp.float32) + reduce_tokens(activation, second_block, 0)
    backward = reduce_width(gathered_grad, second_block, 1)
    grad_hidden = (backward * slopes).astype(jnp.bfloat16)
    grad_tokens = grad_out.astype(jnp.float32) + reduce_tokens(grad_hidden, first_block, 1)
    grad_first = product(gathered, grad_hidden, 0, 0)
    grad_second = product(activation, gathered_grad, 0, 0)
    return (output, grad_tokens, grad_first.astype(jnp.bfloat16), grad_second.astype(jnp.bfloat16))


def solution(mesh):
    in_specs = (
        P(("row", "dp"), "col"),
        P("col", ("row", "dp")),
        P(("row", "dp"), "col"),
        P(("row", "dp"), "col"),
    )
    out_specs = (
        P(("row", "dp"), "col"),
        P(("row", "dp"), "col"),
        P("col", ("row", "dp")),
        P(("row", "dp"), "col"),
    )
    return jax.shard_map(shards, mesh=mesh, in_specs=in_specs, out_specs=out_specs, check_vma=False)
```

profile of v0, /device:TPU:1, one launch (start us, length us, event | category | flops | bytes accessed | tf_op | source)
XLA Modules:
  0.0 563.1 jit_solution(17286682845563766836)
XLA Ops:
  7.2 0.0 copy-start
  7.2 0.0 all-reduce.3.cloned.1.call-start
  7.2 82.1 %all_gather.6 = bf16[640,768]{1,0:T(8,128)(2,1)S(1)} all-gather(bf16[40,768]{1,0:T(8,128)(2,1)} %param.4), channel_id=1, replica_groups=mesh['row'=8,'col'=16,'dp'=2] {'row','dp'}, dimensions={0}, use_global_device_ids=true | all-gather | bytes 1044480 | tf_op jit(solution)/shard_map/all_gather | solution.py:43
  89.4 0.0 copy-start.2
  89.4 75.6 %all_gather.7 = bf16[640,768]{1,0:T(8,128)(2,1)S(1)} all-gather(bf16[40,768]{1,0:T(8,128)(2,1)} %param.7), channel_id=1, replica_groups=mesh['row'=8,'col'=16,'dp'=2] {'row','dp'}, dimensions={0}, use_global_device_ids=true | all-gather | bytes 1044480 | tf_op jit(solution)/shard_map/all_gather | solution.py:44
  165.0 5.3 fusion.10
  170.3 0.0 copy-done.2
  170.3 0.0 copy-done
  170.3 3.7 fusion.9
  174.0 0.0 all-reduce.3.cloned.1.call-update
  174.0 0.0 reduce-scatter.5.cloned.1.call-start
  174.1 199.1 %all-reduce.3.cloned.1.call-done = (f32[640,1536]{1,0:T(8,128)}, f32[640,1536]{1,0:T(8,128)}) async-done(((f32[640,1536]{1,0:T(8,128)}, f32[640,1536]{1,0:T(8,128)}), (f32[640,1536]{1,0:T(8,128)}, f32[640,1536]{1,0:T(8,128)})) %all-reduce.3.cloned.1.call-update) | async-done | bytes 7864336 | tf_op jit(solution)/shard_map/psum | solution.py:32
  373.1 4.6 fusion.6
  377.8 0.0 copy-start.1
  377.8 1.3 copy-done.1
  379.1 3.0 fusion.11
  382.1 0.0 reduce-scatter.5.cloned.1.call-update
  382.1 0.0 reduce-scatter.3.cloned.1.call-start
  382.1 6.6 %fusion.8 = f32[640,768]{1,0:T(8,128)} fusion(bf16[1536,768]{1,0:T(8,128)(2,1)} %param.6, f32[640,1536]{1,0:T(8,128)} %get-tuple-element.8), kind=kOutput, calls=%fused_computation.15 | convolution fusion | flops 1518796800 | bytes 8257536 | tf_op jit(solution)/shard_map/dot_general | solution.py:23
  388.7 0.0 reduce-scatter.3.cloned.1.call-update
  388.7 5.2 fusion.7
  394.0 4.3 copy.8
  398.3 0.0 copy-start.3
  398.3 0.0 copy-start.4
  398.3 6.2 %convolution_convert_fusion = bf16[1536,768]{1,0:T(8,128)(2,1)} fusion(bf16[640,768]{1,0:T(8,128)(2,1)S(1)} %all_gather.7, f32[640,1536]{1,0:T(8,128)} %get-tuple-element.8), kind=kOutput, calls=%fused_computation.10 | convolution fusion | flops 1519976448 | bytes 7274496 | tf_op jit(solution)/shard_map/dot_general | solution.py:23
  404.5 63.5 %reduce-scatter.5.cloned.1.call-done = f32[40,768]{1,0:T(8,128)} async-done(((f32[640,768]{1,0:T(8,128)}), f32[40,768]{1,0:T(8,128)}) %reduce-scatter.5.cloned.1.call-update) | async-done | bytes 122896 | tf_op jit(solution)/shard_map/reduce_scatter | solution.py:36
  468.1 0.0 copy-done.3
  468.1 1.6 convert_add_fusion
  469.6 85.4 %reduce-scatter.3.cloned.1.call-done = f32[40,768]{1,0:T(8,128)} async-done(((f32[640,768]{1,0:T(8,128)}), f32[40,768]{1,0:T(8,128)}) %reduce-scatter.3.cloned.1.call-update) | async-done | bytes 122896 | tf_op jit(solution)/shard_map/reduce_scatter | solution.py:36
  555.1 0.0 copy-done.4
  555.1 1.6 convert_add_fusion.1
Async XLA Ops:
  7.2 163.2 %copy-start = (bf16[768,1536]{1,0:T(8,128)(2,1)S(1)}, bf16[768,1536]{1,0:T(8,128)(2,1)}, u32[]{:S(2)}) copy-start(bf16[768,1536]{1,0:T(8,128)(2,1)} %param.5) | copy-start | bytes 7077892
  7.2 366.0 %all-reduce.3.cloned.1.call-start = ((), (), s32[]{:S(2)}) async-start(), calls=%async_computation.4 | async-start | bytes 15728640 | tf_op jit(solution)/shard_map/psum | solution.py:32
  89.4 81.0 %copy-start.2 = (bf16[640,768]{1,0:T(8,128)(2,1)}, bf16[640,768]{1,0:T(8,128)(2,1)S(1)}, u32[]{:S(2)}) copy-start(bf16[640,768]{1,0:T(8,128)(2,1)S(1)} %all_gather.6) | copy-start | bytes 2949124
  174.0 294.0 %reduce-scatter.5.cloned.1.call-start = ((), (), s32[]{:S(2)}) async-start(), calls=%async_computation.3 | async-start | bytes 2088960 | tf_op jit(solution)/shard_map/reduce_scatter | solution.py:36
  377.8 1.3 copy-start.1
  382.1 173.0 %reduce-scatter.3.cloned.1.call-start = ((), (), s32[]{:S(2)}) async-start(), calls=%async_computation.2 | async-start | bytes 2088960 | tf_op jit(solution)/shard_map/reduce_scatter | solution.py:36
  398.3 69.8 %copy-start.3 = (bf16[40,768]{1,0:T(8,128)(2,1)S(1)}, bf16[40,768]{1,0:T(8,128)(2,1)}, u32[]{:S(2)}) copy-start(bf16[40,768]{1,0:T(8,128)(2,1)} %param.7) | copy-start | bytes 184324
  398.3 156.8 %copy-start.4 = (bf16[40,768]{1,0:T(8,128)(2,1)S(1)}, bf16[40,768]{1,0:T(8,128)(2,1)}, u32[]{:S(2)}) copy-start(bf16[40,768]{1,0:T(8,128)(2,1)} %param.4) | copy-start | bytes 184324
Sparse Core Ops, SparseCore 0:
  174.2 198.9 all-reduce.2
  382.2 85.8 reduce-scatter.4
  472.3 82.7 reduce-scatter.2
where the time goes:
time: 564 us; the launch traced here: 563 us
  waiting for transfers between devices  348 us (62%)
  blocking collectives  158 us (28%)
  matrix products  30 us (5%)
  between operations  13.8 us (2%)
  other arithmetic  7.77 us (1%)
    psum x1, waiting for transfers between devices, reduce_width(): return lax.psum(product(source, weight, 1, contract), 'col')  199 us
    reduce_scatter x2, waiting for transfers between devices, reduce_tokens(): lax.psum_scatter(product(source, weight, 1, contract), ('row', 'dp'), sca...  149 us
    all_gather x1, blocking collectives, shards(): lax.all_gather(tokens, ('row', 'dp'), axis=0, tiled=True)  82.1 us
    all_gather x1, blocking collectives, shards(): lax.all_gather(grad_out, ('row', 'dp'), axis=0, tiled=True)  75.6 us
    dot_general x6, matrix products, product(): lax.dot_general(left_side, right_side, (((left_dim,), (right_dim,)), ((),...  30 us
  transfers between devices with their start and end apart: 3, of which 3 were waited for; matrix products, arithmetic and copies ran while one was open for 4% of the time, Pallas kernels for 0%

commit v1 on v0

v1 whole, which is shorter than its diff:
```python
import functools
import math

import jax
import jax.numpy as jnp
from jax import lax
from jax.experimental import pallas as pl
from jax.experimental.pallas import tpu as pltpu
from jax.sharding import Mesh
from jax.sharding import PartitionSpec as P

BF16, F32 = jnp.bfloat16, jnp.float32
GELU_SCALE = math.sqrt(2.0 / math.pi)
CUBIC = 0.044715
VMEM = pl.BlockSpec(memory_space=pltpu.VMEM)
SMEM = pl.BlockSpec(memory_space=pltpu.SMEM)
N = 4


def gelu_parts(v):
    t = jnp.tanh(GELU_SCALE * (v + CUBIC * v * v * v))
    values = 0.5 * v * (1.0 + t)
    slopes = 0.5 * (1.0 + t) + 0.5 * v * (1.0 - t * t) * GELU_SCALE * (
        1.0 + 3.0 * CUBIC * v * v
    )
    return values, slopes


def dot(a, b, contract_a, contract_b):
    return lax.dot_general(
        a, b, (((contract_a,), (contract_b,)), ((), ())), preferred_element_type=F32
    )


def call(body, outs, flops, traffic, *args):
    specs = [SMEM if a.dtype == jnp.int32 else VMEM for a in args]
    return pl.pallas_call(
        body,
        out_shape=[jax.ShapeDtypeStruct(s, d) for s, d in outs],
        in_specs=specs,
        out_specs=[VMEM] * len(outs),
        compiler_params=pltpu.CompilerParams(vmem_limit_bytes=28 << 20),
        cost_estimate=pl.CostEstimate(flops=flops, bytes_accessed=traffic, transcendentals=0),
    )(*args)


def first_products(at, mine, other, w_in, w_out, rows, keep, one, two, three):
    half = mine.shape[2]
    block = 2 * half
    for a in range(2):
        for d in range(N):
            k = lax.rem(at[0] + d, N)
            both = jnp.concatenate([mine[k, a].astype(F32), other[k, a].astype(F32)], axis=0)
            rows[a, d * block : (d + 1) * block] = both.astype(BF16)
    width = 512
    for n in range(w_in.shape[1] // width):
        cut = slice(n * width, (n + 1) * width)
        for a in range(2):
            if a == 0:
                part = dot(rows[0], w_in[:, cut], 1, 0)
            else:
                part = dot(rows[1], w_out[cut, :], 1, 1)
            keep[a, :, cut] = part[:block]
            for d, out in enumerate((one, two, three), 1):
                out[a, :, cut] = part[d * block : (d + 1) * block].astype(BF16)


def add_blocks(at, keep, one, two, three, mine, first, second, third):
    width = mine.shape[2]
    for e, out in enumerate((mine, first, second, third)):
        start = pl.multiple_of(lax.rem(at[1] + e, N) * width, 128)
        cut = pl.ds(start, width)
        for a in range(2):
            total = keep[a, :, cut]
            for got in (one, two, three):
                total = total + got[a, :, cut].astype(F32)
            out[a] = total.astype(out.dtype)


def activate(mine, one, two, three, out):
    def total(a):
        return (
            mine[a] + one[a].astype(F32) + two[a].astype(F32) + three[a].astype(F32)
        )

    values, slopes = gelu_parts(total(0))
    out[0] = values.astype(BF16)
    out[1] = (total(1) * slopes).astype(BF16)


def assemble(at, mine, one, two, three, out):
    width = mine.shape[2]
    for e, got in enumerate((mine, one, two, three)):
        start = pl.multiple_of(lax.rem(at[1] + N - e, N) * width, 128)
        for a in range(2):
            out[a, :, pl.ds(start, width)] = got[a]


def second_products(at, mine, one, two, three, w_in, w_out, hidden, keep, send):
    block = mine.shape[1]
    half = block // 2
    for a in range(2):
        for d, got in enumerate((mine, one, two, three)):
            hidden[a, d * block : (d + 1) * block] = got[a]
    for a in range(2):
        if a == 0:
            part = dot(hidden[0], w_out[...], 1, 0)
        else:
            part = dot(hidden[1], w_in[...], 1, 1)
        for d in range(N):
            k = lax.rem(at[0] + N - d, N)
            keep[k, a] = part[d * block : d * block + half]
            send[k, a] = part[d * block + half : (d + 1) * block].astype(BF16)


def add_halves(keep, got, *outs):
    for k, out in enumerate(outs):
        out[...] = (keep[k] + got[k].astype(F32)).astype(out.dtype)


def weight_grads(rows_own, hidden_own, rows_far, hidden_far, grad_in, grad_out, lhs, rhs):
    block = rows_own.shape[1] // N
    extent = rows_own.shape[1]
    for a in range(2):
        for i, (rows, hidden) in enumerate(((rows_own, hidden_own), (rows_far, hidden_far))):
            for d in range(N):
                f = (N - d) % N
                lhs[a, i * extent + d * block : i * extent + (d + 1) * block] = rows[
                    a, f * block : (f + 1) * block
                ]
            rhs[a, i * extent : (i + 1) * extent] = hidden[a]
    width = 256
    for n in range(grad_in.shape[0] // width):
        cut = slice(n * width, (n + 1) * width)
        grad_in[cut, :] = dot(lhs[0, :, cut], rhs[1], 0, 0).astype(BF16)
    for n in range(grad_out.shape[0] // width):
        cut = slice(n * width, (n + 1) * width)
        grad_out[cut, :] = dot(rhs[0, :, cut], lhs[1], 0, 0).astype(BF16)


def final_sum(tokens, grad_out, base, *rest):
    *parts, output, grad_tokens = rest
    for a, (source, out) in enumerate(((tokens, output), (grad_out, grad_tokens))):
        total = source[...].astype(F32) + base[a]
        for part in parts:
            total = total + part[a].astype(F32)
        out[...] = total


def shift(value, axis, step):
    return lax.ppermute(value, axis, [(i, (i + step) % N) for i in range(N)])


def swap(value, axis):
    return lax.ppermute(value, axis, [(0, 1), (1, 0)])


def shards(tokens, w_in, w_out, grad_out):
    half, width = tokens.shape
    hidden = w_in.shape[1]
    block = 2 * half
    cut = hidden // N
    at = jnp.stack([lax.axis_index("x"), lax.axis_index("zl")]).astype(jnp.int32)
    product_flops = 2 * 2 * N * block * width * hidden

    mine = jnp.stack([tokens, grad_out])
    own = jnp.stack([mine] + [shift(mine, "y", -k) for k in range(1, N)])
    far = swap(own, "zh")

    def middle(gathered):
        rows, keep, *send = call(
            first_products,
            [((2, N * block, width), BF16), ((2, block, hidden), F32)]
            + [((2, block, hidden), BF16)] * 3,
            product_flops,
            12 << 20,
            at, gathered, swap(gathered, "core"), w_in, w_out,
        )
        got = [shift(s, "x", d) for d, s in enumerate(send, 1)]
        keep, *send = call(
            add_blocks,
            [((2, block, cut), F32)] + [((2, block, cut), BF16)] * 3,
            1 << 20,
            4 << 20,
            at, keep, *got,
        )
        got = [shift(s, "zl", e) for e, s in enumerate(send, 1)]
        (piece,) = call(
            activate, [((2, block, cut), BF16)], 4 << 20, 1 << 20, keep, *got
        )
        got = [shift(piece, "zl", e) for e in range(1, N)]
        (wide,) = call(
            assemble, [((2, block, hidden), BF16)], 0, 1 << 20, at, piece, *got
        )
        got = [shift(wide, "x", d) for d in range(1, N)]
        hid, keep, send = call(
            second_products,
            [
                ((2, N * block, hidden), BF16),
                ((N, 2, half, width), F32),
                ((N, 2, half, width), BF16),
            ],
            product_flops,
            12 << 20,
            at, wide, *got, w_in, w_out,
        )
        return rows, hid, keep, swap(send, "core")

    rows_own, hid_own, keep, got = middle(own)
    base, *send = call(
        add_halves,
        [((2, half, width), F32)] + [((2, half, width), BF16)] * 3,
        1 << 18, 2 << 20, keep, got,
    )
    parts = [shift(s, "y", k) for k, s in enumerate(send, 1)]

    rows_far, hid_far, keep, got = middle(far)
    send = call(
        add_halves, [((2, half, width), BF16)] * 4, 1 << 18, 2 << 20, keep, got
    )
    for k, s in enumerate(send):
        pairs = [
            (y * 2 + z, (y + k) % N * 2 + 1 - z) for y in range(N) for z in range(2)
        ]
        parts.append(lax.ppermute(s, ("y", "zh"), pairs))

    grads = pl.pallas_call(
        weight_grads,
        out_shape=[
            jax.ShapeDtypeStruct((width, hidden), BF16),
            jax.ShapeDtypeStruct((hidden, width), BF16),
        ],
        in_specs=[VMEM] * 4,
        out_specs=[VMEM] * 2,
        scratch_shapes=[
            pltpu.VMEM((2, 2 * N * block, width), BF16),
            pltpu.VMEM((2, 2 * N * block, hidden), BF16),
        ],
        compiler_params=pltpu.CompilerParams(vmem_limit_bytes=36 << 20),
        cost_estimate=pl.CostEstimate(
            flops=2 * product_flops, bytes_accessed=12 << 20, transcendentals=0
        ),
    )(rows_own, hid_own, rows_far, hid_far)

    output, grad_tokens = call(
        final_sum,
        [((half, width), F32)] * 2,
        1 << 20, 2 << 20, tokens, grad_out, base, *parts,
    )
    return output, grad_tokens, grads[0], grads[1]


def solution(mesh):
    fine = Mesh(mesh.devices.reshape(4, 2, 4, 4, 2), ("y", "core", "zl", "x", "zh"))
    row, col = ("y", "core", "zh"), ("zl", "x")
    by_token, in_spec, out_spec = P(row, col), P(col, row), P(row, col)
    return jax.shard_map(
        shards,
        mesh=fine,
        in_specs=(by_token, in_spec, out_spec, by_token),
        out_specs=(by_token, by_token, in_spec, out_spec),
        check_vma=False,
    )
```

time: 564 us -> 180 us (0.32)
  waiting for transfers between devices: 348 us -> 84.6 us
  blocking collectives: 158 us -> 0 us
  starting transfers between devices: 0.12 us -> 71.5 us
  matrix products: 30 us -> 0 us
  Pallas kernels: 0 us -> 18.9 us
  between operations: 13.8 us -> 0.76 us
  other arithmetic: 7.77 us -> 1.02 us
    psum x1 -> x0, waiting for transfers between devices: 199 us -> none  [reduce_width(): return lax.psum(product(source, weight, 1, contract), 'col')]
    all_gather x2 -> x0, blocking collectives: 158 us -> none  [the longest x1 82.1 us: shards(): lax.all_gather(tokens, ('row', 'dp'), axis=0, tiled=True)]
    reduce_scatter x2 -> x0, waiting for transfers between devices: 149 us -> none  [reduce_tokens(): lax.psum_scatter(product(source, weight, 1, contract), ('row', 'dp'), sca...]
    ppermute x0 -> x39, waiting for transfers between devices: none -> 84.6 us  [the longest x30 74.2 us: shift(): return lax.ppermute(value, axis, [(i, (i + step) % N) for i in range(N)])]
    ppermute x0 -> x39, starting transfers between devices: none -> 71.5 us  [the longest x30 48.5 us: shift(): return lax.ppermute(value, axis, [(i, (i + step) % N) for i in range(N)])]
    dot_general x6 -> x0, matrix products: 30 us -> none  [product(): lax.dot_general(left_side, right_side, (((left_dim,), (right_dim,)), ((),...]
    pallas_call x0 -> x14, Pallas kernels: none -> 18.9 us  [the longest x13 13.1 us: call(): pl.pallas_call(body, out_shape=[jax.ShapeDtypeStruct(s, d) for s, d in ou...]
  transfers between devices with their start and end apart: 3 -> 39, of which waited for: 3 -> 17; matrix products, arithmetic and copies ran while one was open for 4% -> 0% of each run, Pallas kernels for 0% -> 10%
where the time goes in v1:
time: 180 us
  waiting for transfers between devices  84.6 us (47%)
  starting transfers between devices  71.5 us (40%)
  Pallas kernels  18.9 us (10%)
  local copies, waits for them, and re-layouts  3.35 us (2%)
    ppermute x30, waiting for transfers between devices, shift(): return lax.ppermute(value, axis, [(i, (i + step) % N) for i in range(N)])  74.2 us
    ppermute x30, starting transfers between devices, shift(): return lax.ppermute(value, axis, [(i, (i + step) % N) for i in range(N)])  48.5 us
    ppermute x4, starting transfers between devices, shards(): parts.append(lax.ppermute(s, ('y', 'zh'), pairs))  13.2 us
    pallas_call x13, Pallas kernels, call(): pl.pallas_call(body, out_shape=[jax.ShapeDtypeStruct(s, d) for s, d in ou...  13.1 us
    ppermute x5, starting transfers between devices, swap(): return lax.ppermute(value, axis, [(0, 1), (1, 0)])  9.73 us
    ppermute x4, waiting for transfers between devices, shards(): parts.append(lax.ppermute(s, ('y', 'zh'), pairs))  7.39 us
    pallas_call x1, Pallas kernels, shards(): pl.pallas_call(weight_grads, out_shape=[jax.ShapeDtypeStruct((width, hidd...  5.8 us
  transfers between devices with their start and end apart: 39, of which 17 were waited for; matrix products, arithmetic and copies ran while one was open for 0% of the time, Pallas kernels for 10%

profile of v1, /device:TPU:1, one launch (start us, length us, event | category | flops | bytes accessed | tf_op | source)
XLA Modules:
  0.0 180.2 jit_solution(11248589812256534083)
XLA Ops:
  1.5 3.8 %collective-permute-start.1 = (bf16[2,40,768]{2,1,0:T(8,128)(2,1)S(1)}, bf16[2,40,768]{2,1,0:T(8,128)(2,1)S(1)}, u32[]{:S(2)}, u32[]{:S(2)}) collective-permute-start(bf16[2,40,768]{2,1,0:T(8,128)(2,1)S(1)} %get-tuple-element.77), channel_id=1, source_target_pairs={{0,128},{64,192},{128,0},{192,64},{1,129},{65,193},{129,1},{193,65... | collective-permute-start | bytes 368648 | tf_op jit(solution)/shard_map/ppermute | solution.py:151
  7.6 3.5 %collective-permute-done = bf16[2,40,768]{2,1,0:T(8,128)(2,1)S(1)} collective-permute-done((bf16[2,40,768]{2,1,0:T(8,128)(2,1)S(1)}, bf16[2,40,768]{2,1,0:T(8,128)(2,1)S(1)}, u32[]{:S(2)}, u32[]{:S(2)}) %collective-permute-start) | collective-permute-done | bytes 122912 | tf_op jit(solution)/shard_map/ppermute | solution.py:151
  11.1 1.9 %collective-permute-done.2 = bf16[2,40,768]{2,1,0:T(8,128)(2,1)S(1)} collective-permute-done((bf16[2,40,768]{2,1,0:T(8,128)(2,1)S(1)}, bf16[2,40,768]{2,1,0:T(8,128)(2,1)S(1)}, u32[]{:S(2)}, u32[]{:S(2)}) %collective-permute-start.2) | collective-permute-done | bytes 122912 | tf_op jit(solution)/shard_map/ppermute | solution.py:151
  14.3 6.3 %collective-permute-start.20 = (bf16[4,2,40,768]{3,2,1,0:T(8,128)(2,1)S(1)}, bf16[4,2,40,768]{3,2,1,0:T(8,128)(2,1)S(1)}, u32[]{:S(2)}, u32[]{:S(2)}) collective-permute-start(bf16[4,2,40,768]{3,2,1,0:T(8,128)(2,1)S(1)} %pad_maximum_fusion.mine), channel_id=1, source_target_pairs={{0,1},{1,0},{2,3},{3,2},{4,5},{5,4},{6,7},{7,6},{8,9},{9,8},{10,11... | collective-permute-start | bytes 1474568 | tf_op jit(solution)/shard_map/ppermute | solution.py:155
  23.9 2.2 %shard_map.75 = (bf16[2,320,768]{2,1,0:T(8,128)(2,1)S(1)}, f32[2,80,1536]{2,1,0:T(8,128)S(1)}, bf16[2,80,1536]{2,1,0:T(8,128)(2,1)S(1)}, bf16[2,80,1536]{2,1,0:T(8,128)(2,1)S(1)}, bf16[2,80,1536]{2,1,0:T(8,128)(2,1)S(1)}) custom-call(s32[2]{0:T(128)S(1)} %pad_add_fusion.at, bf16[4,2,40,768]{3,2,1,0:T(8,128)(2,1)S(1)} %pad_maximum_fusion.mine, ...), custom_call_target="tpu_custom_call" | custom-call | flops 1509949440 | bytes 12582912 | tf_op jit(solution)/shard_map/pallas_call | solution.py:37
  27.5 2.5 %collective-permute-start.5 = (bf16[2,80,1536]{2,1,0:T(8,128)(2,1)S(1)}, bf16[2,80,1536]{2,1,0:T(8,128)(2,1)S(1)}, u32[]{:S(2)}, u32[]{:S(2)}) collective-permute-start(bf16[2,80,1536]{2,1,0:T(8,128)(2,1)S(1)} %get-tuple-element.42), channel_id=1, source_target_pairs={{0,4},{2,6},{4,0},{6,2},{1,5},{3,7},{5,1},{7,3},{8,12},{10,14},{12... | collective-permute-start | bytes 1474568 | tf_op jit(solution)/shard_map/ppermute | solution.py:151
  31.1 3.0 %collective-permute-done.20.mine = bf16[4,2,40,768]{3,2,1,0:T(8,128)(2,1)S(1)} collective-permute-done((bf16[4,2,40,768]{3,2,1,0:T(8,128)(2,1)S(1)}, bf16[4,2,40,768]{3,2,1,0:T(8,128)(2,1)S(1)}, u32[]{:S(2)}, u32[]{:S(2)}) %collective-permute-start.20) | collective-permute-done | bytes 491552 | tf_op jit(solution)/shard_map/ppermute | solution.py:155
  34.9 5.0 %collective-permute-done.4.one = bf16[2,80,1536]{2,1,0:T(8,128)(2,1)S(1)} collective-permute-done((bf16[2,80,1536]{2,1,0:T(8,128)(2,1)S(1)}, bf16[2,80,1536]{2,1,0:T(8,128)(2,1)S(1)}, u32[]{:S(2)}, u32[]{:S(2)}) %collective-permute-start.4) | collective-permute-done | bytes 491552 | tf_op jit(solution)/shard_map/ppermute | solution.py:151
  39.9 11.5 %collective-permute-done.5.two = bf16[2,80,1536]{2,1,0:T(8,128)(2,1)S(1)} collective-permute-done((bf16[2,80,1536]{2,1,0:T(8,128)(2,1)S(1)}, bf16[2,80,1536]{2,1,0:T(8,128)(2,1)S(1)}, u32[]{:S(2)}, u32[]{:S(2)}) %collective-permute-start.5) | collective-permute-done | bytes 491552 | tf_op jit(solution)/shard_map/ppermute | solution.py:151
  53.1 2.2 %shard_map.81 = (bf16[2,320,768]{2,1,0:T(8,128)(2,1)S(1)}, f32[2,80,1536]{2,1,0:T(8,128)S(1)}, bf16[2,80,1536]{2,1,0:T(8,128)(2,1)S(1)}, bf16[2,80,1536]{2,1,0:T(8,128)(2,1)S(1)}, bf16[2,80,1536]{2,1,0:T(8,128)(2,1)S(1)}) custom-call(s32[2]{0:T(128)S(1)} %pad_add_fusion.at, bf16[4,2,40,768]{3,2,1,0:T(8,128)(2,1)S(1)} %collective-permute-done.20.mine, ...), custom_call_target="tpu_custom_call" | custom-call | flops 1509949440 | bytes 12582912 | tf_op jit(solution)/shard_map/pallas_call | solution.py:37
  56.4 2.8 %collective-permute-start.23 = (bf16[2,80,1536]{2,1,0:T(8,128)(2,1)S(1)}, bf16[2,80,1536]{2,1,0:T(8,128)(2,1)S(1)}, u32[]{:S(2)}, u32[]{:S(2)}) collective-permute-start(bf16[2,80,1536]{2,1,0:T(8,128)(2,1)S(1)} %get-tuple-element.56), channel_id=1, source_target_pairs={{0,4},{2,6},{4,0},{6,2},{1,5},{3,7},{5,1},{7,3},{8,12},{10,14},{12... | collective-permute-start | bytes 1474568 | tf_op jit(solution)/shard_map/ppermute | solution.py:151
  62.4 3.4 %collective-permute-done.8.two = bf16[2,80,384]{2,1,0:T(8,128)(2,1)S(1)} collective-permute-done((bf16[2,80,384]{2,1,0:T(8,128)(2,1)S(1)}, bf16[2,80,384]{2,1,0:T(8,128)(2,1)S(1)}, u32[]{:S(2)}, u32[]{:S(2)}) %collective-permute-start.8) | collective-permute-done | bytes 122912 | tf_op jit(solution)/shard_map/ppermute | solution.py:151
  66.0 7.0 %collective-permute-start.12 = (bf16[2,80,384]{2,1,0:T(8,128)(2,1)S(1)}, bf16[2,80,384]{2,1,0:T(8,128)(2,1)S(1)}, u32[]{:S(2)}, u32[]{:S(2)}) collective-permute-start(bf16[2,80,384]{2,1,0:T(8,128)(2,1)S(1)} %shard_map.77.mine), channel_id=1, source_target_pairs={{0,24},{8,0},{16,8},{24,16},{1,25},{9,1},{17,9},{25,17},{2,26},{10... | collective-permute-start | bytes 368648 | tf_op jit(solution)/shard_map/ppermute | solution.py:151
  74.8 7.2 %collective-permute-done.11.two = bf16[2,80,384]{2,1,0:T(8,128)(2,1)S(1)} collective-permute-done((bf16[2,80,384]{2,1,0:T(8,128)(2,1)S(1)}, bf16[2,80,384]{2,1,0:T(8,128)(2,1)S(1)}, u32[]{:S(2)}, u32[]{:S(2)}) %collective-permute-start.11) | collective-permute-done | bytes 122912 | tf_op jit(solution)/shard_map/ppermute | solution.py:151
  85.3 2.0 %collective-permute-start.26 = (bf16[2,80,384]{2,1,0:T(8,128)(2,1)S(1)}, bf16[2,80,384]{2,1,0:T(8,128)(2,1)S(1)}, u32[]{:S(2)}, u32[]{:S(2)}) collective-permute-start(bf16[2,80,384]{2,1,0:T(8,128)(2,1)S(1)} %get-tuple-element.60), channel_id=1, source_target_pairs={{0,16},{8,24},{16,0},{24,8},{1,17},{9,25},{17,1},{25,9},{2,18},{10... | collective-permute-start | bytes 368648 | tf_op jit(solution)/shard_map/ppermute | solution.py:151
  87.3 2.3 %collective-permute-start.27 = (bf16[2,80,384]{2,1,0:T(8,128)(2,1)S(1)}, bf16[2,80,384]{2,1,0:T(8,128)(2,1)S(1)}, u32[]{:S(2)}, u32[]{:S(2)}) collective-permute-start(bf16[2,80,384]{2,1,0:T(8,128)(2,1)S(1)} %get-tuple-element.61), channel_id=1, source_target_pairs={{0,24},{8,0},{16,8},{24,16},{1,25},{9,1},{17,9},{25,17},{2,26},{10... | collective-permute-start | bytes 368648 | tf_op jit(solution)/shard_map/ppermute | solution.py:151
  89.6 3.2 %collective-permute-done.26.two = bf16[2,80,384]{2,1,0:T(8,128)(2,1)S(1)} collective-permute-done((bf16[2,80,384]{2,1,0:T(8,128)(2,1)S(1)}, bf16[2,80,384]{2,1,0:T(8,128)(2,1)S(1)}, u32[]{:S(2)}, u32[]{:S(2)}) %collective-permute-start.26) | collective-permute-done | bytes 122912 | tf_op jit(solution)/shard_map/ppermute | solution.py:151
  93.0 6.6 %collective-permute-start.30 = (bf16[2,80,384]{2,1,0:T(8,128)(2,1)S(1)}, bf16[2,80,384]{2,1,0:T(8,128)(2,1)S(1)}, u32[]{:S(2)}, u32[]{:S(2)}) collective-permute-start(bf16[2,80,384]{2,1,0:T(8,128)(2,1)S(1)} %shard_map.83.mine), channel_id=1, source_target_pairs={{0,24},{8,0},{16,8},{24,16},{1,25},{9,1},{17,9},{25,17},{2,26},{10... | collective-permute-start | bytes 368648 | tf_op jit(solution)/shard_map/ppermute | solution.py:151
  99.7 2.9 %collective-permute-start.14 = (bf16[2,80,1536]{2,1,0:T(8,128)(2,1)S(1)}, bf16[2,80,1536]{2,1,0:T(8,128)(2,1)S(1)}, u32[]{:S(2)}, u32[]{:S(2)}) collective-permute-start(bf16[2,80,1536]{2,1,0:T(8,128)(2,1)S(1)} %shard_map.78.mine), channel_id=1, source_target_pairs={{0,4},{2,6},{4,0},{6,2},{1,5},{3,7},{5,1},{7,3},{8,12},{10,14},{12... | collective-permute-start | bytes 1474568 | tf_op jit(solution)/shard_map/ppermute | solution.py:151
  102.9 7.6 %collective-permute-done.29.two = bf16[2,80,384]{2,1,0:T(8,128)(2,1)S(1)} collective-permute-done((bf16[2,80,384]{2,1,0:T(8,128)(2,1)S(1)}, bf16[2,80,384]{2,1,0:T(8,128)(2,1)S(1)}, u32[]{:S(2)}, u32[]{:S(2)}) %collective-permute-start.29) | collective-permute-done | bytes 122912 | tf_op jit(solution)/shard_map/ppermute | solution.py:151
  111.1 2.6 %collective-permute-start.33 = (bf16[2,80,1536]{2,1,0:T(8,128)(2,1)S(1)}, bf16[2,80,1536]{2,1,0:T(8,128)(2,1)S(1)}, u32[]{:S(2)}, u32[]{:S(2)}) collective-permute-start(bf16[2,80,1536]{2,1,0:T(8,128)(2,1)S(1)} %shard_map.84.mine), channel_id=1, source_target_pairs={{0,6},{2,0},{4,2},{6,4},{1,7},{3,1},{5,3},{7,5},{8,14},{10,8},{12,... | collective-permute-start | bytes 1474568 | tf_op jit(solution)/shard_map/ppermute | solution.py:151
  114.7 13.1 %collective-permute-done.13.one = bf16[2,80,1536]{2,1,0:T(8,128)(2,1)S(1)} collective-permute-done((bf16[2,80,1536]{2,1,0:T(8,128)(2,1)S(1)}, bf16[2,80,1536]{2,1,0:T(8,128)(2,1)S(1)}, u32[]{:S(2)}, u32[]{:S(2)}) %collective-permute-start.13) | collective-permute-done | bytes 491552 | tf_op jit(solution)/shard_map/ppermute | solution.py:151
  127.8 2.3 %shard_map.79 = (bf16[2,320,1536]{2,1,0:T(8,128)(2,1)S(1)}, f32[4,2,40,768]{3,2,1,0:T(8,128)S(1)}, bf16[4,2,40,768]{3,2,1,0:T(8,128)(2,1)S(1)}) custom-call(s32[2]{0:T(128)S(1)} %pad_add_fusion.at, bf16[2,80,1536]{2,1,0:T(8,128)(2,1)S(1)} %shard_map.78.mine, bf16[2,80,1536]{2,1,0:T(8,128)(2,1)S(1)} %collective-permute-done.13.one, ...), custom_call_target="tpu_custom_call" | custom-call | flops 1509949440 | bytes 12582912 | tf_op jit(solution)/shard_map/pallas_call | solution.py:37
  132.5 13.4 %collective-permute-done.31.one = bf16[2,80,1536]{2,1,0:T(8,128)(2,1)S(1)} collective-permute-done((bf16[2,80,1536]{2,1,0:T(8,128)(2,1)S(1)}, bf16[2,80,1536]{2,1,0:T(8,128)(2,1)S(1)}, u32[]{:S(2)}, u32[]{:S(2)}) %collective-permute-start.31) | collective-permute-done | bytes 491552 | tf_op jit(solution)/shard_map/ppermute | solution.py:151
  145.9 2.3 %shard_map.85 = (bf16[2,320,1536]{2,1,0:T(8,128)(2,1)S(1)}, f32[4,2,40,768]{3,2,1,0:T(8,128)S(1)}, bf16[4,2,40,768]{3,2,1,0:T(8,128)(2,1)S(1)}) custom-call(s32[2]{0:T(128)S(1)} %pad_add_fusion.at, bf16[2,80,1536]{2,1,0:T(8,128)(2,1)S(1)} %shard_map.84.mine, bf16[2,80,1536]{2,1,0:T(8,128)(2,1)S(1)} %collective-permute-done.31.one, ...), custom_call_target="tpu_custom_call" | custom-call | flops 1509949440 | bytes 12582912 | tf_op jit(solution)/shard_map/pallas_call | solution.py:37
  149.3 2.5 %collective-permute-start.18 = (bf16[2,40,768]{2,1,0:T(8,128)(2,1)S(1)}, bf16[2,40,768]{2,1,0:T(8,128)(2,1)S(1)}, u32[]{:S(2)}, u32[]{:S(2)}) collective-permute-start(bf16[2,40,768]{2,1,0:T(8,128)(2,1)S(1)} %get-tuple-element.52), channel_id=1, source_target_pairs={{0,128},{64,192},{128,0},{192,64},{1,129},{65,193},{129,1},{193,65... | collective-permute-start | bytes 368648 | tf_op jit(solution)/shard_map/ppermute | solution.py:151
  154.5 4.1 %collective-permute-start.36 = (bf16[2,40,768]{2,1,0:T(8,128)(2,1)S(1)}, bf16[2,40,768]{2,1,0:T(8,128)(2,1)S(1)}, u32[]{:S(2)}, u32[]{:S(2)}) collective-permute-start(bf16[2,40,768]{2,1,0:T(8,128)(2,1)S(1)} %get-tuple-element.65), channel_id=1, source_target_pairs={{0,65},{1,64},{64,129},{65,128},{128,193},{129,192},{192,1},{193,0... | collective-permute-start | bytes 368648 | tf_op jit(solution)/shard_map/ppermute | solution.py:225
  158.6 1.9 %collective-permute-start.37 = (bf16[2,40,768]{2,1,0:T(8,128)(2,1)S(1)}, bf16[2,40,768]{2,1,0:T(8,128)(2,1)S(1)}, u32[]{:S(2)}, u32[]{:S(2)}) collective-permute-start(bf16[2,40,768]{2,1,0:T(8,128)(2,1)S(1)} %get-tuple-element.66), channel_id=1, source_target_pairs={{0,129},{1,128},{64,193},{65,192},{128,1},{129,0},{192,65},{193,64... | collective-permute-start | bytes 368648 | tf_op jit(solution)/shard_map/ppermute | solution.py:225
  160.5 5.7 %collective-permute-start.38 = (bf16[2,40,768]{2,1,0:T(8,128)(2,1)S(1)}, bf16[2,40,768]{2,1,0:T(8,128)(2,1)S(1)}, u32[]{:S(2)}, u32[]{:S(2)}) collective-permute-start(bf16[2,40,768]{2,1,0:T(8,128)(2,1)S(1)} %get-tuple-element.67), channel_id=1, source_target_pairs={{0,193},{1,192},{64,1},{65,0},{128,65},{129,64},{192,129},{193,128... | collective-permute-start | bytes 368648 | tf_op jit(solution)/shard_map/ppermute | solution.py:225
  166.2 5.8 %shard_map.88 = (bf16[768,1536]{1,0:T(8,128)(2,1)}, bf16[1536,768]{1,0:T(8,128)(2,1)}) custom-call(bf16[2,320,768]{2,1,0:T(8,128)(2,1)S(1)} %get-tuple-element.70.rows_own, bf16[2,320,1536]{2,1,0:T(8,128)(2,1)S(1)} %get-tuple-element.71.hidden_own, bf16[2,320,768]{2,1,0:T(8,128)(2,1)S(1)} %get-tuple-element.72.rows_far, ...), custom_call_target="tpu_custom_call" | custom-call | flops 3019898880 | bytes 12582912 | tf_op jit(solution)/shard_map/pallas_call | solution.py:227
  172.0 5.1 %collective-permute-done.37.rest_5_ = bf16[2,40,768]{2,1,0:T(8,128)(2,1)S(1)} collective-permute-done((bf16[2,40,768]{2,1,0:T(8,128)(2,1)S(1)}, bf16[2,40,768]{2,1,0:T(8,128)(2,1)S(1)}, u32[]{:S(2)}, u32[]{:S(2)}) %collective-permute-start.37) | collective-permute-done | bytes 122912 | tf_op jit(solution)/shard_map/ppermute | solution.py:225
  177.1 2.3 %collective-permute-done.38.rest_6_ = bf16[2,40,768]{2,1,0:T(8,128)(2,1)S(1)} collective-permute-done((bf16[2,40,768]{2,1,0:T(8,128)(2,1)S(1)}, bf16[2,40,768]{2,1,0:T(8,128)(2,1)S(1)}, u32[]{:S(2)}, u32[]{:S(2)}) %collective-permute-start.38) | collective-permute-done | bytes 122912 | tf_op jit(solution)/shard_map/ppermute | solution.py:225
  (75 shorter events, 31.5 us)
Async XLA Ops:
  6.1 6.9 %collective-permute-start.2 = (bf16[2,40,768]{2,1,0:T(8,128)(2,1)S(1)}, bf16[2,40,768]{2,1,0:T(8,128)(2,1)S(1)}, u32[]{:S(2)}, u32[]{:S(2)}) collective-permute-start(bf16[2,40,768]{2,1,0:T(8,128)(2,1)S(1)} %get-tuple-element.77), channel_id=1, source_target_pairs={{0,64},{64,128},{128,192},{192,0},{1,65},{65,129},{129,193},{193,1... | collective-permute-start | bytes 368648 | tf_op jit(solution)/shard_map/ppermute | solution.py:151
  13.0 7.6 %collective-permute-start.3 = (bf16[4,2,40,768]{3,2,1,0:T(8,128)(2,1)S(1)}, bf16[4,2,40,768]{3,2,1,0:T(8,128)(2,1)S(1)}, u32[]{:S(2)}, u32[]{:S(2)}) collective-permute-start(bf16[4,2,40,768]{3,2,1,0:T(8,128)(2,1)S(1)} %pad_maximum_fusion.mine), channel_id=1, source_target_pairs={{0,32},{32,0},{1,33},{33,1},{2,34},{34,2},{3,35},{35,3},{4,36},{36... | collective-permute-start | bytes 1474568 | tf_op jit(solution)/shard_map/ppermute | solution.py:155
  14.3 19.9 %collective-permute-start.20 = (bf16[4,2,40,768]{3,2,1,0:T(8,128)(2,1)S(1)}, bf16[4,2,40,768]{3,2,1,0:T(8,128)(2,1)S(1)}, u32[]{:S(2)}, u32[]{:S(2)}) collective-permute-start(bf16[4,2,40,768]{3,2,1,0:T(8,128)(2,1)S(1)} %pad_maximum_fusion.mine), channel_id=1, source_target_pairs={{0,1},{1,0},{2,3},{3,2},{4,5},{5,4},{6,7},{7,6},{8,9},{9,8},{10,11... | collective-permute-start | bytes 1474568 | tf_op jit(solution)/shard_map/ppermute | solution.py:155
  26.2 13.7 %collective-permute-start.4 = (bf16[2,80,1536]{2,1,0:T(8,128)(2,1)S(1)}, bf16[2,80,1536]{2,1,0:T(8,128)(2,1)S(1)}, u32[]{:S(2)}, u32[]{:S(2)}) collective-permute-start(bf16[2,80,1536]{2,1,0:T(8,128)(2,1)S(1)} %get-tuple-element.41), channel_id=1, source_target_pairs={{0,2},{2,4},{4,6},{6,0},{1,3},{3,5},{5,7},{7,1},{8,10},{10,12},{12... | collective-permute-start | bytes 1474568 | tf_op jit(solution)/shard_map/ppermute | solution.py:151
  27.5 24.0 %collective-permute-start.5 = (bf16[2,80,1536]{2,1,0:T(8,128)(2,1)S(1)}, bf16[2,80,1536]{2,1,0:T(8,128)(2,1)S(1)}, u32[]{:S(2)}, u32[]{:S(2)}) collective-permute-start(bf16[2,80,1536]{2,1,0:T(8,128)(2,1)S(1)} %get-tuple-element.42), channel_id=1, source_target_pairs={{0,4},{2,6},{4,0},{6,2},{1,5},{3,7},{5,1},{7,3},{8,12},{10,14},{12... | collective-permute-start | bytes 1474568 | tf_op jit(solution)/shard_map/ppermute | solution.py:151
  30.0 21.5 %collective-permute-start.6 = (bf16[2,80,1536]{2,1,0:T(8,128)(2,1)S(1)}, bf16[2,80,1536]{2,1,0:T(8,128)(2,1)S(1)}, u32[]{:S(2)}, u32[]{:S(2)}) collective-permute-start(bf16[2,80,1536]{2,1,0:T(8,128)(2,1)S(1)} %get-tuple-element.43), channel_id=1, source_target_pairs={{0,6},{2,0},{4,2},{6,4},{1,7},{3,1},{5,3},{7,5},{8,14},{10,8},{12,... | collective-permute-start | bytes 1474568 | tf_op jit(solution)/shard_map/ppermute | solution.py:151
  34.1 19.0 %collective-permute-start.21 = (bf16[4,2,40,768]{3,2,1,0:T(8,128)(2,1)S(1)}, bf16[4,2,40,768]{3,2,1,0:T(8,128)(2,1)S(1)}, u32[]{:S(2)}, u32[]{:S(2)}) collective-permute-start(bf16[4,2,40,768]{3,2,1,0:T(8,128)(2,1)S(1)} %collective-permute-done.20.mine), channel_id=1, source_target_pairs={{0,32},{32,0},{1,33},{33,1},{2,34},{34,2},{3,35},{35,3},{4,36},{36... | collective-permute-start | bytes 1474568 | tf_op jit(solution)/shard_map/ppermute | solution.py:155
  52.3 8.5 %collective-permute-start.7 = (bf16[2,80,384]{2,1,0:T(8,128)(2,1)S(1)}, bf16[2,80,384]{2,1,0:T(8,128)(2,1)S(1)}, u32[]{:S(2)}, u32[]{:S(2)}) collective-permute-start(bf16[2,80,384]{2,1,0:T(8,128)(2,1)S(1)} %get-tuple-element.45), channel_id=1, source_target_pairs={{0,8},{8,16},{16,24},{24,0},{1,9},{9,17},{17,25},{25,1},{2,10},{10... | collective-permute-start | bytes 368648 | tf_op jit(solution)/shard_map/ppermute | solution.py:151
  55.3 27.7 %collective-permute-start.22 = (bf16[2,80,1536]{2,1,0:T(8,128)(2,1)S(1)}, bf16[2,80,1536]{2,1,0:T(8,128)(2,1)S(1)}, u32[]{:S(2)}, u32[]{:S(2)}) collective-permute-start(bf16[2,80,1536]{2,1,0:T(8,128)(2,1)S(1)} %get-tuple-element.55), channel_id=1, source_target_pairs={{0,2},{2,4},{4,6},{6,0},{1,3},{3,5},{5,7},{7,1},{8,10},{10,12},{12... | collective-permute-start | bytes 1474568 | tf_op jit(solution)/shard_map/ppermute | solution.py:151
  56.4 26.6 %collective-permute-start.23 = (bf16[2,80,1536]{2,1,0:T(8,128)(2,1)S(1)}, bf16[2,80,1536]{2,1,0:T(8,128)(2,1)S(1)}, u32[]{:S(2)}, u32[]{:S(2)}) collective-permute-start(bf16[2,80,1536]{2,1,0:T(8,128)(2,1)S(1)} %get-tuple-element.56), channel_id=1, source_target_pairs={{0,4},{2,6},{4,0},{6,2},{1,5},{3,7},{5,1},{7,3},{8,12},{10,14},{12... | collective-permute-start | bytes 1474568 | tf_op jit(solution)/shard_map/ppermute | solution.py:151
  59.3 23.7 %collective-permute-start.24 = (bf16[2,80,1536]{2,1,0:T(8,128)(2,1)S(1)}, bf16[2,80,1536]{2,1,0:T(8,128)(2,1)S(1)}, u32[]{:S(2)}, u32[]{:S(2)}) collective-permute-start(bf16[2,80,1536]{2,1,0:T(8,128)(2,1)S(1)} %get-tuple-element.57), channel_id=1, source_target_pairs={{0,6},{2,0},{4,2},{6,4},{1,7},{3,1},{5,3},{7,5},{8,14},{10,8},{12,... | collective-permute-start | bytes 1474568 | tf_op jit(solution)/shard_map/ppermute | solution.py:151
  66.0 8.8 %collective-permute-start.12 = (bf16[2,80,384]{2,1,0:T(8,128)(2,1)S(1)}, bf16[2,80,384]{2,1,0:T(8,128)(2,1)S(1)}, u32[]{:S(2)}, u32[]{:S(2)}) collective-permute-start(bf16[2,80,384]{2,1,0:T(8,128)(2,1)S(1)} %shard_map.77.mine), channel_id=1, source_target_pairs={{0,24},{8,0},{16,8},{24,16},{1,25},{9,1},{17,9},{25,17},{2,26},{10... | collective-permute-start | bytes 368648 | tf_op jit(solution)/shard_map/ppermute | solution.py:151
  72.9 9.1 %collective-permute-start.11 = (bf16[2,80,384]{2,1,0:T(8,128)(2,1)S(1)}, bf16[2,80,384]{2,1,0:T(8,128)(2,1)S(1)}, u32[]{:S(2)}, u32[]{:S(2)}) collective-permute-start(bf16[2,80,384]{2,1,0:T(8,128)(2,1)S(1)} %shard_map.77.mine), channel_id=1, source_target_pairs={{0,16},{8,24},{16,0},{24,8},{1,17},{9,25},{17,1},{25,9},{2,18},{10... | collective-permute-start | bytes 368648 | tf_op jit(solution)/shard_map/ppermute | solution.py:151
  74.8 7.2 %collective-permute-start.10 = (bf16[2,80,384]{2,1,0:T(8,128)(2,1)S(1)}, bf16[2,80,384]{2,1,0:T(8,128)(2,1)S(1)}, u32[]{:S(2)}, u32[]{:S(2)}) collective-permute-start(bf16[2,80,384]{2,1,0:T(8,128)(2,1)S(1)} %shard_map.77.mine), channel_id=1, source_target_pairs={{0,8},{8,16},{16,24},{24,0},{1,9},{9,17},{17,25},{25,1},{2,10},{10... | collective-permute-start | bytes 368648 | tf_op jit(solution)/shard_map/ppermute | solution.py:151
  82.6 31.3 %collective-permute-start.15 = (bf16[2,80,1536]{2,1,0:T(8,128)(2,1)S(1)}, bf16[2,80,1536]{2,1,0:T(8,128)(2,1)S(1)}, u32[]{:S(2)}, u32[]{:S(2)}) collective-permute-start(bf16[2,80,1536]{2,1,0:T(8,128)(2,1)S(1)} %shard_map.78.mine), channel_id=1, source_target_pairs={{0,6},{2,0},{4,2},{6,4},{1,7},{3,1},{5,3},{7,5},{8,14},{10,8},{12,... | collective-permute-start | bytes 1474568 | tf_op jit(solution)/shard_map/ppermute | solution.py:151
  85.3 7.5 %collective-permute-start.26 = (bf16[2,80,384]{2,1,0:T(8,128)(2,1)S(1)}, bf16[2,80,384]{2,1,0:T(8,128)(2,1)S(1)}, u32[]{:S(2)}, u32[]{:S(2)}) collective-permute-start(bf16[2,80,384]{2,1,0:T(8,128)(2,1)S(1)} %get-tuple-element.60), channel_id=1, source_target_pairs={{0,16},{8,24},{16,0},{24,8},{1,17},{9,25},{17,1},{25,9},{2,18},{10... | collective-permute-start | bytes 368648 | tf_op jit(solution)/shard_map/ppermute | solution.py:151
  93.0 9.5 %collective-permute-start.30 = (bf16[2,80,384]{2,1,0:T(8,128)(2,1)S(1)}, bf16[2,80,384]{2,1,0:T(8,128)(2,1)S(1)}, u32[]{:S(2)}, u32[]{:S(2)}) collective-permute-start(bf16[2,80,384]{2,1,0:T(8,128)(2,1)S(1)} %shard_map.83.mine), channel_id=1, source_target_pairs={{0,24},{8,0},{16,8},{24,16},{1,25},{9,1},{17,9},{25,17},{2,26},{10... | collective-permute-start | bytes 368648 | tf_op jit(solution)/shard_map/ppermute | solution.py:151
  99.7 15.0 %collective-permute-start.14 = (bf16[2,80,1536]{2,1,0:T(8,128)(2,1)S(1)}, bf16[2,80,1536]{2,1,0:T(8,128)(2,1)S(1)}, u32[]{:S(2)}, u32[]{:S(2)}) collective-permute-start(bf16[2,80,1536]{2,1,0:T(8,128)(2,1)S(1)} %shard_map.78.mine), channel_id=1, source_target_pairs={{0,4},{2,6},{4,0},{6,2},{1,5},{3,7},{5,1},{7,3},{8,12},{10,14},{12... | collective-permute-start | bytes 1474568 | tf_op jit(solution)/shard_map/ppermute | solution.py:151
  102.5 25.3 %collective-permute-start.13 = (bf16[2,80,1536]{2,1,0:T(8,128)(2,1)S(1)}, bf16[2,80,1536]{2,1,0:T(8,128)(2,1)S(1)}, u32[]{:S(2)}, u32[]{:S(2)}) collective-permute-start(bf16[2,80,1536]{2,1,0:T(8,128)(2,1)S(1)} %shard_map.78.mine), channel_id=1, source_target_pairs={{0,2},{2,4},{4,6},{6,0},{1,3},{3,5},{5,7},{7,1},{8,10},{10,12},{12... | collective-permute-start | bytes 1474568 | tf_op jit(solution)/shard_map/ppermute | solution.py:151
  102.6 8.0 %collective-permute-start.29 = (bf16[2,80,384]{2,1,0:T(8,128)(2,1)S(1)}, bf16[2,80,384]{2,1,0:T(8,128)(2,1)S(1)}, u32[]{:S(2)}, u32[]{:S(2)}) collective-permute-start(bf16[2,80,384]{2,1,0:T(8,128)(2,1)S(1)} %shard_map.83.mine), channel_id=1, source_target_pairs={{0,16},{8,24},{16,0},{24,8},{1,17},{9,25},{17,1},{25,9},{2,18},{10... | collective-permute-start | bytes 368648 | tf_op jit(solution)/shard_map/ppermute | solution.py:151
  102.6 8.0 %collective-permute-start.28 = (bf16[2,80,384]{2,1,0:T(8,128)(2,1)S(1)}, bf16[2,80,384]{2,1,0:T(8,128)(2,1)S(1)}, u32[]{:S(2)}, u32[]{:S(2)}) collective-permute-start(bf16[2,80,384]{2,1,0:T(8,128)(2,1)S(1)} %shard_map.83.mine), channel_id=1, source_target_pairs={{0,8},{8,16},{16,24},{24,0},{1,9},{9,17},{17,25},{25,1},{2,10},{10... | collective-permute-start | bytes 368648 | tf_op jit(solution)/shard_map/ppermute | solution.py:151
  111.1 19.7 %collective-permute-start.33 = (bf16[2,80,1536]{2,1,0:T(8,128)(2,1)S(1)}, bf16[2,80,1536]{2,1,0:T(8,128)(2,1)S(1)}, u32[]{:S(2)}, u32[]{:S(2)}) collective-permute-start(bf16[2,80,1536]{2,1,0:T(8,128)(2,1)S(1)} %shard_map.84.mine), channel_id=1, source_target_pairs={{0,6},{2,0},{4,2},{6,4},{1,7},{3,1},{5,3},{7,5},{8,14},{10,8},{12,... | collective-permute-start | bytes 1474568 | tf_op jit(solution)/shard_map/ppermute | solution.py:151
  113.7 18.8 %collective-permute-start.32 = (bf16[2,80,1536]{2,1,0:T(8,128)(2,1)S(1)}, bf16[2,80,1536]{2,1,0:T(8,128)(2,1)S(1)}, u32[]{:S(2)}, u32[]{:S(2)}) collective-permute-start(bf16[2,80,1536]{2,1,0:T(8,128)(2,1)S(1)} %shard_map.84.mine), channel_id=1, source_target_pairs={{0,4},{2,6},{4,0},{6,2},{1,5},{3,7},{5,1},{7,3},{8,12},{10,14},{12... | collective-permute-start | bytes 1474568 | tf_op jit(solution)/shard_map/ppermute | solution.py:151
  114.0 32.0 %collective-permute-start.31 = (bf16[2,80,1536]{2,1,0:T(8,128)(2,1)S(1)}, bf16[2,80,1536]{2,1,0:T(8,128)(2,1)S(1)}, u32[]{:S(2)}, u32[]{:S(2)}) collective-permute-start(bf16[2,80,1536]{2,1,0:T(8,128)(2,1)S(1)} %shard_map.84.mine), channel_id=1, source_target_pairs={{0,2},{2,4},{4,6},{6,0},{1,3},{3,5},{5,7},{7,1},{8,10},{10,12},{12... | collective-permute-start | bytes 1474568 | tf_op jit(solution)/shard_map/ppermute | solution.py:151
  130.1 18.7 %collective-permute-start.16 = (bf16[4,2,40,768]{3,2,1,0:T(8,128)(2,1)S(1)}, bf16[4,2,40,768]{3,2,1,0:T(8,128)(2,1)S(1)}, u32[]{:S(2)}, u32[]{:S(2)}) collective-permute-start(bf16[4,2,40,768]{3,2,1,0:T(8,128)(2,1)S(1)} %get-tuple-element.49), channel_id=1, source_target_pairs={{0,32},{32,0},{1,33},{33,1},{2,34},{34,2},{3,35},{35,3},{4,36},{36... | collective-permute-start | bytes 1474568 | tf_op jit(solution)/shard_map/ppermute | solution.py:155
  148.9 9.7 %collective-permute-start.17 = (bf16[2,40,768]{2,1,0:T(8,128)(2,1)S(1)}, bf16[2,40,768]{2,1,0:T(8,128)(2,1)S(1)}, u32[]{:S(2)}, u32[]{:S(2)}) collective-permute-start(bf16[2,40,768]{2,1,0:T(8,128)(2,1)S(1)} %get-tuple-element.51), channel_id=1, source_target_pairs={{0,64},{64,128},{128,192},{192,0},{1,65},{65,129},{129,193},{193,1... | collective-permute-start | bytes 368648 | tf_op jit(solution)/shard_map/ppermute | solution.py:151
  149.3 11.2 %collective-permute-start.18 = (bf16[2,40,768]{2,1,0:T(8,128)(2,1)S(1)}, bf16[2,40,768]{2,1,0:T(8,128)(2,1)S(1)}, u32[]{:S(2)}, u32[]{:S(2)}) collective-permute-start(bf16[2,40,768]{2,1,0:T(8,128)(2,1)S(1)} %get-tuple-element.52), channel_id=1, source_target_pairs={{0,128},{64,192},{128,0},{192,64},{1,129},{65,193},{129,1},{193,65... | collective-permute-start | bytes 368648 | tf_op jit(solution)/shard_map/ppermute | solution.py:151
  151.8 20.2 %collective-permute-start.19 = (bf16[2,40,768]{2,1,0:T(8,128)(2,1)S(1)}, bf16[2,40,768]{2,1,0:T(8,128)(2,1)S(1)}, u32[]{:S(2)}, u32[]{:S(2)}) collective-permute-start(bf16[2,40,768]{2,1,0:T(8,128)(2,1)S(1)} %get-tuple-element.53), channel_id=1, source_target_pairs={{0,192},{64,0},{128,64},{192,128},{1,193},{65,1},{129,65},{193,129... | collective-permute-start | bytes 368648 | tf_op jit(solution)/shard_map/ppermute | solution.py:151
  153.0 19.1 %collective-permute-start.35 = (bf16[2,40,768]{2,1,0:T(8,128)(2,1)S(1)}, bf16[2,40,768]{2,1,0:T(8,128)(2,1)S(1)}, u32[]{:S(2)}, u32[]{:S(2)}) collective-permute-start(bf16[2,40,768]{2,1,0:T(8,128)(2,1)S(1)} %get-tuple-element.64), channel_id=1, source_target_pairs={{0,1},{1,0},{64,65},{65,64},{128,129},{129,128},{192,193},{193,192... | collective-permute-start | bytes 368648 | tf_op jit(solution)/shard_map/ppermute | solution.py:225
  154.5 17.5 %collective-permute-start.36 = (bf16[2,40,768]{2,1,0:T(8,128)(2,1)S(1)}, bf16[2,40,768]{2,1,0:T(8,128)(2,1)S(1)}, u32[]{:S(2)}, u32[]{:S(2)}) collective-permute-start(bf16[2,40,768]{2,1,0:T(8,128)(2,1)S(1)} %get-tuple-element.65), channel_id=1, source_target_pairs={{0,65},{1,64},{64,129},{65,128},{128,193},{129,192},{192,1},{193,0... | collective-permute-start | bytes 368648 | tf_op jit(solution)/shard_map/ppermute | solution.py:225
  158.6 18.6 %collective-permute-start.37 = (bf16[2,40,768]{2,1,0:T(8,128)(2,1)S(1)}, bf16[2,40,768]{2,1,0:T(8,128)(2,1)S(1)}, u32[]{:S(2)}, u32[]{:S(2)}) collective-permute-start(bf16[2,40,768]{2,1,0:T(8,128)(2,1)S(1)} %get-tuple-element.66), channel_id=1, source_target_pairs={{0,129},{1,128},{64,193},{65,192},{128,1},{129,0},{192,65},{193,64... | collective-permute-start | bytes 368648 | tf_op jit(solution)/shard_map/ppermute | solution.py:225
  160.5 18.9 %collective-permute-start.38 = (bf16[2,40,768]{2,1,0:T(8,128)(2,1)S(1)}, bf16[2,40,768]{2,1,0:T(8,128)(2,1)S(1)}, u32[]{:S(2)}, u32[]{:S(2)}) collective-permute-start(bf16[2,40,768]{2,1,0:T(8,128)(2,1)S(1)} %get-tuple-element.67), channel_id=1, source_target_pairs={{0,193},{1,192},{64,1},{65,0},{128,65},{129,64},{192,129},{193,128... | collective-permute-start | bytes 368648 | tf_op jit(solution)/shard_map/ppermute | solution.py:225
  (13 other events, 124.9 us)

commit v2 on v1

v2 whole, which is shorter than its diff:
```python
import functools
import math

import jax
import jax.numpy as jnp
from jax import lax
from jax.experimental import pallas as pl
from jax.experimental.pallas import tpu as pltpu
from jax.sharding import Mesh
from jax.sharding import PartitionSpec as P

BF16, F32 = jnp.bfloat16, jnp.float32
GELU_SCALE = math.sqrt(2.0 / math.pi)
CUBIC = 0.044715
VMEM = pl.BlockSpec(memory_space=pltpu.VMEM)
SMEM = pl.BlockSpec(memory_space=pltpu.SMEM)
N = 4


def gelu_parts(v):
    t = jnp.tanh(GELU_SCALE * (v + CUBIC * v * v * v))
    values = 0.5 * v * (1.0 + t)
    slopes = 0.5 * (1.0 + t) + 0.5 * v * (1.0 - t * t) * GELU_SCALE * (
        1.0 + 3.0 * CUBIC * v * v
    )
    return values, slopes


def dot(a, b, contract_a, contract_b):
    return lax.dot_general(
        a, b, (((contract_a,), (contract_b,)), ((), ())), preferred_element_type=F32
    )


class Order:
    def __init__(self):
        self.last = None

    def call(self, body, outs, *args, limit=28, scratch=(), after=(), flops=0, traffic=0):
        anyplace = pl.BlockSpec(memory_space=pl.ANY)
        specs = [SMEM if a.dtype == jnp.int32 else VMEM for a in args]
        before = list(after) + ([] if self.last is None else [self.last])

        def ordered(*refs):
            ins, rest = refs[: len(args)], refs[len(args) + len(before) :]
            results, token, scratches = rest[: len(outs)], rest[len(outs)], rest[len(outs) + 1 :]
            body(*ins, *results, *scratches)
            token[...] = jnp.zeros_like(token)

        *results, self.last = pl.pallas_call(
            ordered,
            out_shape=[jax.ShapeDtypeStruct(s, d) for s, d in outs]
            + [jax.ShapeDtypeStruct((8, 128), F32)],
            in_specs=specs + [anyplace] * len(before),
            out_specs=[VMEM] * (len(outs) + 1),
            scratch_shapes=scratch,
            compiler_params=pltpu.CompilerParams(vmem_limit_bytes=limit << 20),
            cost_estimate=pl.CostEstimate(
                flops=flops, bytes_accessed=traffic, transcendentals=0
            ),
        )(*args, *before)
        return results


def first_products(at, mine, other, w_in, w_out, rows, keep, one, two, three):
    half = mine.shape[2]
    block = 2 * half
    for a in range(2):
        for d in range(N):
            k = lax.rem(at[0] + d, N)
            both = jnp.concatenate(
                [mine[k, a].astype(F32), other[k, a].astype(F32)], axis=0
            )
            rows[a, d * block : (d + 1) * block] = both.astype(BF16)
    width = 512
    for n in range(w_in.shape[1] // width):
        cut = slice(n * width, (n + 1) * width)
        for a in range(2):
            if a == 0:
                part = dot(rows[0], w_in[:, cut], 1, 0)
            else:
                part = dot(rows[1], w_out[cut, :], 1, 1)
            keep[a, :, cut] = part[:block]
            for d, out in enumerate((one, two, three), 1):
                out[a, :, cut] = part[d * block : (d + 1) * block].astype(BF16)


def add_blocks(at, keep, one, two, three, mine, first, second, third):
    width = mine.shape[2]
    for e, out in enumerate((mine, first, second, third)):
        start = pl.multiple_of(lax.rem(at[1] + e, N) * width, 128)
        cut = pl.ds(start, width)
        for a in range(2):
            total = keep[a, :, cut]
            for got in (one, two, three):
                total = total + got[a, :, cut].astype(F32)
            out[a] = total.astype(out.dtype)


def activate(mine, one, two, three, out):
    def total(a):
        return (
            mine[a] + one[a].astype(F32) + two[a].astype(F32) + three[a].astype(F32)
        )

    values, slopes = gelu_parts(total(0))
    out[0] = values.astype(BF16)
    out[1] = (total(1) * slopes).astype(BF16)


def assemble(at, mine, one, two, three, out):
    width = mine.shape[-1]
    for e, got in enumerate((mine, one, two, three)):
        start = pl.multiple_of(lax.rem(at[1] + N - e, N) * width, 128)
        for a in range(2):
            out[a, :, pl.ds(start, width)] = got[a]


def second_products(at, mine, one, two, three, w_in, w_out, hidden, keep, send):
    block = mine.shape[1]
    half = block // 2
    for a in range(2):
        for d, got in enumerate((mine, one, two, three)):
            hidden[a, d * block : (d + 1) * block] = got[a]
    for a in range(2):
        if a == 0:
            part = dot(hidden[0], w_out[...], 1, 0)
        else:
            part = dot(hidden[1], w_in[...], 1, 1)
        for d in range(N):
            k = lax.rem(at[0] + N - d, N)
            keep[k, a] = part[d * block : d * block + half]
            send[k, a] = part[d * block + half : (d + 1) * block].astype(BF16)


def add_halves(keep, got, base, *outs):
    for k, out in enumerate((base, *outs)):
        out[...] = (keep[k] + got[k].astype(F32)).astype(out.dtype)


def add_all(base, *refs):
    total = base[...]
    for got in refs[:-1]:
        total = total + got[...].astype(F32)
    refs[-1][...] = total.astype(BF16)


def weight_grad(rows, hidden, *rest, of_rows):
    *before, out, lhs = rest
    which = 0 if of_rows else 1
    block = rows.shape[1] // N
    for d in range(N):
        f = (N - d) % N
        lhs[d * block : (d + 1) * block] = rows[which, f * block : (f + 1) * block]
    width = 256
    for n in range(out.shape[0] // width):
        cut = slice(n * width, (n + 1) * width)
        if of_rows:
            part = dot(lhs[:, cut], hidden[1], 0, 0)
        else:
            part = dot(hidden[0, :, cut], lhs[...], 0, 0)
        if before:
            part = part + before[0][cut, :]
        out[cut, :] = part.astype(out.dtype)


def own_sum(tokens, grad_out, base, *refs):
    *parts, out = refs
    for a, source in enumerate((tokens, grad_out)):
        total = source[...].astype(F32) + base[a]
        for part in parts:
            total = total + part[a].astype(F32)
        out[a] = total


def final_sum(base, got, output, grad_tokens):
    for a, out in enumerate((output, grad_tokens)):
        out[...] = base[a] + got[a].astype(F32)


def keep_as_is(source, out):
    out[...] = source[...]


def shift(value, axis, step):
    return lax.ppermute(value, axis, [(i, (i + step) % N) for i in range(N)])


def swap(value, axis):
    return lax.ppermute(value, axis, [(0, 1), (1, 0)])


def shards(tokens, w_in, w_out, grad_out):
    half, width = tokens.shape
    hidden = w_in.shape[1]
    block = 2 * half
    cut = hidden // N
    at = jnp.stack([lax.axis_index("x"), lax.axis_index("zl")]).astype(jnp.int32)
    order = Order()
    product_flops = 4 * N * block * width * hidden

    mine = jnp.stack([tokens, grad_out])

    def send(values, axis):
        return [shift(s, axis, d) for d, s in enumerate(values, 1)]

    def first(rows):
        rows, keep, *out = order.call(
            first_products,
            [((2, N * block, width), BF16), ((2, block, hidden), F32)]
            + [((2, block, hidden), BF16)] * 3,
            at, rows, swap(rows, "core"), w_in, w_out,
        )
        return rows, keep, send(out, "x")

    def add(keep, got):
        keep, *out = order.call(
            add_blocks,
            [((2, block, cut), F32)] + [((2, block, cut), BF16)] * 3,
            at, keep, *got,
        )
        return keep, send(out, "zl")

    def act(keep, got):
        return order.call(activate, [((2, block, cut), BF16)], keep, *got)[0]

    def spread(wide):
        return [wide] + send([wide] * 3, "x")

    def second(wide, after=()):
        hid, keep, out = order.call(
            second_products,
            [
                ((2, N * block, hidden), BF16),
                ((N, 2, half, width), F32),
                ((N, 2, half, width), BF16),
            ],
            at, *wide, w_in, w_out, after=after,
        )
        return hid, keep, out

    part = ((2, half, width), BF16)

    def halves(keep, got):
        base, *out = order.call(
            add_halves, [((2, half, width), F32)] + [part] * 3, keep, swap(got, "core")
        )
        return base, send(out, "y")

    def grad(shape, of_rows, dtype, rows, hid, *before):
        return order.call(
            functools.partial(weight_grad, of_rows=of_rows),
            [(shape, dtype)],
            rows, hid, *before,
            scratch=[pltpu.VMEM(rows.shape[1:], BF16)],
        )[0]

    own = jnp.stack([mine] + [shift(mine, "y", -k) for k in range(1, N)])
    far = swap(own, "zh")
    rows_o, keep_o, got_o = first(own)
    (far,) = order.call(keep_as_is, [(far.shape, BF16)], far, after=got_o)
    rows_f, keep_f, got_f = first(far)
    keep_o, got_o = add(keep_o, got_o)
    piece_o = act(keep_o, got_o)
    got_o = send([piece_o] * 3, "zl")
    keep_f, got_f = add(keep_f, got_f)
    (wide_o,) = order.call(
        assemble, [((2, block, hidden), BF16)], at, piece_o, *got_o
    )
    wide_o = spread(wide_o)
    piece_f = act(keep_f, got_f)
    got_f = send([piece_f] * 3, "zl")
    hid_o, keep_o, got_o = second(wide_o, got_f)
    (wide_f,) = order.call(
        assemble, [((2, block, hidden), BF16)], at, piece_f, *got_f
    )
    wide_f = spread(wide_f)
    base, parts = halves(keep_o, got_o)
    (own_total,) = order.call(
        own_sum, [((2, half, width), F32)], tokens, grad_out, base, *parts
    )
    grad_in = grad((width, hidden), True, F32, rows_o, hid_o)
    grad_second = grad((hidden, width), False, F32, rows_o, hid_o)
    hid_f, keep_f, got_f = second(wide_f)
    base, parts = halves(keep_f, got_f)
    grad_in = grad((width, hidden), True, BF16, rows_f, hid_f, grad_in)
    (total,) = order.call(add_all, [part], base, *parts)
    got = swap(total, "zh")
    grad_second = grad((hidden, width), False, BF16, rows_f, hid_f, grad_second)
    output, grad_tokens = order.call(
        final_sum, [((half, width), F32)] * 2, own_total, got
    )
    return output, grad_tokens, grad_in, grad_second


def solution(mesh):
    fine = Mesh(mesh.devices.reshape(4, 2, 4, 4, 2), ("y", "core", "zl", "x", "zh"))
    row, col = ("y", "core", "zh"), ("zl", "x")
    by_token, in_spec, out_spec = P(row, col), P(col, row), P(row, col)
    return jax.shard_map(
        shards,
        mesh=fine,
        in_specs=(by_token, in_spec, out_spec, by_token),
        out_specs=(by_token, by_token, in_spec, out_spec),
        check_vma=False,
    )
```

time: 180 us -> 173 us (0.961); the launches traced: 180 us -> 171 us
  starting transfers between devices: 71.5 us -> 60.8 us
  Pallas kernels: 18.9 us -> 21.7 us
    ppermute x4 -> x0, starting transfers between devices: 13.2 us -> none  [shards(): parts.append(lax.ppermute(s, ('y', 'zh'), pairs))]
    ppermute x5 -> x6, waiting for transfers between devices: 3.03 us -> 12 us  [swap(): return lax.ppermute(value, axis, [(0, 1), (1, 0)])]
    ppermute x5 -> x6, starting transfers between devices: 9.73 us -> 17.2 us  [swap(): return lax.ppermute(value, axis, [(0, 1), (1, 0)])]
    ppermute x4 -> x0, waiting for transfers between devices: 7.39 us -> none  [shards(): parts.append(lax.ppermute(s, ('y', 'zh'), pairs))]
    ppermute x30 -> x33, starting transfers between devices: 48.5 us -> 43.6 us  [shift(): return lax.ppermute(value, axis, [(i, (i + step) % N) for i in range(N)])]
    ppermute x30 -> x33, waiting for transfers between devices: 74.2 us -> 71.2 us  [shift(): return lax.ppermute(value, axis, [(i, (i + step) % N) for i in range(N)])]
    pallas_call x14 -> x20, Pallas kernels: 18.9 us -> 21.7 us  [call(): pl.pallas_call(ordered, out_shape=[jax.ShapeDtypeStruct(s, d) for s, d in...]
  transfers between devices with their start and end apart: 39 -> 39, of which waited for: 17 -> 25; matrix products, arithmetic and copies ran while one was open for 0% -> 0% of each run, Pallas kernels for 10% -> 8%
where the time goes in v2:
time: 173 us; the launch traced here: 171 us
  waiting for transfers between devices  83.2 us (48%)
  starting transfers between devices  60.8 us (35%)
  Pallas kernels  21.7 us (13%)
  local copies, waits for them, and re-layouts  3.35 us (2%)
    ppermute x33, waiting for transfers between devices, shift(): return lax.ppermute(value, axis, [(i, (i + step) % N) for i in range(N)])  71.2 us
    ppermute x33, starting transfers between devices, shift(): return lax.ppermute(value, axis, [(i, (i + step) % N) for i in range(N)])  43.6 us
    pallas_call x20, Pallas kernels, call(): pl.pallas_call(ordered, out_shape=[jax.ShapeDtypeStruct(s, d) for s, d in...  21.7 us
    ppermute x6, starting transfers between devices, swap(): return lax.ppermute(value, axis, [(0, 1), (1, 0)])  17.2 us
    ppermute x6, waiting for transfers between devices, swap(): return lax.ppermute(value, axis, [(0, 1), (1, 0)])  12 us
  transfers between devices with their start and end apart: 39, of which 25 were waited for; matrix products, arithmetic and copies ran while one was open for 0% of the time, Pallas kernels for 8%

profile of v2, /device:TPU:1, one launch (start us, length us, event | category | flops | bytes accessed | tf_op | source)
XLA Modules:
  0.0 170.9 jit_solution(11797023471452452724)
XLA Ops:
  1.5 3.8 %collective-permute-start.1 = (bf16[2,40,768]{2,1,0:T(8,128)(2,1)S(1)}, bf16[2,40,768]{2,1,0:T(8,128)(2,1)S(1)}, u32[]{:S(2)}, u32[]{:S(2)}) collective-permute-start(bf16[2,40,768]{2,1,0:T(8,128)(2,1)S(1)} %get-tuple-element.133), channel_id=1, source_target_pairs={{0,128},{64,192},{128,0},{192,64},{1,129},{65,193},{129,1},{193,65... | collective-permute-start | bytes 368648 | tf_op jit(solution)/shard_map/ppermute | solution.py:186
  7.6 3.5 %collective-permute-done = bf16[2,40,768]{2,1,0:T(8,128)(2,1)S(1)} collective-permute-done((bf16[2,40,768]{2,1,0:T(8,128)(2,1)S(1)}, bf16[2,40,768]{2,1,0:T(8,128)(2,1)S(1)}, u32[]{:S(2)}, u32[]{:S(2)}) %collective-permute-start) | collective-permute-done | bytes 122912 | tf_op jit(solution)/shard_map/ppermute | solution.py:186
  11.1 1.9 %collective-permute-done.2 = bf16[2,40,768]{2,1,0:T(8,128)(2,1)S(1)} collective-permute-done((bf16[2,40,768]{2,1,0:T(8,128)(2,1)S(1)}, bf16[2,40,768]{2,1,0:T(8,128)(2,1)S(1)}, u32[]{:S(2)}, u32[]{:S(2)}) %collective-permute-start.2) | collective-permute-done | bytes 122912 | tf_op jit(solution)/shard_map/ppermute | solution.py:186
  14.3 6.3 %collective-permute-start.7 = (bf16[4,2,40,768]{3,2,1,0:T(8,128)(2,1)S(1)}, bf16[4,2,40,768]{3,2,1,0:T(8,128)(2,1)S(1)}, u32[]{:S(2)}, u32[]{:S(2)}) collective-permute-start(bf16[4,2,40,768]{3,2,1,0:T(8,128)(2,1)S(1)} %pad_maximum_fusion.refs_1_), channel_id=1, source_target_pairs={{0,1},{1,0},{2,3},{3,2},{4,5},{5,4},{6,7},{7,6},{8,9},{9,8},{10,11... | collective-permute-start | bytes 1474568 | tf_op jit(solution)/shard_map/ppermute | solution.py:190
  23.9 2.2 %shard_map.75 = (bf16[2,320,768]{2,1,0:T(8,128)(2,1)S(1)}, f32[2,80,1536]{2,1,0:T(8,128)S(1)}, bf16[2,80,1536]{2,1,0:T(8,128)(2,1)S(1)}, bf16[2,80,1536]{2,1,0:T...) custom-call(s32[2]{0:T(128)S(1)} %pad_add_fusion.refs_0_, ...), custom_call_target="tpu_custom_call" | custom-call | tf_op jit(solution)/shard_map/pallas_call | solution.py:50
  27.5 2.4 %collective-permute-start.5 = (bf16[2,80,1536]{2,1,0:T(8,128)(2,1)S(1)}, bf16[2,80,1536]{2,1,0:T(8,128)(2,1)S(1)}, u32[]{:S(2)}, u32[]{:S(2)}) collective-permute-start(bf16[2,80,1536]{2,1,0:T(8,128)(2,1)S(1)} %get-tuple-element.70), channel_id=1, source_target_pairs={{0,4},{2,6},{4,0},{6,2},{1,5},{3,7},{5,1},{7,3},{8,12},{10,14},{12... | collective-permute-start | bytes 1474568 | tf_op jit(solution)/shard_map/ppermute | solution.py:186
  31.1 3.2 %collective-permute-done.7.refs_0_ = bf16[4,2,40,768]{3,2,1,0:T(8,128)(2,1)S(1)} collective-permute-done((bf16[4,2,40,768]{3,2,1,0:T(8,128)(2,1)S(1)}, bf16[4,2,40,768]{3,2,1,0:T(8,128)(2,1)S(1)}, u32[]{:S(2)}, u32[]{:S(2)}) %collective-permute-start.7) | collective-permute-done | bytes 491552 | tf_op jit(solution)/shard_map/ppermute | solution.py:190
  34.3 5.7 %collective-permute-done.4.refs_1_.refs_2_ = bf16[2,80,1536]{2,1,0:T(8,128)(2,1)S(1)} collective-permute-done((bf16[2,80,1536]{2,1,0:T(8,128)(2,1)S(1)}, bf16[2,80,1536]{2,1,0:T(8,128)(2,1)S(1)}, u32[]{:S(2)}, u32[]{:S(2)}) %collective-permute-start.4) | collective-permute-done | bytes 491552 | tf_op jit(solution)/shard_map/ppermute | solution.py:186
  40.0 11.5 %collective-permute-done.5.refs_2_.refs_3_ = bf16[2,80,1536]{2,1,0:T(8,128)(2,1)S(1)} collective-permute-done((bf16[2,80,1536]{2,1,0:T(8,128)(2,1)S(1)}, bf16[2,80,1536]{2,1,0:T(8,128)(2,1)S(1)}, u32[]{:S(2)}, u32[]{:S(2)}) %collective-permute-start.5) | collective-permute-done | bytes 491552 | tf_op jit(solution)/shard_map/ppermute | solution.py:186
  54.2 2.2 %shard_map.77 = (bf16[2,320,768]{2,1,0:T(8,128)(2,1)S(1)}, f32[2,80,1536]{2,1,0:T(8,128)S(1)}, bf16[2,80,1536]{2,1,0:T(8,128)(2,1)S(1)}, bf16[2,80,1536]{2,1,0:T...) custom-call(s32[2]{0:T(128)S(1)} %pad_add_fusion.refs_0_, ...), custom_call_target="tpu_custom_call" | custom-call | tf_op jit(solution)/shard_map/pallas_call | solution.py:50
  57.6 2.1 %collective-permute-start.16 = (bf16[2,80,1536]{2,1,0:T(8,128)(2,1)S(1)}, bf16[2,80,1536]{2,1,0:T(8,128)(2,1)S(1)}, u32[]{:S(2)}, u32[]{:S(2)}) collective-permute-start(bf16[2,80,1536]{2,1,0:T(8,128)(2,1)S(1)} %get-tuple-element.84), channel_id=1, source_target_pairs={{0,4},{2,6},{4,0},{6,2},{1,5},{3,7},{5,1},{7,3},{8,12},{10,14},{12... | collective-permute-start | bytes 1474568 | tf_op jit(solution)/shard_map/ppermute | solution.py:186
  63.8 3.7 %collective-permute-done.9.refs_1_ = bf16[2,80,384]{2,1,0:T(8,128)(2,1)S(1)} collective-permute-done((bf16[2,80,384]{2,1,0:T(8,128)(2,1)S(1)}, bf16[2,80,384]{2,1,0:T(8,128)(2,1)S(1)}, u32[]{:S(2)}, u32[]{:S(2)}) %collective-permute-start.9) | collective-permute-done | bytes 122912 | tf_op jit(solution)/shard_map/ppermute | solution.py:186
  67.6 6.3 %collective-permute-done.10.refs_2_ = bf16[2,80,384]{2,1,0:T(8,128)(2,1)S(1)} collective-permute-done((bf16[2,80,384]{2,1,0:T(8,128)(2,1)S(1)}, bf16[2,80,384]{2,1,0:T(8,128)(2,1)S(1)}, u32[]{:S(2)}, u32[]{:S(2)}) %collective-permute-start.10) | collective-permute-done | bytes 122912 | tf_op jit(solution)/shard_map/ppermute | solution.py:186
  77.2 4.1 %collective-permute-done.16.refs_3_ = bf16[2,80,1536]{2,1,0:T(8,128)(2,1)S(1)} collective-permute-done((bf16[2,80,1536]{2,1,0:T(8,128)(2,1)S(1)}, bf16[2,80,1536]{2,1,0:T(8,128)(2,1)S(1)}, u32[]{:S(2)}, u32[]{:S(2)}) %collective-permute-start.16) | collective-permute-done | bytes 491552 | tf_op jit(solution)/shard_map/ppermute | solution.py:186
  84.5 3.2 %collective-permute-start.20 = (bf16[2,80,1536]{2,1,0:T(8,128)(2,1)S(1)}, bf16[2,80,1536]{2,1,0:T(8,128)(2,1)S(1)}, u32[]{:S(2)}, u32[]{:S(2)}) collective-permute-start(bf16[2,80,1536]{2,1,0:T(8,128)(2,1)S(1)} %get-tuple-element.88.refs_1_), channel_id=1, source_target_pairs={{0,6},{2,0},{4,2},{6,4},{1,7},{3,1},{5,3},{7,5},{8,14},{10,8},{12,... | collective-permute-start | bytes 1474568 | tf_op jit(solution)/shard_map/ppermute | solution.py:186
  90.4 3.7 %collective-permute-done.22.refs_2_ = bf16[2,80,384]{2,1,0:T(8,128)(2,1)S(1)} collective-permute-done((bf16[2,80,384]{2,1,0:T(8,128)(2,1)S(1)}, bf16[2,80,384]{2,1,0:T(8,128)(2,1)S(1)}, u32[]{:S(2)}, u32[]{:S(2)}) %collective-permute-start.22) | collective-permute-done | bytes 122912 | tf_op jit(solution)/shard_map/ppermute | solution.py:186
  94.7 3.3 %collective-permute-start.26 = (bf16[2,80,384]{2,1,0:T(8,128)(2,1)S(1)}, bf16[2,80,384]{2,1,0:T(8,128)(2,1)S(1)}, u32[]{:S(2)}, u32[]{:S(2)}) collective-permute-start(bf16[2,80,384]{2,1,0:T(8,128)(2,1)S(1)} %get-tuple-element.94.refs_1_), channel_id=1, source_target_pairs={{0,24},{8,0},{16,8},{24,16},{1,25},{9,1},{17,9},{25,17},{2,26},{10... | collective-permute-start | bytes 368648 | tf_op jit(solution)/shard_map/ppermute | solution.py:186
  98.0 1.9 %collective-permute-done.26.refs_9_.refs_4_ = bf16[2,80,384]{2,1,0:T(8,128)(2,1)S(1)} collective-permute-done((bf16[2,80,384]{2,1,0:T(8,128)(2,1)S(1)}, bf16[2,80,384]{2,1,0:T(8,128)(2,1)S(1)}, u32[]{:S(2)}, u32[]{:S(2)}) %collective-permute-start.26) | collective-permute-done | bytes 122912 | tf_op jit(solution)/shard_map/ppermute | solution.py:186
  101.7 3.3 %collective-permute-done.25.refs_8_.refs_3_ = bf16[2,80,384]{2,1,0:T(8,128)(2,1)S(1)} collective-permute-done((bf16[2,80,384]{2,1,0:T(8,128)(2,1)S(1)}, bf16[2,80,384]{2,1,0:T(8,128)(2,1)S(1)}, u32[]{:S(2)}, u32[]{:S(2)}) %collective-permute-start.25) | collective-permute-done | bytes 122912 | tf_op jit(solution)/shard_map/ppermute | solution.py:186
  106.5 4.5 %collective-permute-done.18.refs_2_ = bf16[2,80,1536]{2,1,0:T(8,128)(2,1)S(1)} collective-permute-done((bf16[2,80,1536]{2,1,0:T(8,128)(2,1)S(1)}, bf16[2,80,1536]{2,1,0:T(8,128)(2,1)S(1)}, u32[]{:S(2)}, u32[]{:S(2)}) %collective-permute-start.18) | collective-permute-done | bytes 491552 | tf_op jit(solution)/shard_map/ppermute | solution.py:186
  111.0 2.2 %shard_map.83 = (bf16[2,320,1536]{2,1,0:T(8,128)(2,1)S(1)}, f32[4,2,40,768]{3,2,1,0:T(8,128)S(1)}, bf16[4,2,40,768]{3,2,1,0:T(8,128)(2,1)S(1)}, f32[8,128]{1,0:T(8,128)S(1)}) custom-call(s32[2]{0:T(128)S(1)} %pad_add_fusion.refs_0_, bf16[2,80,1536]{2,1,0:T(8,128)(2,1)S(1)} %get-tuple-element.88.refs_1_, ...), custom_call_target="tpu_custom_call" | custom-call | tf_op jit(solution)/shard_map/pallas_call | solution.py:50
  113.3 6.5 %collective-permute-start.27 = (bf16[4,2,40,768]{3,2,1,0:T(8,128)(2,1)S(1)}, bf16[4,2,40,768]{3,2,1,0:T(8,128)(2,1)S(1)}, u32[]{:S(2)}, u32[]{:S(2)}) collective-permute-start(bf16[4,2,40,768]{3,2,1,0:T(8,128)(2,1)S(1)} %get-tuple-element.97), channel_id=1, source_target_pairs={{0,32},{32,0},{1,33},{33,1},{2,34},{34,2},{3,35},{35,3},{4,36},{36... | collective-permute-start | bytes 1474568 | tf_op jit(solution)/shard_map/ppermute | solution.py:190
  121.5 3.0 %collective-permute-start.32 = (bf16[2,80,1536]{2,1,0:T(8,128)(2,1)S(1)}, bf16[2,80,1536]{2,1,0:T(8,128)(2,1)S(1)}, u32[]{:S(2)}, u32[]{:S(2)}) collective-permute-start(bf16[2,80,1536]{2,1,0:T(8,128)(2,1)S(1)} %get-tuple-element.106.refs_1_), channel_id=1, source_target_pairs={{0,4},{2,6},{4,0},{6,2},{1,5},{3,7},{5,1},{7,3},{8,12},{10,14},{12... | collective-permute-start | bytes 1474568 | tf_op jit(solution)/shard_map/ppermute | solution.py:186
  125.6 2.5 %collective-permute-start.29 = (bf16[2,40,768]{2,1,0:T(8,128)(2,1)S(1)}, bf16[2,40,768]{2,1,0:T(8,128)(2,1)S(1)}, u32[]{:S(2)}, u32[]{:S(2)}) collective-permute-start(bf16[2,40,768]{2,1,0:T(8,128)(2,1)S(1)} %get-tuple-element.102), channel_id=1, source_target_pairs={{0,128},{64,192},{128,0},{192,64},{1,129},{65,193},{129,1},{193,65... | collective-permute-start | bytes 368648 | tf_op jit(solution)/shard_map/ppermute | solution.py:186
  128.1 2.5 %collective-permute-done.28.refs_3_ = bf16[2,40,768]{2,1,0:T(8,128)(2,1)S(1)} collective-permute-done((bf16[2,40,768]{2,1,0:T(8,128)(2,1)S(1)}, bf16[2,40,768]{2,1,0:T(8,128)(2,1)S(1)}, u32[]{:S(2)}, u32[]{:S(2)}) %collective-permute-start.28) | collective-permute-done | bytes 122912 | tf_op jit(solution)/shard_map/ppermute | solution.py:186
  130.9 2.3 %collective-permute-done.29.refs_4_ = bf16[2,40,768]{2,1,0:T(8,128)(2,1)S(1)} collective-permute-done((bf16[2,40,768]{2,1,0:T(8,128)(2,1)S(1)}, bf16[2,40,768]{2,1,0:T(8,128)(2,1)S(1)}, u32[]{:S(2)}, u32[]{:S(2)}) %collective-permute-start.29) | collective-permute-done | bytes 122912 | tf_op jit(solution)/shard_map/ppermute | solution.py:186
  137.5 9.3 %collective-permute-done.31.refs_2_ = bf16[2,80,1536]{2,1,0:T(8,128)(2,1)S(1)} collective-permute-done((bf16[2,80,1536]{2,1,0:T(8,128)(2,1)S(1)}, bf16[2,80,1536]{2,1,0:T(8,128)(2,1)S(1)}, u32[]{:S(2)}, u32[]{:S(2)}) %collective-permute-start.31) | collective-permute-done | bytes 491552 | tf_op jit(solution)/shard_map/ppermute | solution.py:186
  146.8 2.3 %shard_map.89 = (bf16[2,320,1536]{2,1,0:T(8,128)(2,1)S(1)}, f32[4,2,40,768]{3,2,1,0:T(8,128)S(1)}, bf16[4,2,40,768]{3,2,1,0:T(8,128)(2,1)S(1)}, f32[8,128]{1,0:T(8,128)S(1)}) custom-call(s32[2]{0:T(128)S(1)} %pad_add_fusion.refs_0_, bf16[2,80,1536]{2,1,0:T(8,128)(2,1)S(1)} %get-tuple-element.106.refs_1_, ...), custom_call_target="tpu_custom_call" | custom-call | tf_op jit(solution)/shard_map/pallas_call | solution.py:50
  151.5 2.5 %collective-permute-start.36 = (bf16[2,40,768]{2,1,0:T(8,128)(2,1)S(1)}, bf16[2,40,768]{2,1,0:T(8,128)(2,1)S(1)}, u32[]{:S(2)}, u32[]{:S(2)}) collective-permute-start(bf16[2,40,768]{2,1,0:T(8,128)(2,1)S(1)} %get-tuple-element.117), channel_id=1, source_target_pairs={{0,128},{64,192},{128,0},{192,64},{1,129},{65,193},{129,1},{193,65... | collective-permute-start | bytes 368648 | tf_op jit(solution)/shard_map/ppermute | solution.py:186
  155.1 2.8 %shard_map.91 = (bf16[768,1536]{1,0:T(8,128)(2,1)}, f32[8,128]{1,0:T(8,128)S(1)}) custom-call(bf16[2,320,768]{2,1,0:T(8,128)(2,1)S(1)} %get-tuple-element.119.refs_0_, bf16[2,320,1536]{2,1,0:T(8,128)(2,1)S(1)} %get-tuple-element.120.refs_1_, f32[768,1536]{1,0:T(8,128)S(1)} %get-tuple-element.121.refs_2_, f32[8,128]{1,0:T(8,128)S(1)} %get-tuple-element.122.refs_3_), custom_call_target="tpu_custom_call" | custom-call | tf_op jit(solution)/shard_map/pallas_call | solution.py:50
  161.5 2.8 %shard_map.93 = (bf16[1536,768]{1,0:T(8,128)(2,1)}, f32[8,128]{1,0:T(8,128)S(1)}) custom-call(bf16[2,320,768]{2,1,0:T(8,128)(2,1)S(1)} %get-tuple-element.119.refs_0_, bf16[2,320,1536]{2,1,0:T(8,128)(2,1)S(1)} %get-tuple-element.120.refs_1_, f32[1536,768]{1,0:T(8,128)S(1)} %get-tuple-element.125.refs_2_, f32[8,128]{1,0:T(8,128)S(1)} %get-tuple-element.126.refs_3_), custom_call_target="tpu_custom_call" | custom-call | tf_op jit(solution)/shard_map/pallas_call | solution.py:50
  164.3 5.8 %collective-permute-done.38.refs_1_ = bf16[2,40,768]{2,1,0:T(8,128)(2,1)S(1)} collective-permute-done((bf16[2,40,768]{2,1,0:T(8,128)(2,1)S(1)}, bf16[2,40,768]{2,1,0:T(8,128)(2,1)S(1)}, u32[]{:S(2)}, u32[]{:S(2)}) %collective-permute-start.38) | collective-permute-done | bytes 122912 | tf_op jit(solution)/shard_map/ppermute | solution.py:190
  (81 shorter events, 46.6 us)
Async XLA Ops:
  1.5 6.1 %collective-permute-start.1 = (bf16[2,40,768]{2,1,0:T(8,128)(2,1)S(1)}, bf16[2,40,768]{2,1,0:T(8,128)(2,1)S(1)}, u32[]{:S(2)}, u32[]{:S(2)}) collective-permute-start(bf16[2,40,768]{2,1,0:T(8,128)(2,1)S(1)} %get-tuple-element.133), channel_id=1, source_target_pairs={{0,128},{64,192},{128,0},{192,64},{1,129},{65,193},{129,1},{193,65... | collective-permute-start | bytes 368648 | tf_op jit(solution)/shard_map/ppermute | solution.py:186
  5.3 5.8 %collective-permute-start = (bf16[2,40,768]{2,1,0:T(8,128)(2,1)S(1)}, bf16[2,40,768]{2,1,0:T(8,128)(2,1)S(1)}, u32[]{:S(2)}, u32[]{:S(2)}) collective-permute-start(bf16[2,40,768]{2,1,0:T(8,128)(2,1)S(1)} %get-tuple-element.133), channel_id=1, source_target_pairs={{0,192},{64,0},{128,64},{192,128},{1,193},{65,1},{129,65},{193,129... | collective-permute-start | bytes 368648 | tf_op jit(solution)/shard_map/ppermute | solution.py:186
  6.1 6.9 %collective-permute-start.2 = (bf16[2,40,768]{2,1,0:T(8,128)(2,1)S(1)}, bf16[2,40,768]{2,1,0:T(8,128)(2,1)S(1)}, u32[]{:S(2)}, u32[]{:S(2)}) collective-permute-start(bf16[2,40,768]{2,1,0:T(8,128)(2,1)S(1)} %get-tuple-element.133), channel_id=1, source_target_pairs={{0,64},{64,128},{128,192},{192,0},{1,65},{65,129},{129,193},{193,1... | collective-permute-start | bytes 368648 | tf_op jit(solution)/shard_map/ppermute | solution.py:186
  13.0 7.6 %collective-permute-start.3 = (bf16[4,2,40,768]{3,2,1,0:T(8,128)(2,1)S(1)}, bf16[4,2,40,768]{3,2,1,0:T(8,128)(2,1)S(1)}, u32[]{:S(2)}, u32[]{:S(2)}) collective-permute-start(bf16[4,2,40,768]{3,2,1,0:T(8,128)(2,1)S(1)} %pad_maximum_fusion.refs_1_), channel_id=1, source_target_pairs={{0,32},{32,0},{1,33},{33,1},{2,34},{34,2},{3,35},{35,3},{4,36},{36... | collective-permute-start | bytes 1474568 | tf_op jit(solution)/shard_map/ppermute | solution.py:190
  14.3 19.9 %collective-permute-start.7 = (bf16[4,2,40,768]{3,2,1,0:T(8,128)(2,1)S(1)}, bf16[4,2,40,768]{3,2,1,0:T(8,128)(2,1)S(1)}, u32[]{:S(2)}, u32[]{:S(2)}) collective-permute-start(bf16[4,2,40,768]{3,2,1,0:T(8,128)(2,1)S(1)} %pad_maximum_fusion.refs_1_), channel_id=1, source_target_pairs={{0,1},{1,0},{2,3},{3,2},{4,5},{5,4},{6,7},{7,6},{8,9},{9,8},{10,11... | collective-permute-start | bytes 1474568 | tf_op jit(solution)/shard_map/ppermute | solution.py:190
  26.2 13.8 %collective-permute-start.4 = (bf16[2,80,1536]{2,1,0:T(8,128)(2,1)S(1)}, bf16[2,80,1536]{2,1,0:T(8,128)(2,1)S(1)}, u32[]{:S(2)}, u32[]{:S(2)}) collective-permute-start(bf16[2,80,1536]{2,1,0:T(8,128)(2,1)S(1)} %get-tuple-element.69), channel_id=1, source_target_pairs={{0,2},{2,4},{4,6},{6,0},{1,3},{3,5},{5,7},{7,1},{8,10},{10,12},{12... | collective-permute-start | bytes 1474568 | tf_op jit(solution)/shard_map/ppermute | solution.py:186
  27.5 24.0 %collective-permute-start.5 = (bf16[2,80,1536]{2,1,0:T(8,128)(2,1)S(1)}, bf16[2,80,1536]{2,1,0:T(8,128)(2,1)S(1)}, u32[]{:S(2)}, u32[]{:S(2)}) collective-permute-start(bf16[2,80,1536]{2,1,0:T(8,128)(2,1)S(1)} %get-tuple-element.70), channel_id=1, source_target_pairs={{0,4},{2,6},{4,0},{6,2},{1,5},{3,7},{5,1},{7,3},{8,12},{10,14},{12... | collective-permute-start | bytes 1474568 | tf_op jit(solution)/shard_map/ppermute | solution.py:186
  29.9 21.6 %collective-permute-start.6 = (bf16[2,80,1536]{2,1,0:T(8,128)(2,1)S(1)}, bf16[2,80,1536]{2,1,0:T(8,128)(2,1)S(1)}, u32[]{:S(2)}, u32[]{:S(2)}) collective-permute-start(bf16[2,80,1536]{2,1,0:T(8,128)(2,1)S(1)} %get-tuple-element.71), channel_id=1, source_target_pairs={{0,6},{2,0},{4,2},{6,4},{1,7},{3,1},{5,3},{7,5},{8,14},{10,8},{12,... | collective-permute-start | bytes 1474568 | tf_op jit(solution)/shard_map/ppermute | solution.py:186
  56.5 20.7 %collective-permute-start.15 = (bf16[2,80,1536]{2,1,0:T(8,128)(2,1)S(1)}, bf16[2,80,1536]{2,1,0:T(8,128)(2,1)S(1)}, u32[]{:S(2)}, u32[]{:S(2)}) collective-permute-start(bf16[2,80,1536]{2,1,0:T(8,128)(2,1)S(1)} %get-tuple-element.83), channel_id=1, source_target_pairs={{0,2},{2,4},{4,6},{6,0},{1,3},{3,5},{5,7},{7,1},{8,10},{10,12},{12... | collective-permute-start | bytes 1474568 | tf_op jit(solution)/shard_map/ppermute | solution.py:186
  57.6 23.6 %collective-permute-start.16 = (bf16[2,80,1536]{2,1,0:T(8,128)(2,1)S(1)}, bf16[2,80,1536]{2,1,0:T(8,128)(2,1)S(1)}, u32[]{:S(2)}, u32[]{:S(2)}) collective-permute-start(bf16[2,80,1536]{2,1,0:T(8,128)(2,1)S(1)} %get-tuple-element.84), channel_id=1, source_target_pairs={{0,4},{2,6},{4,0},{6,2},{1,5},{3,7},{5,1},{7,3},{8,12},{10,14},{12... | collective-permute-start | bytes 1474568 | tf_op jit(solution)/shard_map/ppermute | solution.py:186
  59.7 21.5 %collective-permute-start.17 = (bf16[2,80,1536]{2,1,0:T(8,128)(2,1)S(1)}, bf16[2,80,1536]{2,1,0:T(8,128)(2,1)S(1)}, u32[]{:S(2)}, u32[]{:S(2)}) collective-permute-start(bf16[2,80,1536]{2,1,0:T(8,128)(2,1)S(1)} %get-tuple-element.85), channel_id=1, source_target_pairs={{0,6},{2,0},{4,2},{6,4},{1,7},{3,1},{5,3},{7,5},{8,14},{10,8},{12,... | collective-permute-start | bytes 1474568 | tf_op jit(solution)/shard_map/ppermute | solution.py:186
  61.8 5.7 %collective-permute-start.9 = (bf16[2,80,384]{2,1,0:T(8,128)(2,1)S(1)}, bf16[2,80,384]{2,1,0:T(8,128)(2,1)S(1)}, u32[]{:S(2)}, u32[]{:S(2)}) collective-permute-start(bf16[2,80,384]{2,1,0:T(8,128)(2,1)S(1)} %get-tuple-element.77), channel_id=1, source_target_pairs={{0,8},{8,16},{16,24},{24,0},{1,9},{9,17},{17,25},{25,1},{2,10},{10... | collective-permute-start | bytes 368648 | tf_op jit(solution)/shard_map/ppermute | solution.py:186
  62.6 11.2 %collective-permute-start.10 = (bf16[2,80,384]{2,1,0:T(8,128)(2,1)S(1)}, bf16[2,80,384]{2,1,0:T(8,128)(2,1)S(1)}, u32[]{:S(2)}, u32[]{:S(2)}) collective-permute-start(bf16[2,80,384]{2,1,0:T(8,128)(2,1)S(1)} %get-tuple-element.78), channel_id=1, source_target_pairs={{0,16},{8,24},{16,0},{24,8},{1,17},{9,25},{17,1},{25,9},{2,18},{10... | collective-permute-start | bytes 368648 | tf_op jit(solution)/shard_map/ppermute | solution.py:186
  67.5 6.3 %collective-permute-start.11 = (bf16[2,80,384]{2,1,0:T(8,128)(2,1)S(1)}, bf16[2,80,384]{2,1,0:T(8,128)(2,1)S(1)}, u32[]{:S(2)}, u32[]{:S(2)}) collective-permute-start(bf16[2,80,384]{2,1,0:T(8,128)(2,1)S(1)} %get-tuple-element.79), channel_id=1, source_target_pairs={{0,24},{8,0},{16,8},{24,16},{1,25},{9,1},{17,9},{25,17},{2,26},{10... | collective-permute-start | bytes 368648 | tf_op jit(solution)/shard_map/ppermute | solution.py:186
  74.0 8.8 %collective-permute-start.14 = (bf16[2,80,384]{2,1,0:T(8,128)(2,1)S(1)}, bf16[2,80,384]{2,1,0:T(8,128)(2,1)S(1)}, u32[]{:S(2)}, u32[]{:S(2)}) collective-permute-start(bf16[2,80,384]{2,1,0:T(8,128)(2,1)S(1)} %get-tuple-element.81.refs_1_), channel_id=1, source_target_pairs={{0,24},{8,0},{16,8},{24,16},{1,25},{9,1},{17,9},{25,17},{2,26},{10... | collective-permute-start | bytes 368648 | tf_op jit(solution)/shard_map/ppermute | solution.py:186
  75.4 8.5 %collective-permute-start.13 = (bf16[2,80,384]{2,1,0:T(8,128)(2,1)S(1)}, bf16[2,80,384]{2,1,0:T(8,128)(2,1)S(1)}, u32[]{:S(2)}, u32[]{:S(2)}) collective-permute-start(bf16[2,80,384]{2,1,0:T(8,128)(2,1)S(1)} %get-tuple-element.81.refs_1_), channel_id=1, source_target_pairs={{0,16},{8,24},{16,0},{24,8},{1,17},{9,25},{17,1},{25,9},{2,18},{10... | collective-permute-start | bytes 368648 | tf_op jit(solution)/shard_map/ppermute | solution.py:186
  77.2 6.7 %collective-permute-start.12 = (bf16[2,80,384]{2,1,0:T(8,128)(2,1)S(1)}, bf16[2,80,384]{2,1,0:T(8,128)(2,1)S(1)}, u32[]{:S(2)}, u32[]{:S(2)}) collective-permute-start(bf16[2,80,384]{2,1,0:T(8,128)(2,1)S(1)} %get-tuple-element.81.refs_1_), channel_id=1, source_target_pairs={{0,8},{8,16},{16,24},{24,0},{1,9},{9,17},{17,25},{25,1},{2,10},{10... | collective-permute-start | bytes 368648 | tf_op jit(solution)/shard_map/ppermute | solution.py:186
  82.0 7.5 %collective-permute-start.21 = (bf16[2,80,384]{2,1,0:T(8,128)(2,1)S(1)}, bf16[2,80,384]{2,1,0:T(8,128)(2,1)S(1)}, u32[]{:S(2)}, u32[]{:S(2)}) collective-permute-start(bf16[2,80,384]{2,1,0:T(8,128)(2,1)S(1)} %get-tuple-element.90), channel_id=1, source_target_pairs={{0,8},{8,16},{16,24},{24,0},{1,9},{9,17},{17,25},{25,1},{2,10},{10... | collective-permute-start | bytes 368648 | tf_op jit(solution)/shard_map/ppermute | solution.py:186
  84.5 22.0 %collective-permute-start.20 = (bf16[2,80,1536]{2,1,0:T(8,128)(2,1)S(1)}, bf16[2,80,1536]{2,1,0:T(8,128)(2,1)S(1)}, u32[]{:S(2)}, u32[]{:S(2)}) collective-permute-start(bf16[2,80,1536]{2,1,0:T(8,128)(2,1)S(1)} %get-tuple-element.88.refs_1_), channel_id=1, source_target_pairs={{0,6},{2,0},{4,2},{6,4},{1,7},{3,1},{5,3},{7,5},{8,14},{10,8},{12,... | collective-permute-start | bytes 1474568 | tf_op jit(solution)/shard_map/ppermute | solution.py:186
  87.7 18.8 %collective-permute-start.19 = (bf16[2,80,1536]{2,1,0:T(8,128)(2,1)S(1)}, bf16[2,80,1536]{2,1,0:T(8,128)(2,1)S(1)}, u32[]{:S(2)}, u32[]{:S(2)}) collective-permute-start(bf16[2,80,1536]{2,1,0:T(8,128)(2,1)S(1)} %get-tuple-element.88.refs_1_), channel_id=1, source_target_pairs={{0,4},{2,6},{4,0},{6,2},{1,5},{3,7},{5,1},{7,3},{8,12},{10,14},{12... | collective-permute-start | bytes 1474568 | tf_op jit(solution)/shard_map/ppermute | solution.py:186
  87.7 23.3 %collective-permute-start.18 = (bf16[2,80,1536]{2,1,0:T(8,128)(2,1)S(1)}, bf16[2,80,1536]{2,1,0:T(8,128)(2,1)S(1)}, u32[]{:S(2)}, u32[]{:S(2)}) collective-permute-start(bf16[2,80,1536]{2,1,0:T(8,128)(2,1)S(1)} %get-tuple-element.88.refs_1_), channel_id=1, source_target_pairs={{0,2},{2,4},{4,6},{6,0},{1,3},{3,5},{5,7},{7,1},{8,10},{10,12},{12... | collective-permute-start | bytes 1474568 | tf_op jit(solution)/shard_map/ppermute | solution.py:186
  98.0 7.0 %collective-permute-start.25 = (bf16[2,80,384]{2,1,0:T(8,128)(2,1)S(1)}, bf16[2,80,384]{2,1,0:T(8,128)(2,1)S(1)}, u32[]{:S(2)}, u32[]{:S(2)}) collective-permute-start(bf16[2,80,384]{2,1,0:T(8,128)(2,1)S(1)} %get-tuple-element.94.refs_1_), channel_id=1, source_target_pairs={{0,16},{8,24},{16,0},{24,8},{1,17},{9,25},{17,1},{25,9},{2,18},{10... | collective-permute-start | bytes 368648 | tf_op jit(solution)/shard_map/ppermute | solution.py:186
  99.9 6.6 %collective-permute-start.24 = (bf16[2,80,384]{2,1,0:T(8,128)(2,1)S(1)}, bf16[2,80,384]{2,1,0:T(8,128)(2,1)S(1)}, u32[]{:S(2)}, u32[]{:S(2)}) collective-permute-start(bf16[2,80,384]{2,1,0:T(8,128)(2,1)S(1)} %get-tuple-element.94.refs_1_), channel_id=1, source_target_pairs={{0,8},{8,16},{16,24},{24,0},{1,9},{9,17},{17,25},{25,1},{2,10},{10... | collective-permute-start | bytes 368648 | tf_op jit(solution)/shard_map/ppermute | solution.py:186
  113.3 11.8 %collective-permute-start.27 = (bf16[4,2,40,768]{3,2,1,0:T(8,128)(2,1)S(1)}, bf16[4,2,40,768]{3,2,1,0:T(8,128)(2,1)S(1)}, u32[]{:S(2)}, u32[]{:S(2)}) collective-permute-start(bf16[4,2,40,768]{3,2,1,0:T(8,128)(2,1)S(1)} %get-tuple-element.97), channel_id=1, source_target_pairs={{0,32},{32,0},{1,33},{33,1},{2,34},{34,2},{3,35},{35,3},{4,36},{36... | collective-permute-start | bytes 1474568 | tf_op jit(solution)/shard_map/ppermute | solution.py:190
  120.4 17.1 %collective-permute-start.33 = (bf16[2,80,1536]{2,1,0:T(8,128)(2,1)S(1)}, bf16[2,80,1536]{2,1,0:T(8,128)(2,1)S(1)}, u32[]{:S(2)}, u32[]{:S(2)}) collective-permute-start(bf16[2,80,1536]{2,1,0:T(8,128)(2,1)S(1)} %get-tuple-element.106.refs_1_), channel_id=1, source_target_pairs={{0,6},{2,0},{4,2},{6,4},{1,7},{3,1},{5,3},{7,5},{8,14},{10,8},{12,... | collective-permute-start | bytes 1474568 | tf_op jit(solution)/shard_map/ppermute | solution.py:186
  121.5 16.0 %collective-permute-start.32 = (bf16[2,80,1536]{2,1,0:T(8,128)(2,1)S(1)}, bf16[2,80,1536]{2,1,0:T(8,128)(2,1)S(1)}, u32[]{:S(2)}, u32[]{:S(2)}) collective-permute-start(bf16[2,80,1536]{2,1,0:T(8,128)(2,1)S(1)} %get-tuple-element.106.refs_1_), channel_id=1, source_target_pairs={{0,4},{2,6},{4,0},{6,2},{1,5},{3,7},{5,1},{7,3},{8,12},{10,14},{12... | collective-permute-start | bytes 1474568 | tf_op jit(solution)/shard_map/ppermute | solution.py:186
  124.6 22.2 %collective-permute-start.31 = (bf16[2,80,1536]{2,1,0:T(8,128)(2,1)S(1)}, bf16[2,80,1536]{2,1,0:T(8,128)(2,1)S(1)}, u32[]{:S(2)}, u32[]{:S(2)}) collective-permute-start(bf16[2,80,1536]{2,1,0:T(8,128)(2,1)S(1)} %get-tuple-element.106.refs_1_), channel_id=1, source_target_pairs={{0,2},{2,4},{4,6},{6,0},{1,3},{3,5},{5,7},{7,1},{8,10},{10,12},{12... | collective-permute-start | bytes 1474568 | tf_op jit(solution)/shard_map/ppermute | solution.py:186
  125.6 7.7 %collective-permute-start.29 = (bf16[2,40,768]{2,1,0:T(8,128)(2,1)S(1)}, bf16[2,40,768]{2,1,0:T(8,128)(2,1)S(1)}, u32[]{:S(2)}, u32[]{:S(2)}) collective-permute-start(bf16[2,40,768]{2,1,0:T(8,128)(2,1)S(1)} %get-tuple-element.102), channel_id=1, source_target_pairs={{0,128},{64,192},{128,0},{192,64},{1,129},{65,193},{129,1},{193,65... | collective-permute-start | bytes 368648 | tf_op jit(solution)/shard_map/ppermute | solution.py:186
  151.2 6.8 %collective-permute-start.35 = (bf16[2,40,768]{2,1,0:T(8,128)(2,1)S(1)}, bf16[2,40,768]{2,1,0:T(8,128)(2,1)S(1)}, u32[]{:S(2)}, u32[]{:S(2)}) collective-permute-start(bf16[2,40,768]{2,1,0:T(8,128)(2,1)S(1)} %get-tuple-element.116), channel_id=1, source_target_pairs={{0,64},{64,128},{128,192},{192,0},{1,65},{65,129},{129,193},{193,1... | collective-permute-start | bytes 368648 | tf_op jit(solution)/shard_map/ppermute | solution.py:186
  151.5 8.2 %collective-permute-start.36 = (bf16[2,40,768]{2,1,0:T(8,128)(2,1)S(1)}, bf16[2,40,768]{2,1,0:T(8,128)(2,1)S(1)}, u32[]{:S(2)}, u32[]{:S(2)}) collective-permute-start(bf16[2,40,768]{2,1,0:T(8,128)(2,1)S(1)} %get-tuple-element.117), channel_id=1, source_target_pairs={{0,128},{64,192},{128,0},{192,64},{1,129},{65,193},{129,1},{193,65... | collective-permute-start | bytes 368648 | tf_op jit(solution)/shard_map/ppermute | solution.py:186
  154.1 5.9 %collective-permute-start.37 = (bf16[2,40,768]{2,1,0:T(8,128)(2,1)S(1)}, bf16[2,40,768]{2,1,0:T(8,128)(2,1)S(1)}, u32[]{:S(2)}, u32[]{:S(2)}) collective-permute-start(bf16[2,40,768]{2,1,0:T(8,128)(2,1)S(1)} %get-tuple-element.118), channel_id=1, source_target_pairs={{0,192},{64,0},{128,64},{192,128},{1,193},{65,1},{129,65},{193,129... | collective-permute-start | bytes 368648 | tf_op jit(solution)/shard_map/ppermute | solution.py:186
  160.0 10.2 %collective-permute-start.38 = (bf16[2,40,768]{2,1,0:T(8,128)(2,1)S(1)}, bf16[2,40,768]{2,1,0:T(8,128)(2,1)S(1)}, u32[]{:S(2)}, u32[]{:S(2)}) collective-permute-start(bf16[2,40,768]{2,1,0:T(8,128)(2,1)S(1)} %get-tuple-element.124), channel_id=1, source_target_pairs={{0,1},{1,0},{2,3},{3,2},{4,5},{5,4},{6,7},{7,6},{8,9},{9,8},{10,11... | collective-permute-start | bytes 368648 | tf_op jit(solution)/shard_map/ppermute | solution.py:190
  (13 other events, 141.0 us)

commit v3 on v2

--- a/solution.py
+++ b/solution.py
@@ -252,6 +252,7 @@
             functools.partial(weight_grad, of_rows=of_rows),
             [(shape, dtype)],
             rows, hid, *before,
+            flops=product_flops // 2, traffic=8 << 20,
             scratch=[pltpu.VMEM(rows.shape[1:], BF16)],
         )[0]
 
@@ -270,17 +271,17 @@
     wide_o = spread(wide_o)
     piece_f = act(keep_f, got_f)
     got_f = send([piece_f] * 3, "zl")
-    hid_o, keep_o, got_o = second(wide_o, got_f)
     (wide_f,) = order.call(
-        assemble, [((2, block, hidden), BF16)], at, piece_f, *got_f
+        assemble, [((2, block, hidden), BF16)], at, piece_f, *got_f, after=wide_o[1:]
     )
     wide_f = spread(wide_f)
+    hid_o, keep_o, got_o = second(wide_o)
+    grad_in = grad((width, hidden), True, F32, rows_o, hid_o)
+    grad_second = grad((hidden, width), False, F32, rows_o, hid_o)
     base, parts = halves(keep_o, got_o)
     (own_total,) = order.call(
         own_sum, [((2, half, width), F32)], tokens, grad_out, base, *parts
     )
-    grad_in = grad((width, hidden), True, F32, rows_o, hid_o)
-    grad_second = grad((hidden, width), False, F32, rows_o, hid_o)
     hid_f, keep_f, got_f = second(wide_f)
     base, parts = halves(keep_f, got_f)
     grad_in = grad((width, hidden), True, BF16, rows_f, hid_f, grad_in)

time: 173 us -> 170 us (0.983)
  waiting for transfers between devices: 83.2 us -> 72.9 us
  starting transfers between devices: 60.8 us -> 69 us
    ppermute x33, waiting for transfers between devices: 71.2 us -> 60.8 us  [shift(): return lax.ppermute(value, axis, [(i, (i + step) % N) for i in range(N)])]
    ppermute x33, starting transfers between devices: 43.6 us -> 52.7 us  [shift(): return lax.ppermute(value, axis, [(i, (i + step) % N) for i in range(N)])]
  transfers between devices with their start and end apart: 39 -> 39, of which waited for: 25 -> 20; matrix products, arithmetic and copies ran while one was open for 0% -> 0% of each run, Pallas kernels for 8% -> 8%
where the time goes in v3:
time: 170 us; the launch traced here: 169 us
  waiting for transfers between devices  72.9 us (43%)
  starting transfers between devices  69 us (41%)
  Pallas kernels  21.8 us (13%)
  local copies, waits for them, and re-layouts  3.35 us (2%)
    ppermute x33, waiting for transfers between devices, shift(): return lax.ppermute(value, axis, [(i, (i + step) % N) for i in range(N)])  60.8 us
    ppermute x33, starting transfers between devices, shift(): return lax.ppermute(value, axis, [(i, (i + step) % N) for i in range(N)])  52.7 us
    pallas_call x20, Pallas kernels, call(): pl.pallas_call(ordered, out_shape=[jax.ShapeDtypeStruct(s, d) for s, d in...  21.8 us
    ppermute x6, starting transfers between devices, swap(): return lax.ppermute(value, axis, [(0, 1), (1, 0)])  16.4 us
    ppermute x6, waiting for transfers between devices, swap(): return lax.ppermute(value, axis, [(0, 1), (1, 0)])  12.1 us
  transfers between devices with their start and end apart: 39, of which 20 were waited for; matrix products, arithmetic and copies ran while one was open for 0% of the time, Pallas kernels for 8%

profile of v3, /device:TPU:1, one launch (start us, length us, event | category | flops | bytes accessed | tf_op | source)
XLA Modules:
  0.0 168.9 jit_solution(2099986032119429052)
XLA Ops:
  1.5 2.2 %collective-permute-start.2 = (bf16[2,40,768]{2,1,0:T(8,128)(2,1)S(1)}, bf16[2,40,768]{2,1,0:T(8,128)(2,1)S(1)}, u32[]{:S(2)}, u32[]{:S(2)}) collective-permute-start(bf16[2,40,768]{2,1,0:T(8,128)(2,1)S(1)} %get-tuple-element.133), channel_id=1, source_target_pairs={{0,64},{64,128},{128,192},{192,0},{1,65},{65,129},{129,193},{193,1... | collective-permute-start | bytes 368648 | tf_op jit(solution)/shard_map/ppermute | solution.py:186
  3.7 2.6 %collective-permute-start.1 = (bf16[2,40,768]{2,1,0:T(8,128)(2,1)S(1)}, bf16[2,40,768]{2,1,0:T(8,128)(2,1)S(1)}, u32[]{:S(2)}, u32[]{:S(2)}) collective-permute-start(bf16[2,40,768]{2,1,0:T(8,128)(2,1)S(1)} %get-tuple-element.133), channel_id=1, source_target_pairs={{0,128},{64,192},{128,0},{192,64},{1,129},{65,193},{129,1},{193,65... | collective-permute-start | bytes 368648 | tf_op jit(solution)/shard_map/ppermute | solution.py:186
  7.4 4.3 %collective-permute-done.1 = bf16[2,40,768]{2,1,0:T(8,128)(2,1)S(1)} collective-permute-done((bf16[2,40,768]{2,1,0:T(8,128)(2,1)S(1)}, bf16[2,40,768]{2,1,0:T(8,128)(2,1)S(1)}, u32[]{:S(2)}, u32[]{:S(2)}) %collective-permute-start.1) | collective-permute-done | bytes 122912 | tf_op jit(solution)/shard_map/ppermute | solution.py:186
  13.7 6.7 %collective-permute-start.7 = (bf16[4,2,40,768]{3,2,1,0:T(8,128)(2,1)S(1)}, bf16[4,2,40,768]{3,2,1,0:T(8,128)(2,1)S(1)}, u32[]{:S(2)}, u32[]{:S(2)}) collective-permute-start(bf16[4,2,40,768]{3,2,1,0:T(8,128)(2,1)S(1)} %pad_maximum_fusion.refs_1_), channel_id=1, source_target_pairs={{0,1},{1,0},{2,3},{3,2},{4,5},{5,4},{6,7},{7,6},{8,9},{9,8},{10,11... | collective-permute-start | bytes 1474568 | tf_op jit(solution)/shard_map/ppermute | solution.py:190
  23.7 2.2 %shard_map.75 = (bf16[2,320,768]{2,1,0:T(8,128)(2,1)S(1)}, f32[2,80,1536]{2,1,0:T(8,128)S(1)}, bf16[2,80,1536]{2,1,0:T(8,128)(2,1)S(1)}, bf16[2,80,1536]{2,1,0:T...) custom-call(s32[2]{0:T(128)S(1)} %pad_add_fusion.refs_0_, ...), custom_call_target="tpu_custom_call" | custom-call | tf_op jit(solution)/shard_map/pallas_call | solution.py:50
  27.3 2.5 %collective-permute-start.5 = (bf16[2,80,1536]{2,1,0:T(8,128)(2,1)S(1)}, bf16[2,80,1536]{2,1,0:T(8,128)(2,1)S(1)}, u32[]{:S(2)}, u32[]{:S(2)}) collective-permute-start(bf16[2,80,1536]{2,1,0:T(8,128)(2,1)S(1)} %get-tuple-element.70), channel_id=1, source_target_pairs={{0,4},{2,6},{4,0},{6,2},{1,5},{3,7},{5,1},{7,3},{8,12},{10,14},{12... | collective-permute-start | bytes 1474568 | tf_op jit(solution)/shard_map/ppermute | solution.py:186
  30.9 3.2 %collective-permute-done.7.refs_0_ = bf16[4,2,40,768]{3,2,1,0:T(8,128)(2,1)S(1)} collective-permute-done((bf16[4,2,40,768]{3,2,1,0:T(8,128)(2,1)S(1)}, bf16[4,2,40,768]{3,2,1,0:T(8,128)(2,1)S(1)}, u32[]{:S(2)}, u32[]{:S(2)}) %collective-permute-start.7) | collective-permute-done | bytes 491552 | tf_op jit(solution)/shard_map/ppermute | solution.py:190
  34.1 5.7 %collective-permute-done.4.refs_1_.refs_2_ = bf16[2,80,1536]{2,1,0:T(8,128)(2,1)S(1)} collective-permute-done((bf16[2,80,1536]{2,1,0:T(8,128)(2,1)S(1)}, bf16[2,80,1536]{2,1,0:T(8,128)(2,1)S(1)}, u32[]{:S(2)}, u32[]{:S(2)}) %collective-permute-start.4) | collective-permute-done | bytes 491552 | tf_op jit(solution)/shard_map/ppermute | solution.py:186
  39.8 11.5 %collective-permute-done.5.refs_2_.refs_3_ = bf16[2,80,1536]{2,1,0:T(8,128)(2,1)S(1)} collective-permute-done((bf16[2,80,1536]{2,1,0:T(8,128)(2,1)S(1)}, bf16[2,80,1536]{2,1,0:T(8,128)(2,1)S(1)}, u32[]{:S(2)}, u32[]{:S(2)}) %collective-permute-start.5) | collective-permute-done | bytes 491552 | tf_op jit(solution)/shard_map/ppermute | solution.py:186
  54.1 2.2 %shard_map.77 = (bf16[2,320,768]{2,1,0:T(8,128)(2,1)S(1)}, f32[2,80,1536]{2,1,0:T(8,128)S(1)}, bf16[2,80,1536]{2,1,0:T(8,128)(2,1)S(1)}, bf16[2,80,1536]{2,1,0:T...) custom-call(s32[2]{0:T(128)S(1)} %pad_add_fusion.refs_0_, ...), custom_call_target="tpu_custom_call" | custom-call | tf_op jit(solution)/shard_map/pallas_call | solution.py:50
  63.6 3.7 %collective-permute-done.9.refs_1_ = bf16[2,80,384]{2,1,0:T(8,128)(2,1)S(1)} collective-permute-done((bf16[2,80,384]{2,1,0:T(8,128)(2,1)S(1)}, bf16[2,80,384]{2,1,0:T(8,128)(2,1)S(1)}, u32[]{:S(2)}, u32[]{:S(2)}) %collective-permute-start.9) | collective-permute-done | bytes 122912 | tf_op jit(solution)/shard_map/ppermute | solution.py:186
  67.4 6.3 %collective-permute-done.10.refs_2_ = bf16[2,80,384]{2,1,0:T(8,128)(2,1)S(1)} collective-permute-done((bf16[2,80,384]{2,1,0:T(8,128)(2,1)S(1)}, bf16[2,80,384]{2,1,0:T(8,128)(2,1)S(1)}, u32[]{:S(2)}, u32[]{:S(2)}) %collective-permute-start.10) | collective-permute-done | bytes 122912 | tf_op jit(solution)/shard_map/ppermute | solution.py:186
  75.8 2.2 %collective-permute-start.14 = (bf16[2,80,384]{2,1,0:T(8,128)(2,1)S(1)}, bf16[2,80,384]{2,1,0:T(8,128)(2,1)S(1)}, u32[]{:S(2)}, u32[]{:S(2)}) collective-permute-start(bf16[2,80,384]{2,1,0:T(8,128)(2,1)S(1)} %get-tuple-element.81.refs_1_), channel_id=1, source_target_pairs={{0,24},{8,0},{16,8},{24,16},{1,25},{9,1},{17,9},{25,17},{2,26},{10... | collective-permute-start | bytes 368648 | tf_op jit(solution)/shard_map/ppermute | solution.py:186
  78.0 3.1 %collective-permute-done.16.refs_3_ = bf16[2,80,1536]{2,1,0:T(8,128)(2,1)S(1)} collective-permute-done((bf16[2,80,1536]{2,1,0:T(8,128)(2,1)S(1)}, bf16[2,80,1536]{2,1,0:T(8,128)(2,1)S(1)}, u32[]{:S(2)}, u32[]{:S(2)}) %collective-permute-start.16) | collective-permute-done | bytes 491552 | tf_op jit(solution)/shard_map/ppermute | solution.py:186
  82.7 3.0 %collective-permute-done.13.refs_3_ = bf16[2,80,384]{2,1,0:T(8,128)(2,1)S(1)} collective-permute-done((bf16[2,80,384]{2,1,0:T(8,128)(2,1)S(1)}, bf16[2,80,384]{2,1,0:T(8,128)(2,1)S(1)}, u32[]{:S(2)}, u32[]{:S(2)}) %collective-permute-start.13) | collective-permute-done | bytes 122912 | tf_op jit(solution)/shard_map/ppermute | solution.py:186
  89.1 4.5 %collective-permute-start.22 = (bf16[2,80,384]{2,1,0:T(8,128)(2,1)S(1)}, bf16[2,80,384]{2,1,0:T(8,128)(2,1)S(1)}, u32[]{:S(2)}, u32[]{:S(2)}) collective-permute-start(bf16[2,80,384]{2,1,0:T(8,128)(2,1)S(1)} %get-tuple-element.91), channel_id=1, source_target_pairs={{0,16},{8,24},{16,0},{24,8},{1,17},{9,25},{17,1},{25,9},{2,18},{10... | collective-permute-start | bytes 368648 | tf_op jit(solution)/shard_map/ppermute | solution.py:186
  93.6 3.1 %collective-permute-start.23 = (bf16[2,80,384]{2,1,0:T(8,128)(2,1)S(1)}, bf16[2,80,384]{2,1,0:T(8,128)(2,1)S(1)}, u32[]{:S(2)}, u32[]{:S(2)}) collective-permute-start(bf16[2,80,384]{2,1,0:T(8,128)(2,1)S(1)} %get-tuple-element.92), channel_id=1, source_target_pairs={{0,24},{8,0},{16,8},{24,16},{1,25},{9,1},{17,9},{25,17},{2,26},{10... | collective-permute-start | bytes 368648 | tf_op jit(solution)/shard_map/ppermute | solution.py:186
  96.7 2.1 %collective-permute-done.23.refs_3_ = bf16[2,80,384]{2,1,0:T(8,128)(2,1)S(1)} collective-permute-done((bf16[2,80,384]{2,1,0:T(8,128)(2,1)S(1)}, bf16[2,80,384]{2,1,0:T(8,128)(2,1)S(1)}, u32[]{:S(2)}, u32[]{:S(2)}) %collective-permute-start.23) | collective-permute-done | bytes 122912 | tf_op jit(solution)/shard_map/ppermute | solution.py:186
  99.0 2.2 %collective-permute-start.24 = (bf16[2,80,384]{2,1,0:T(8,128)(2,1)S(1)}, bf16[2,80,384]{2,1,0:T(8,128)(2,1)S(1)}, u32[]{:S(2)}, u32[]{:S(2)}) collective-permute-start(bf16[2,80,384]{2,1,0:T(8,128)(2,1)S(1)} %get-tuple-element.94.refs_1_), channel_id=1, source_target_pairs={{0,8},{8,16},{16,24},{24,0},{1,9},{9,17},{17,25},{25,1},{2,10},{10... | collective-permute-start | bytes 368648 | tf_op jit(solution)/shard_map/ppermute | solution.py:186
  101.2 3.1 %collective-permute-start.25 = (bf16[2,80,384]{2,1,0:T(8,128)(2,1)S(1)}, bf16[2,80,384]{2,1,0:T(8,128)(2,1)S(1)}, u32[]{:S(2)}, u32[]{:S(2)}) collective-permute-start(bf16[2,80,384]{2,1,0:T(8,128)(2,1)S(1)} %get-tuple-element.94.refs_1_), channel_id=1, source_target_pairs={{0,16},{8,24},{16,0},{24,8},{1,17},{9,25},{17,1},{25,9},{2,18},{10... | collective-permute-start | bytes 368648 | tf_op jit(solution)/shard_map/ppermute | solution.py:186
  104.3 2.3 %collective-permute-done.24.refs_2_ = bf16[2,80,384]{2,1,0:T(8,128)(2,1)S(1)} collective-permute-done((bf16[2,80,384]{2,1,0:T(8,128)(2,1)S(1)}, bf16[2,80,384]{2,1,0:T(8,128)(2,1)S(1)}, u32[]{:S(2)}, u32[]{:S(2)}) %collective-permute-start.24) | collective-permute-done | bytes 122912 | tf_op jit(solution)/shard_map/ppermute | solution.py:186
  106.5 2.3 %collective-permute-start.26 = (bf16[2,80,384]{2,1,0:T(8,128)(2,1)S(1)}, bf16[2,80,384]{2,1,0:T(8,128)(2,1)S(1)}, u32[]{:S(2)}, u32[]{:S(2)}) collective-permute-start(bf16[2,80,384]{2,1,0:T(8,128)(2,1)S(1)} %get-tuple-element.94.refs_1_), channel_id=1, source_target_pairs={{0,24},{8,0},{16,8},{24,16},{1,25},{9,1},{17,9},{25,17},{2,26},{10... | collective-permute-start | bytes 368648 | tf_op jit(solution)/shard_map/ppermute | solution.py:186
  108.9 3.5 %collective-permute-done.25.refs_3_ = bf16[2,80,384]{2,1,0:T(8,128)(2,1)S(1)} collective-permute-done((bf16[2,80,384]{2,1,0:T(8,128)(2,1)S(1)}, bf16[2,80,384]{2,1,0:T(8,128)(2,1)S(1)}, u32[]{:S(2)}, u32[]{:S(2)}) %collective-permute-start.25) | collective-permute-done | bytes 122912 | tf_op jit(solution)/shard_map/ppermute | solution.py:186
  113.0 2.3 %shard_map.84 = (bf16[2,320,1536]{2,1,0:T(8,128)(2,1)S(1)}, f32[4,2,40,768]{3,2,1,0:T(8,128)S(1)}, bf16[4,2,40,768]{3,2,1,0:T(8,128)(2,1)S(1)}, f32[8,128]{1,0:T(8,128)S(1)}) custom-call(s32[2]{0:T(128)S(1)} %pad_add_fusion.refs_0_, bf16[2,80,1536]{2,1,0:T(8,128)(2,1)S(1)} %get-tuple-element.88.refs_1_, ...), custom_call_target="tpu_custom_call" | custom-call | tf_op jit(solution)/shard_map/pallas_call | solution.py:50
  115.2 3.8 %collective-permute-start.27 = (bf16[4,2,40,768]{3,2,1,0:T(8,128)(2,1)S(1)}, bf16[4,2,40,768]{3,2,1,0:T(8,128)(2,1)S(1)}, u32[]{:S(2)}, u32[]{:S(2)}) collective-permute-start(bf16[4,2,40,768]{3,2,1,0:T(8,128)(2,1)S(1)} %get-tuple-element.98), channel_id=1, source_target_pairs={{0,32},{32,0},{1,33},{33,1},{2,34},{34,2},{3,35},{35,3},{4,36},{36... | collective-permute-start | bytes 1474568 | tf_op jit(solution)/shard_map/ppermute | solution.py:190
  129.5 2.3 %collective-permute-done.28.refs_3_ = bf16[2,40,768]{2,1,0:T(8,128)(2,1)S(1)} collective-permute-done((bf16[2,40,768]{2,1,0:T(8,128)(2,1)S(1)}, bf16[2,40,768]{2,1,0:T(8,128)(2,1)S(1)}, u32[]{:S(2)}, u32[]{:S(2)}) %collective-permute-start.28) | collective-permute-done | bytes 122912 | tf_op jit(solution)/shard_map/ppermute | solution.py:186
  132.3 2.2 %collective-permute-done.29.refs_4_ = bf16[2,40,768]{2,1,0:T(8,128)(2,1)S(1)} collective-permute-done((bf16[2,40,768]{2,1,0:T(8,128)(2,1)S(1)}, bf16[2,40,768]{2,1,0:T(8,128)(2,1)S(1)}, u32[]{:S(2)}, u32[]{:S(2)}) %collective-permute-start.29) | collective-permute-done | bytes 122912 | tf_op jit(solution)/shard_map/ppermute | solution.py:186
  135.9 7.6 %collective-permute-done.32.refs_3_ = bf16[2,80,1536]{2,1,0:T(8,128)(2,1)S(1)} collective-permute-done((bf16[2,80,1536]{2,1,0:T(8,128)(2,1)S(1)}, bf16[2,80,1536]{2,1,0:T(8,128)(2,1)S(1)}, u32[]{:S(2)}, u32[]{:S(2)}) %collective-permute-start.32) | collective-permute-done | bytes 491552 | tf_op jit(solution)/shard_map/ppermute | solution.py:186
  143.9 2.3 %shard_map.89 = (bf16[2,320,1536]{2,1,0:T(8,128)(2,1)S(1)}, f32[4,2,40,768]{3,2,1,0:T(8,128)S(1)}, bf16[4,2,40,768]{3,2,1,0:T(8,128)(2,1)S(1)}, f32[8,128]{1,0:T(8,128)S(1)}) custom-call(s32[2]{0:T(128)S(1)} %pad_add_fusion.refs_0_, bf16[2,80,1536]{2,1,0:T(8,128)(2,1)S(1)} %get-tuple-element.110.refs_1_, ...), custom_call_target="tpu_custom_call" | custom-call | tf_op jit(solution)/shard_map/pallas_call | solution.py:50
  153.4 2.8 %shard_map.91 = (bf16[768,1536]{1,0:T(8,128)(2,1)}, f32[8,128]{1,0:T(8,128)S(1)}) custom-call(bf16[2,320,768]{2,1,0:T(8,128)(2,1)S(1)} %get-tuple-element.119.refs_0_, bf16[2,320,1536]{2,1,0:T(8,128)(2,1)S(1)} %get-tuple-element.120.refs_1_, f32[768,1536]{1,0:T(8,128)S(1)} %get-tuple-element.121.refs_2_, f32[8,128]{1,0:T(8,128)S(1)} %get-tuple-element.122.refs_3_), custom_call_target="tpu_custom_call" | custom-call | flops 754974720 | bytes 8388608 | tf_op jit(solution)/shard_map/pallas_call | solution.py:50
  159.4 2.9 %shard_map.93 = (bf16[1536,768]{1,0:T(8,128)(2,1)}, f32[8,128]{1,0:T(8,128)S(1)}) custom-call(bf16[2,320,768]{2,1,0:T(8,128)(2,1)S(1)} %get-tuple-element.119.refs_0_, bf16[2,320,1536]{2,1,0:T(8,128)(2,1)S(1)} %get-tuple-element.120.refs_1_, f32[1536,768]{1,0:T(8,128)S(1)} %get-tuple-element.125.refs_2_, f32[8,128]{1,0:T(8,128)S(1)} %get-tuple-element.126.refs_3_), custom_call_target="tpu_custom_call" | custom-call | flops 754974720 | bytes 8388608 | tf_op jit(solution)/shard_map/pallas_call | solution.py:50
  162.3 5.9 %collective-permute-done.38.refs_1_ = bf16[2,40,768]{2,1,0:T(8,128)(2,1)S(1)} collective-permute-done((bf16[2,40,768]{2,1,0:T(8,128)(2,1)S(1)}, bf16[2,40,768]{2,1,0:T(8,128)(2,1)S(1)}, u32[]{:S(2)}, u32[]{:S(2)}) %collective-permute-start.38) | collective-permute-done | bytes 122912 | tf_op jit(solution)/shard_map/ppermute | solution.py:190
  (81 shorter events, 51.6 us)
Async XLA Ops:
  1.5 5.9 %collective-permute-start.2 = (bf16[2,40,768]{2,1,0:T(8,128)(2,1)S(1)}, bf16[2,40,768]{2,1,0:T(8,128)(2,1)S(1)}, u32[]{:S(2)}, u32[]{:S(2)}) collective-permute-start(bf16[2,40,768]{2,1,0:T(8,128)(2,1)S(1)} %get-tuple-element.133), channel_id=1, source_target_pairs={{0,64},{64,128},{128,192},{192,0},{1,65},{65,129},{129,193},{193,1... | collective-permute-start | bytes 368648 | tf_op jit(solution)/shard_map/ppermute | solution.py:186
  3.7 8.0 %collective-permute-start.1 = (bf16[2,40,768]{2,1,0:T(8,128)(2,1)S(1)}, bf16[2,40,768]{2,1,0:T(8,128)(2,1)S(1)}, u32[]{:S(2)}, u32[]{:S(2)}) collective-permute-start(bf16[2,40,768]{2,1,0:T(8,128)(2,1)S(1)} %get-tuple-element.133), channel_id=1, source_target_pairs={{0,128},{64,192},{128,0},{192,64},{1,129},{65,193},{129,1},{193,65... | collective-permute-start | bytes 368648 | tf_op jit(solution)/shard_map/ppermute | solution.py:186
  11.8 8.6 %collective-permute-start.3 = (bf16[4,2,40,768]{3,2,1,0:T(8,128)(2,1)S(1)}, bf16[4,2,40,768]{3,2,1,0:T(8,128)(2,1)S(1)}, u32[]{:S(2)}, u32[]{:S(2)}) collective-permute-start(bf16[4,2,40,768]{3,2,1,0:T(8,128)(2,1)S(1)} %pad_maximum_fusion.refs_1_), channel_id=1, source_target_pairs={{0,32},{32,0},{1,33},{33,1},{2,34},{34,2},{3,35},{35,3},{4,36},{36... | collective-permute-start | bytes 1474568 | tf_op jit(solution)/shard_map/ppermute | solution.py:190
  13.7 20.4 %collective-permute-start.7 = (bf16[4,2,40,768]{3,2,1,0:T(8,128)(2,1)S(1)}, bf16[4,2,40,768]{3,2,1,0:T(8,128)(2,1)S(1)}, u32[]{:S(2)}, u32[]{:S(2)}) collective-permute-start(bf16[4,2,40,768]{3,2,1,0:T(8,128)(2,1)S(1)} %pad_maximum_fusion.refs_1_), channel_id=1, source_target_pairs={{0,1},{1,0},{2,3},{3,2},{4,5},{5,4},{6,7},{7,6},{8,9},{9,8},{10,11... | collective-permute-start | bytes 1474568 | tf_op jit(solution)/shard_map/ppermute | solution.py:190
  26.0 13.8 %collective-permute-start.4 = (bf16[2,80,1536]{2,1,0:T(8,128)(2,1)S(1)}, bf16[2,80,1536]{2,1,0:T(8,128)(2,1)S(1)}, u32[]{:S(2)}, u32[]{:S(2)}) collective-permute-start(bf16[2,80,1536]{2,1,0:T(8,128)(2,1)S(1)} %get-tuple-element.69), channel_id=1, source_target_pairs={{0,2},{2,4},{4,6},{6,0},{1,3},{3,5},{5,7},{7,1},{8,10},{10,12},{12... | collective-permute-start | bytes 1474568 | tf_op jit(solution)/shard_map/ppermute | solution.py:186
  27.3 24.0 %collective-permute-start.5 = (bf16[2,80,1536]{2,1,0:T(8,128)(2,1)S(1)}, bf16[2,80,1536]{2,1,0:T(8,128)(2,1)S(1)}, u32[]{:S(2)}, u32[]{:S(2)}) collective-permute-start(bf16[2,80,1536]{2,1,0:T(8,128)(2,1)S(1)} %get-tuple-element.70), channel_id=1, source_target_pairs={{0,4},{2,6},{4,0},{6,2},{1,5},{3,7},{5,1},{7,3},{8,12},{10,14},{12... | collective-permute-start | bytes 1474568 | tf_op jit(solution)/shard_map/ppermute | solution.py:186
  29.7 21.6 %collective-permute-start.6 = (bf16[2,80,1536]{2,1,0:T(8,128)(2,1)S(1)}, bf16[2,80,1536]{2,1,0:T(8,128)(2,1)S(1)}, u32[]{:S(2)}, u32[]{:S(2)}) collective-permute-start(bf16[2,80,1536]{2,1,0:T(8,128)(2,1)S(1)} %get-tuple-element.71), channel_id=1, source_target_pairs={{0,6},{2,0},{4,2},{6,4},{1,7},{3,1},{5,3},{7,5},{8,14},{10,8},{12,... | collective-permute-start | bytes 1474568 | tf_op jit(solution)/shard_map/ppermute | solution.py:186
  56.3 19.5 %collective-permute-start.15 = (bf16[2,80,1536]{2,1,0:T(8,128)(2,1)S(1)}, bf16[2,80,1536]{2,1,0:T(8,128)(2,1)S(1)}, u32[]{:S(2)}, u32[]{:S(2)}) collective-permute-start(bf16[2,80,1536]{2,1,0:T(8,128)(2,1)S(1)} %get-tuple-element.83), channel_id=1, source_target_pairs={{0,2},{2,4},{4,6},{6,0},{1,3},{3,5},{5,7},{7,1},{8,10},{10,12},{12... | collective-permute-start | bytes 1474568 | tf_op jit(solution)/shard_map/ppermute | solution.py:186
  57.4 23.6 %collective-permute-start.16 = (bf16[2,80,1536]{2,1,0:T(8,128)(2,1)S(1)}, bf16[2,80,1536]{2,1,0:T(8,128)(2,1)S(1)}, u32[]{:S(2)}, u32[]{:S(2)}) collective-permute-start(bf16[2,80,1536]{2,1,0:T(8,128)(2,1)S(1)} %get-tuple-element.84), channel_id=1, source_target_pairs={{0,4},{2,6},{4,0},{6,2},{1,5},{3,7},{5,1},{7,3},{8,12},{10,14},{12... | collective-permute-start | bytes 1474568 | tf_op jit(solution)/shard_map/ppermute | solution.py:186
  59.5 21.5 %collective-permute-start.17 = (bf16[2,80,1536]{2,1,0:T(8,128)(2,1)S(1)}, bf16[2,80,1536]{2,1,0:T(8,128)(2,1)S(1)}, u32[]{:S(2)}, u32[]{:S(2)}) collective-permute-start(bf16[2,80,1536]{2,1,0:T(8,128)(2,1)S(1)} %get-tuple-element.85), channel_id=1, source_target_pairs={{0,6},{2,0},{4,2},{6,4},{1,7},{3,1},{5,3},{7,5},{8,14},{10,8},{12,... | collective-permute-start | bytes 1474568 | tf_op jit(solution)/shard_map/ppermute | solution.py:186
  61.6 5.7 %collective-permute-start.9 = (bf16[2,80,384]{2,1,0:T(8,128)(2,1)S(1)}, bf16[2,80,384]{2,1,0:T(8,128)(2,1)S(1)}, u32[]{:S(2)}, u32[]{:S(2)}) collective-permute-start(bf16[2,80,384]{2,1,0:T(8,128)(2,1)S(1)} %get-tuple-element.77), channel_id=1, source_target_pairs={{0,8},{8,16},{16,24},{24,0},{1,9},{9,17},{17,25},{25,1},{2,10},{10... | collective-permute-start | bytes 368648 | tf_op jit(solution)/shard_map/ppermute | solution.py:186
  62.5 11.2 %collective-permute-start.10 = (bf16[2,80,384]{2,1,0:T(8,128)(2,1)S(1)}, bf16[2,80,384]{2,1,0:T(8,128)(2,1)S(1)}, u32[]{:S(2)}, u32[]{:S(2)}) collective-permute-start(bf16[2,80,384]{2,1,0:T(8,128)(2,1)S(1)} %get-tuple-element.78), channel_id=1, source_target_pairs={{0,16},{8,24},{16,0},{24,8},{1,17},{9,25},{17,1},{25,9},{2,18},{10... | collective-permute-start | bytes 368648 | tf_op jit(solution)/shard_map/ppermute | solution.py:186
  67.3 6.4 %collective-permute-start.11 = (bf16[2,80,384]{2,1,0:T(8,128)(2,1)S(1)}, bf16[2,80,384]{2,1,0:T(8,128)(2,1)S(1)}, u32[]{:S(2)}, u32[]{:S(2)}) collective-permute-start(bf16[2,80,384]{2,1,0:T(8,128)(2,1)S(1)} %get-tuple-element.79), channel_id=1, source_target_pairs={{0,24},{8,0},{16,8},{24,16},{1,25},{9,1},{17,9},{25,17},{2,26},{10... | collective-permute-start | bytes 368648 | tf_op jit(solution)/shard_map/ppermute | solution.py:186
  73.9 8.8 %collective-permute-start.12 = (bf16[2,80,384]{2,1,0:T(8,128)(2,1)S(1)}, bf16[2,80,384]{2,1,0:T(8,128)(2,1)S(1)}, u32[]{:S(2)}, u32[]{:S(2)}) collective-permute-start(bf16[2,80,384]{2,1,0:T(8,128)(2,1)S(1)} %get-tuple-element.81.refs_1_), channel_id=1, source_target_pairs={{0,8},{8,16},{16,24},{24,0},{1,9},{9,17},{17,25},{25,1},{2,10},{10... | collective-permute-start | bytes 368648 | tf_op jit(solution)/shard_map/ppermute | solution.py:186
  75.8 9.9 %collective-permute-start.13 = (bf16[2,80,384]{2,1,0:T(8,128)(2,1)S(1)}, bf16[2,80,384]{2,1,0:T(8,128)(2,1)S(1)}, u32[]{:S(2)}, u32[]{:S(2)}) collective-permute-start(bf16[2,80,384]{2,1,0:T(8,128)(2,1)S(1)} %get-tuple-element.81.refs_1_), channel_id=1, source_target_pairs={{0,16},{8,24},{16,0},{24,8},{1,17},{9,25},{17,1},{25,9},{2,18},{10... | collective-permute-start | bytes 368648 | tf_op jit(solution)/shard_map/ppermute | solution.py:186
  75.8 9.9 %collective-permute-start.14 = (bf16[2,80,384]{2,1,0:T(8,128)(2,1)S(1)}, bf16[2,80,384]{2,1,0:T(8,128)(2,1)S(1)}, u32[]{:S(2)}, u32[]{:S(2)}) collective-permute-start(bf16[2,80,384]{2,1,0:T(8,128)(2,1)S(1)} %get-tuple-element.81.refs_1_), channel_id=1, source_target_pairs={{0,24},{8,0},{16,8},{24,16},{1,25},{9,1},{17,9},{25,17},{2,26},{10... | collective-permute-start | bytes 368648 | tf_op jit(solution)/shard_map/ppermute | solution.py:186
  81.9 11.8 %collective-permute-start.21 = (bf16[2,80,384]{2,1,0:T(8,128)(2,1)S(1)}, bf16[2,80,384]{2,1,0:T(8,128)(2,1)S(1)}, u32[]{:S(2)}, u32[]{:S(2)}) collective-permute-start(bf16[2,80,384]{2,1,0:T(8,128)(2,1)S(1)} %get-tuple-element.90), channel_id=1, source_target_pairs={{0,8},{8,16},{16,24},{24,0},{1,9},{9,17},{17,25},{25,1},{2,10},{10... | collective-permute-start | bytes 368648 | tf_op jit(solution)/shard_map/ppermute | solution.py:186
  86.3 26.0 %collective-permute-start.18 = (bf16[2,80,1536]{2,1,0:T(8,128)(2,1)S(1)}, bf16[2,80,1536]{2,1,0:T(8,128)(2,1)S(1)}, u32[]{:S(2)}, u32[]{:S(2)}) collective-permute-start(bf16[2,80,1536]{2,1,0:T(8,128)(2,1)S(1)} %get-tuple-element.88.refs_1_), channel_id=1, source_target_pairs={{0,2},{2,4},{4,6},{6,0},{1,3},{3,5},{5,7},{7,1},{8,10},{10,12},{12... | collective-permute-start | bytes 1474568 | tf_op jit(solution)/shard_map/ppermute | solution.py:186
  86.5 25.8 %collective-permute-start.19 = (bf16[2,80,1536]{2,1,0:T(8,128)(2,1)S(1)}, bf16[2,80,1536]{2,1,0:T(8,128)(2,1)S(1)}, u32[]{:S(2)}, u32[]{:S(2)}) collective-permute-start(bf16[2,80,1536]{2,1,0:T(8,128)(2,1)S(1)} %get-tuple-element.88.refs_1_), channel_id=1, source_target_pairs={{0,4},{2,6},{4,0},{6,2},{1,5},{3,7},{5,1},{7,3},{8,12},{10,14},{12... | collective-permute-start | bytes 1474568 | tf_op jit(solution)/shard_map/ppermute | solution.py:186
  87.8 24.6 %collective-permute-start.20 = (bf16[2,80,1536]{2,1,0:T(8,128)(2,1)S(1)}, bf16[2,80,1536]{2,1,0:T(8,128)(2,1)S(1)}, u32[]{:S(2)}, u32[]{:S(2)}) collective-permute-start(bf16[2,80,1536]{2,1,0:T(8,128)(2,1)S(1)} %get-tuple-element.88.refs_1_), channel_id=1, source_target_pairs={{0,6},{2,0},{4,2},{6,4},{1,7},{3,1},{5,3},{7,5},{8,14},{10,8},{12,... | collective-permute-start | bytes 1474568 | tf_op jit(solution)/shard_map/ppermute | solution.py:186
  89.1 7.6 %collective-permute-start.22 = (bf16[2,80,384]{2,1,0:T(8,128)(2,1)S(1)}, bf16[2,80,384]{2,1,0:T(8,128)(2,1)S(1)}, u32[]{:S(2)}, u32[]{:S(2)}) collective-permute-start(bf16[2,80,384]{2,1,0:T(8,128)(2,1)S(1)} %get-tuple-element.91), channel_id=1, source_target_pairs={{0,16},{8,24},{16,0},{24,8},{1,17},{9,25},{17,1},{25,9},{2,18},{10... | collective-permute-start | bytes 368648 | tf_op jit(solution)/shard_map/ppermute | solution.py:186
  99.0 7.5 %collective-permute-start.24 = (bf16[2,80,384]{2,1,0:T(8,128)(2,1)S(1)}, bf16[2,80,384]{2,1,0:T(8,128)(2,1)S(1)}, u32[]{:S(2)}, u32[]{:S(2)}) collective-permute-start(bf16[2,80,384]{2,1,0:T(8,128)(2,1)S(1)} %get-tuple-element.94.refs_1_), channel_id=1, source_target_pairs={{0,8},{8,16},{16,24},{24,0},{1,9},{9,17},{17,25},{25,1},{2,10},{10... | collective-permute-start | bytes 368648 | tf_op jit(solution)/shard_map/ppermute | solution.py:186
  101.2 11.2 %collective-permute-start.25 = (bf16[2,80,384]{2,1,0:T(8,128)(2,1)S(1)}, bf16[2,80,384]{2,1,0:T(8,128)(2,1)S(1)}, u32[]{:S(2)}, u32[]{:S(2)}) collective-permute-start(bf16[2,80,384]{2,1,0:T(8,128)(2,1)S(1)} %get-tuple-element.94.refs_1_), channel_id=1, source_target_pairs={{0,16},{8,24},{16,0},{24,8},{1,17},{9,25},{17,1},{25,9},{2,18},{10... | collective-permute-start | bytes 368648 | tf_op jit(solution)/shard_map/ppermute | solution.py:186
  106.5 5.8 %collective-permute-start.26 = (bf16[2,80,384]{2,1,0:T(8,128)(2,1)S(1)}, bf16[2,80,384]{2,1,0:T(8,128)(2,1)S(1)}, u32[]{:S(2)}, u32[]{:S(2)}) collective-permute-start(bf16[2,80,384]{2,1,0:T(8,128)(2,1)S(1)} %get-tuple-element.94.refs_1_), channel_id=1, source_target_pairs={{0,24},{8,0},{16,8},{24,16},{1,25},{9,1},{17,9},{25,17},{2,26},{10... | collective-permute-start | bytes 368648 | tf_op jit(solution)/shard_map/ppermute | solution.py:186
  115.2 11.1 %collective-permute-start.27 = (bf16[4,2,40,768]{3,2,1,0:T(8,128)(2,1)S(1)}, bf16[4,2,40,768]{3,2,1,0:T(8,128)(2,1)S(1)}, u32[]{:S(2)}, u32[]{:S(2)}) collective-permute-start(bf16[4,2,40,768]{3,2,1,0:T(8,128)(2,1)S(1)} %get-tuple-element.98), channel_id=1, source_target_pairs={{0,32},{32,0},{1,33},{33,1},{2,34},{34,2},{3,35},{35,3},{4,36},{36... | collective-permute-start | bytes 1474568 | tf_op jit(solution)/shard_map/ppermute | solution.py:190
  119.0 16.8 %collective-permute-start.31 = (bf16[2,80,1536]{2,1,0:T(8,128)(2,1)S(1)}, bf16[2,80,1536]{2,1,0:T(8,128)(2,1)S(1)}, u32[]{:S(2)}, u32[]{:S(2)}) collective-permute-start(bf16[2,80,1536]{2,1,0:T(8,128)(2,1)S(1)} %get-tuple-element.110.refs_1_), channel_id=1, source_target_pairs={{0,2},{2,4},{4,6},{6,0},{1,3},{3,5},{5,7},{7,1},{8,10},{10,12},{12... | collective-permute-start | bytes 1474568 | tf_op jit(solution)/shard_map/ppermute | solution.py:186
  120.0 23.5 %collective-permute-start.32 = (bf16[2,80,1536]{2,1,0:T(8,128)(2,1)S(1)}, bf16[2,80,1536]{2,1,0:T(8,128)(2,1)S(1)}, u32[]{:S(2)}, u32[]{:S(2)}) collective-permute-start(bf16[2,80,1536]{2,1,0:T(8,128)(2,1)S(1)} %get-tuple-element.110.refs_1_), channel_id=1, source_target_pairs={{0,4},{2,6},{4,0},{6,2},{1,5},{3,7},{5,1},{7,3},{8,12},{10,14},{12... | collective-permute-start | bytes 1474568 | tf_op jit(solution)/shard_map/ppermute | solution.py:186
  121.4 22.5 %collective-permute-start.33 = (bf16[2,80,1536]{2,1,0:T(8,128)(2,1)S(1)}, bf16[2,80,1536]{2,1,0:T(8,128)(2,1)S(1)}, u32[]{:S(2)}, u32[]{:S(2)}) collective-permute-start(bf16[2,80,1536]{2,1,0:T(8,128)(2,1)S(1)} %get-tuple-element.110.refs_1_), channel_id=1, source_target_pairs={{0,6},{2,0},{4,2},{6,4},{1,7},{3,1},{5,3},{7,5},{8,14},{10,8},{12,... | collective-permute-start | bytes 1474568 | tf_op jit(solution)/shard_map/ppermute | solution.py:186
  127.4 7.2 %collective-permute-start.29 = (bf16[2,40,768]{2,1,0:T(8,128)(2,1)S(1)}, bf16[2,40,768]{2,1,0:T(8,128)(2,1)S(1)}, u32[]{:S(2)}, u32[]{:S(2)}) collective-permute-start(bf16[2,40,768]{2,1,0:T(8,128)(2,1)S(1)} %get-tuple-element.106), channel_id=1, source_target_pairs={{0,128},{64,192},{128,0},{192,64},{1,129},{65,193},{129,1},{193,65... | collective-permute-start | bytes 368648 | tf_op jit(solution)/shard_map/ppermute | solution.py:186
  149.0 7.2 %collective-permute-start.35 = (bf16[2,40,768]{2,1,0:T(8,128)(2,1)S(1)}, bf16[2,40,768]{2,1,0:T(8,128)(2,1)S(1)}, u32[]{:S(2)}, u32[]{:S(2)}) collective-permute-start(bf16[2,40,768]{2,1,0:T(8,128)(2,1)S(1)} %get-tuple-element.116), channel_id=1, source_target_pairs={{0,64},{64,128},{128,192},{192,0},{1,65},{65,129},{129,193},{193,1... | collective-permute-start | bytes 368648 | tf_op jit(solution)/shard_map/ppermute | solution.py:186
  150.0 7.8 %collective-permute-start.36 = (bf16[2,40,768]{2,1,0:T(8,128)(2,1)S(1)}, bf16[2,40,768]{2,1,0:T(8,128)(2,1)S(1)}, u32[]{:S(2)}, u32[]{:S(2)}) collective-permute-start(bf16[2,40,768]{2,1,0:T(8,128)(2,1)S(1)} %get-tuple-element.117), channel_id=1, source_target_pairs={{0,128},{64,192},{128,0},{192,64},{1,129},{65,193},{129,1},{193,65... | collective-permute-start | bytes 368648 | tf_op jit(solution)/shard_map/ppermute | solution.py:186
  157.8 10.3 %collective-permute-start.38 = (bf16[2,40,768]{2,1,0:T(8,128)(2,1)S(1)}, bf16[2,40,768]{2,1,0:T(8,128)(2,1)S(1)}, u32[]{:S(2)}, u32[]{:S(2)}) collective-permute-start(bf16[2,40,768]{2,1,0:T(8,128)(2,1)S(1)} %get-tuple-element.124), channel_id=1, source_target_pairs={{0,1},{1,0},{2,3},{3,2},{4,5},{5,4},{6,7},{7,6},{8,9},{9,8},{10,11... | collective-permute-start | bytes 368648 | tf_op jit(solution)/shard_map/ppermute | solution.py:190
  (13 other events, 116.9 us)

commit v4 on v3

--- a/solution.py
+++ b/solution.py
@@ -204,12 +204,12 @@
     def send(values, axis):
         return [shift(s, axis, d) for d, s in enumerate(values, 1)]
 
-    def first(rows):
+    def first(rows, after=()):
         rows, keep, *out = order.call(
             first_products,
             [((2, N * block, width), BF16), ((2, block, hidden), F32)]
             + [((2, block, hidden), BF16)] * 3,
-            at, rows, swap(rows, "core"), w_in, w_out,
+            at, rows, swap(rows, "core"), w_in, w_out, after=after,
         )
         return rows, keep, send(out, "x")
 
@@ -259,8 +259,8 @@
     own = jnp.stack([mine] + [shift(mine, "y", -k) for k in range(1, N)])
     far = swap(own, "zh")
     rows_o, keep_o, got_o = first(own)
-    (far,) = order.call(keep_as_is, [(far.shape, BF16)], far, after=got_o)
-    rows_f, keep_f, got_f = first(far)
+    (far,) = order.call(keep_as_is, [(far.shape, BF16)], far, after=got_o[:2])
+    rows_f, keep_f, got_f = first(far, got_o)
     keep_o, got_o = add(keep_o, got_o)
     piece_o = act(keep_o, got_o)
     got_o = send([piece_o] * 3, "zl")

time: 170 us -> 169 us (level)
  starting transfers between devices: 69 us -> 61.5 us
  waiting for transfers between devices: 72.9 us -> 79.1 us
    ppermute x33, waiting for transfers between devices: 60.8 us -> 67.1 us  [shift(): return lax.ppermute(value, axis, [(i, (i + step) % N) for i in range(N)])]
    ppermute x33, starting transfers between devices: 52.7 us -> 47.1 us  [shift(): return lax.ppermute(value, axis, [(i, (i + step) % N) for i in range(N)])]
    ppermute x6, starting transfers between devices: 16.4 us -> 14.4 us  [swap(): return lax.ppermute(value, axis, [(0, 1), (1, 0)])]
  transfers between devices with their start and end apart: 39 -> 39, of which waited for: 20 -> 21; matrix products, arithmetic and copies ran while one was open for 0% -> 0% of each run, Pallas kernels for 8% -> 8%
where the time goes in v4:
time: 169 us; the launch traced here: 167 us
  waiting for transfers between devices  79.1 us (47%)
  starting transfers between devices  61.5 us (36%)
  Pallas kernels  21.7 us (13%)
  local copies, waits for them, and re-layouts  3.35 us (2%)
    ppermute x33, waiting for transfers between devices, shift(): return lax.ppermute(value, axis, [(i, (i + step) % N) for i in range(N)])  67.1 us
    ppermute x33, starting transfers between devices, shift(): return lax.ppermute(value, axis, [(i, (i + step) % N) for i in range(N)])  47.1 us
    pallas_call x20, Pallas kernels, call(): pl.pallas_call(ordered, out_shape=[jax.ShapeDtypeStruct(s, d) for s, d in...  21.7 us
    ppermute x6, starting transfers between devices, swap(): return lax.ppermute(value, axis, [(0, 1), (1, 0)])  14.4 us
    ppermute x6, waiting for transfers between devices, swap(): return lax.ppermute(value, axis, [(0, 1), (1, 0)])  12 us
  transfers between devices with their start and end apart: 39, of which 21 were waited for; matrix products, arithmetic and copies ran while one was open for 0% of the time, Pallas kernels for 8%

profile of v4, /device:TPU:1, one launch (start us, length us, event | category | flops | bytes accessed | tf_op | source)
XLA Modules:
  0.0 167.4 jit_solution(11063172476871124842)
XLA Ops:
  1.5 2.2 %collective-permute-start.2 = (bf16[2,40,768]{2,1,0:T(8,128)(2,1)S(1)}, bf16[2,40,768]{2,1,0:T(8,128)(2,1)S(1)}, u32[]{:S(2)}, u32[]{:S(2)}) collective-permute-start(bf16[2,40,768]{2,1,0:T(8,128)(2,1)S(1)} %get-tuple-element.133), channel_id=1, source_target_pairs={{0,64},{64,128},{128,192},{192,0},{1,65},{65,129},{129,193},{193,1... | collective-permute-start | bytes 368648 | tf_op jit(solution)/shard_map/ppermute | solution.py:186
  3.7 2.6 %collective-permute-start.1 = (bf16[2,40,768]{2,1,0:T(8,128)(2,1)S(1)}, bf16[2,40,768]{2,1,0:T(8,128)(2,1)S(1)}, u32[]{:S(2)}, u32[]{:S(2)}) collective-permute-start(bf16[2,40,768]{2,1,0:T(8,128)(2,1)S(1)} %get-tuple-element.133), channel_id=1, source_target_pairs={{0,128},{64,192},{128,0},{192,64},{1,129},{65,193},{129,1},{193,65... | collective-permute-start | bytes 368648 | tf_op jit(solution)/shard_map/ppermute | solution.py:186
  7.4 4.3 %collective-permute-done.1 = bf16[2,40,768]{2,1,0:T(8,128)(2,1)S(1)} collective-permute-done((bf16[2,40,768]{2,1,0:T(8,128)(2,1)S(1)}, bf16[2,40,768]{2,1,0:T(8,128)(2,1)S(1)}, u32[]{:S(2)}, u32[]{:S(2)}) %collective-permute-start.1) | collective-permute-done | bytes 122912 | tf_op jit(solution)/shard_map/ppermute | solution.py:186
  13.7 6.7 %collective-permute-start.7 = (bf16[4,2,40,768]{3,2,1,0:T(8,128)(2,1)S(1)}, bf16[4,2,40,768]{3,2,1,0:T(8,128)(2,1)S(1)}, u32[]{:S(2)}, u32[]{:S(2)}) collective-permute-start(bf16[4,2,40,768]{3,2,1,0:T(8,128)(2,1)S(1)} %pad_maximum_fusion.refs_1_), channel_id=1, source_target_pairs={{0,1},{1,0},{2,3},{3,2},{4,5},{5,4},{6,7},{7,6},{8,9},{9,8},{10,11... | collective-permute-start | bytes 1474568 | tf_op jit(solution)/shard_map/ppermute | solution.py:190
  23.7 2.2 %shard_map.75 = (bf16[2,320,768]{2,1,0:T(8,128)(2,1)S(1)}, f32[2,80,1536]{2,1,0:T(8,128)S(1)}, bf16[2,80,1536]{2,1,0:T(8,128)(2,1)S(1)}, bf16[2,80,1536]{2,1,0:T...) custom-call(s32[2]{0:T(128)S(1)} %pad_add_fusion.refs_0_, ...), custom_call_target="tpu_custom_call" | custom-call | tf_op jit(solution)/shard_map/pallas_call | solution.py:50
  27.3 2.5 %collective-permute-start.5 = (bf16[2,80,1536]{2,1,0:T(8,128)(2,1)S(1)}, bf16[2,80,1536]{2,1,0:T(8,128)(2,1)S(1)}, u32[]{:S(2)}, u32[]{:S(2)}) collective-permute-start(bf16[2,80,1536]{2,1,0:T(8,128)(2,1)S(1)} %get-tuple-element.70), channel_id=1, source_target_pairs={{0,4},{2,6},{4,0},{6,2},{1,5},{3,7},{5,1},{7,3},{8,12},{10,14},{12... | collective-permute-start | bytes 1474568 | tf_op jit(solution)/shard_map/ppermute | solution.py:186
  30.9 3.2 %collective-permute-done.7.refs_0_ = bf16[4,2,40,768]{3,2,1,0:T(8,128)(2,1)S(1)} collective-permute-done((bf16[4,2,40,768]{3,2,1,0:T(8,128)(2,1)S(1)}, bf16[4,2,40,768]{3,2,1,0:T(8,128)(2,1)S(1)}, u32[]{:S(2)}, u32[]{:S(2)}) %collective-permute-start.7) | collective-permute-done | bytes 491552 | tf_op jit(solution)/shard_map/ppermute | solution.py:190
  34.1 5.7 %collective-permute-done.4.refs_1_.refs_5_.refs_2_ = bf16[2,80,1536]{2,1,0:T(8,128)(2,1)S(1)} collective-permute-done((bf16[2,80,1536]{2,1,0:T(8,128)(2,1)S(1)}, bf16[2,80,1536]{2,1,0:T(8,128)(2,1)S(1)}, u32[]{:S(2)}, u32[]{:S(2)}) %collective-permute-start.4) | collective-permute-done | bytes 491552 | tf_op jit(solution)/shard_map/ppermute | solution.py:186
  39.8 11.5 %collective-permute-done.5.refs_2_.refs_6_.refs_3_ = bf16[2,80,1536]{2,1,0:T(8,128)(2,1)S(1)} collective-permute-done((bf16[2,80,1536]{2,1,0:T(8,128)(2,1)S(1)}, bf16[2,80,1536]{2,1,0:T(8,128)(2,1)S(1)}, u32[]{:S(2)}, u32[]{:S(2)}) %collective-permute-start.5) | collective-permute-done | bytes 491552 | tf_op jit(solution)/shard_map/ppermute | solution.py:186
  54.1 2.2 %shard_map.77 = (bf16[2,320,768]{2,1,0:T(8,128)(2,1)S(1)}, f32[2,80,1536]{2,1,0:T(8,128)S(1)}, bf16[2,80,1536]{2,1,0:T(8,128)(2,1)S(1)}, bf16[2,80,1536]{2,1,0:T...) custom-call(s32[2]{0:T(128)S(1)} %pad_add_fusion.refs_0_, ...), custom_call_target="tpu_custom_call" | custom-call | tf_op jit(solution)/shard_map/pallas_call | solution.py:50
  61.9 3.7 %collective-permute-done.9.refs_1_ = bf16[2,80,384]{2,1,0:T(8,128)(2,1)S(1)} collective-permute-done((bf16[2,80,384]{2,1,0:T(8,128)(2,1)S(1)}, bf16[2,80,384]{2,1,0:T(8,128)(2,1)S(1)}, u32[]{:S(2)}, u32[]{:S(2)}) %collective-permute-start.9) | collective-permute-done | bytes 122912 | tf_op jit(solution)/shard_map/ppermute | solution.py:186
  65.6 6.3 %collective-permute-done.10.refs_2_ = bf16[2,80,384]{2,1,0:T(8,128)(2,1)S(1)} collective-permute-done((bf16[2,80,384]{2,1,0:T(8,128)(2,1)S(1)}, bf16[2,80,384]{2,1,0:T(8,128)(2,1)S(1)}, u32[]{:S(2)}, u32[]{:S(2)}) %collective-permute-start.10) | collective-permute-done | bytes 122912 | tf_op jit(solution)/shard_map/ppermute | solution.py:186
  74.0 6.5 %collective-permute-done.15.refs_2_ = bf16[2,80,1536]{2,1,0:T(8,128)(2,1)S(1)} collective-permute-done((bf16[2,80,1536]{2,1,0:T(8,128)(2,1)S(1)}, bf16[2,80,1536]{2,1,0:T(8,128)(2,1)S(1)}, u32[]{:S(2)}, u32[]{:S(2)}) %collective-permute-start.15) | collective-permute-done | bytes 491552 | tf_op jit(solution)/shard_map/ppermute | solution.py:186
  84.5 2.3 %collective-permute-done.14.refs_4_ = bf16[2,80,384]{2,1,0:T(8,128)(2,1)S(1)} collective-permute-done((bf16[2,80,384]{2,1,0:T(8,128)(2,1)S(1)}, bf16[2,80,384]{2,1,0:T(8,128)(2,1)S(1)}, u32[]{:S(2)}, u32[]{:S(2)}) %collective-permute-start.14) | collective-permute-done | bytes 122912 | tf_op jit(solution)/shard_map/ppermute | solution.py:186
  87.7 2.4 %collective-permute-start.20 = (bf16[2,80,1536]{2,1,0:T(8,128)(2,1)S(1)}, bf16[2,80,1536]{2,1,0:T(8,128)(2,1)S(1)}, u32[]{:S(2)}, u32[]{:S(2)}) collective-permute-start(bf16[2,80,1536]{2,1,0:T(8,128)(2,1)S(1)} %get-tuple-element.88.refs_1_), channel_id=1, source_target_pairs={{0,6},{2,0},{4,2},{6,4},{1,7},{3,1},{5,3},{7,5},{8,14},{10,8},{12,... | collective-permute-start | bytes 1474568 | tf_op jit(solution)/shard_map/ppermute | solution.py:186
  90.1 3.5 %collective-permute-start.22 = (bf16[2,80,384]{2,1,0:T(8,128)(2,1)S(1)}, bf16[2,80,384]{2,1,0:T(8,128)(2,1)S(1)}, u32[]{:S(2)}, u32[]{:S(2)}) collective-permute-start(bf16[2,80,384]{2,1,0:T(8,128)(2,1)S(1)} %get-tuple-element.91), channel_id=1, source_target_pairs={{0,16},{8,24},{16,0},{24,8},{1,17},{9,25},{17,1},{25,9},{2,18},{10... | collective-permute-start | bytes 368648 | tf_op jit(solution)/shard_map/ppermute | solution.py:186
  93.6 3.1 %collective-permute-start.23 = (bf16[2,80,384]{2,1,0:T(8,128)(2,1)S(1)}, bf16[2,80,384]{2,1,0:T(8,128)(2,1)S(1)}, u32[]{:S(2)}, u32[]{:S(2)}) collective-permute-start(bf16[2,80,384]{2,1,0:T(8,128)(2,1)S(1)} %get-tuple-element.92), channel_id=1, source_target_pairs={{0,24},{8,0},{16,8},{24,16},{1,25},{9,1},{17,9},{25,17},{2,26},{10... | collective-permute-start | bytes 368648 | tf_op jit(solution)/shard_map/ppermute | solution.py:186
  96.7 2.4 %collective-permute-done.23.refs_3_ = bf16[2,80,384]{2,1,0:T(8,128)(2,1)S(1)} collective-permute-done((bf16[2,80,384]{2,1,0:T(8,128)(2,1)S(1)}, bf16[2,80,384]{2,1,0:T(8,128)(2,1)S(1)}, u32[]{:S(2)}, u32[]{:S(2)}) %collective-permute-start.23) | collective-permute-done | bytes 122912 | tf_op jit(solution)/shard_map/ppermute | solution.py:186
  99.3 3.6 %collective-permute-start.24 = (bf16[2,80,384]{2,1,0:T(8,128)(2,1)S(1)}, bf16[2,80,384]{2,1,0:T(8,128)(2,1)S(1)}, u32[]{:S(2)}, u32[]{:S(2)}) collective-permute-start(bf16[2,80,384]{2,1,0:T(8,128)(2,1)S(1)} %get-tuple-element.94.refs_1_), channel_id=1, source_target_pairs={{0,8},{8,16},{16,24},{24,0},{1,9},{9,17},{17,25},{25,1},{2,10},{10... | collective-permute-start | bytes 368648 | tf_op jit(solution)/shard_map/ppermute | solution.py:186
  104.2 2.3 %collective-permute-done.24.refs_2_ = bf16[2,80,384]{2,1,0:T(8,128)(2,1)S(1)} collective-permute-done((bf16[2,80,384]{2,1,0:T(8,128)(2,1)S(1)}, bf16[2,80,384]{2,1,0:T(8,128)(2,1)S(1)}, u32[]{:S(2)}, u32[]{:S(2)}) %collective-permute-start.24) | collective-permute-done | bytes 122912 | tf_op jit(solution)/shard_map/ppermute | solution.py:186
  106.5 2.3 %collective-permute-start.26 = (bf16[2,80,384]{2,1,0:T(8,128)(2,1)S(1)}, bf16[2,80,384]{2,1,0:T(8,128)(2,1)S(1)}, u32[]{:S(2)}, u32[]{:S(2)}) collective-permute-start(bf16[2,80,384]{2,1,0:T(8,128)(2,1)S(1)} %get-tuple-element.94.refs_1_), channel_id=1, source_target_pairs={{0,24},{8,0},{16,8},{24,16},{1,25},{9,1},{17,9},{25,17},{2,26},{10... | collective-permute-start | bytes 368648 | tf_op jit(solution)/shard_map/ppermute | solution.py:186
  108.8 4.1 %collective-permute-done.25.refs_3_ = bf16[2,80,384]{2,1,0:T(8,128)(2,1)S(1)} collective-permute-done((bf16[2,80,384]{2,1,0:T(8,128)(2,1)S(1)}, bf16[2,80,384]{2,1,0:T(8,128)(2,1)S(1)}, u32[]{:S(2)}, u32[]{:S(2)}) %collective-permute-start.25) | collective-permute-done | bytes 122912 | tf_op jit(solution)/shard_map/ppermute | solution.py:186
  113.6 2.3 %shard_map.84 = (bf16[2,320,1536]{2,1,0:T(8,128)(2,1)S(1)}, f32[4,2,40,768]{3,2,1,0:T(8,128)S(1)}, bf16[4,2,40,768]{3,2,1,0:T(8,128)(2,1)S(1)}, f32[8,128]{1,0:T(8,128)S(1)}) custom-call(s32[2]{0:T(128)S(1)} %pad_add_fusion.refs_0_, bf16[2,80,1536]{2,1,0:T(8,128)(2,1)S(1)} %get-tuple-element.88.refs_1_, ...), custom_call_target="tpu_custom_call" | custom-call | tf_op jit(solution)/shard_map/pallas_call | solution.py:50
  117.8 2.9 %collective-permute-start.32 = (bf16[2,80,1536]{2,1,0:T(8,128)(2,1)S(1)}, bf16[2,80,1536]{2,1,0:T(8,128)(2,1)S(1)}, u32[]{:S(2)}, u32[]{:S(2)}) collective-permute-start(bf16[2,80,1536]{2,1,0:T(8,128)(2,1)S(1)} %get-tuple-element.110.refs_1_), channel_id=1, source_target_pairs={{0,4},{2,6},{4,0},{6,2},{1,5},{3,7},{5,1},{7,3},{8,12},{10,14},{12... | collective-permute-start | bytes 1474568 | tf_op jit(solution)/shard_map/ppermute | solution.py:186
  124.8 2.1 %collective-permute-start.29 = (bf16[2,40,768]{2,1,0:T(8,128)(2,1)S(1)}, bf16[2,40,768]{2,1,0:T(8,128)(2,1)S(1)}, u32[]{:S(2)}, u32[]{:S(2)}) collective-permute-start(bf16[2,40,768]{2,1,0:T(8,128)(2,1)S(1)} %get-tuple-element.106), channel_id=1, source_target_pairs={{0,128},{64,192},{128,0},{192,64},{1,129},{65,193},{129,1},{193,65... | collective-permute-start | bytes 368648 | tf_op jit(solution)/shard_map/ppermute | solution.py:186
  126.8 2.3 %collective-permute-done.28.refs_3_ = bf16[2,40,768]{2,1,0:T(8,128)(2,1)S(1)} collective-permute-done((bf16[2,40,768]{2,1,0:T(8,128)(2,1)S(1)}, bf16[2,40,768]{2,1,0:T(8,128)(2,1)S(1)}, u32[]{:S(2)}, u32[]{:S(2)}) %collective-permute-start.28) | collective-permute-done | bytes 122912 | tf_op jit(solution)/shard_map/ppermute | solution.py:186
  129.9 2.3 %collective-permute-done.29.refs_4_ = bf16[2,40,768]{2,1,0:T(8,128)(2,1)S(1)} collective-permute-done((bf16[2,40,768]{2,1,0:T(8,128)(2,1)S(1)}, bf16[2,40,768]{2,1,0:T(8,128)(2,1)S(1)}, u32[]{:S(2)}, u32[]{:S(2)}) %collective-permute-start.29) | collective-permute-done | bytes 122912 | tf_op jit(solution)/shard_map/ppermute | solution.py:186
  133.3 9.2 %collective-permute-done.32.refs_3_ = bf16[2,80,1536]{2,1,0:T(8,128)(2,1)S(1)} collective-permute-done((bf16[2,80,1536]{2,1,0:T(8,128)(2,1)S(1)}, bf16[2,80,1536]{2,1,0:T(8,128)(2,1)S(1)}, u32[]{:S(2)}, u32[]{:S(2)}) %collective-permute-start.32) | collective-permute-done | bytes 491552 | tf_op jit(solution)/shard_map/ppermute | solution.py:186
  142.6 2.3 %shard_map.89 = (bf16[2,320,1536]{2,1,0:T(8,128)(2,1)S(1)}, f32[4,2,40,768]{3,2,1,0:T(8,128)S(1)}, bf16[4,2,40,768]{3,2,1,0:T(8,128)(2,1)S(1)}, f32[8,128]{1,0:T(8,128)S(1)}) custom-call(s32[2]{0:T(128)S(1)} %pad_add_fusion.refs_0_, bf16[2,80,1536]{2,1,0:T(8,128)(2,1)S(1)} %get-tuple-element.110.refs_1_, ...), custom_call_target="tpu_custom_call" | custom-call | tf_op jit(solution)/shard_map/pallas_call | solution.py:50
  152.2 2.8 %shard_map.91 = (bf16[768,1536]{1,0:T(8,128)(2,1)}, f32[8,128]{1,0:T(8,128)S(1)}) custom-call(bf16[2,320,768]{2,1,0:T(8,128)(2,1)S(1)} %get-tuple-element.119.refs_0_, bf16[2,320,1536]{2,1,0:T(8,128)(2,1)S(1)} %get-tuple-element.120.refs_1_, f32[768,1536]{1,0:T(8,128)S(1)} %get-tuple-element.121.refs_2_, f32[8,128]{1,0:T(8,128)S(1)} %get-tuple-element.122.refs_3_), custom_call_target="tpu_custom_call" | custom-call | flops 754974720 | bytes 8388608 | tf_op jit(solution)/shard_map/pallas_call | solution.py:50
  158.1 2.8 %shard_map.93 = (bf16[1536,768]{1,0:T(8,128)(2,1)}, f32[8,128]{1,0:T(8,128)S(1)}) custom-call(bf16[2,320,768]{2,1,0:T(8,128)(2,1)S(1)} %get-tuple-element.119.refs_0_, bf16[2,320,1536]{2,1,0:T(8,128)(2,1)S(1)} %get-tuple-element.120.refs_1_, f32[1536,768]{1,0:T(8,128)S(1)} %get-tuple-element.125.refs_2_, f32[8,128]{1,0:T(8,128)S(1)} %get-tuple-element.126.refs_3_), custom_call_target="tpu_custom_call" | custom-call | flops 754974720 | bytes 8388608 | tf_op jit(solution)/shard_map/pallas_call | solution.py:50
  160.9 5.8 %collective-permute-done.38.refs_1_ = bf16[2,40,768]{2,1,0:T(8,128)(2,1)S(1)} collective-permute-done((bf16[2,40,768]{2,1,0:T(8,128)(2,1)S(1)}, bf16[2,40,768]{2,1,0:T(8,128)(2,1)S(1)}, u32[]{:S(2)}, u32[]{:S(2)}) %collective-permute-start.38) | collective-permute-done | bytes 122912 | tf_op jit(solution)/shard_map/ppermute | solution.py:190
  (81 shorter events, 46.0 us)
Async XLA Ops:
  1.5 5.9 %collective-permute-start.2 = (bf16[2,40,768]{2,1,0:T(8,128)(2,1)S(1)}, bf16[2,40,768]{2,1,0:T(8,128)(2,1)S(1)}, u32[]{:S(2)}, u32[]{:S(2)}) collective-permute-start(bf16[2,40,768]{2,1,0:T(8,128)(2,1)S(1)} %get-tuple-element.133), channel_id=1, source_target_pairs={{0,64},{64,128},{128,192},{192,0},{1,65},{65,129},{129,193},{193,1... | collective-permute-start | bytes 368648 | tf_op jit(solution)/shard_map/ppermute | solution.py:186
  3.7 8.0 %collective-permute-start.1 = (bf16[2,40,768]{2,1,0:T(8,128)(2,1)S(1)}, bf16[2,40,768]{2,1,0:T(8,128)(2,1)S(1)}, u32[]{:S(2)}, u32[]{:S(2)}) collective-permute-start(bf16[2,40,768]{2,1,0:T(8,128)(2,1)S(1)} %get-tuple-element.133), channel_id=1, source_target_pairs={{0,128},{64,192},{128,0},{192,64},{1,129},{65,193},{129,1},{193,65... | collective-permute-start | bytes 368648 | tf_op jit(solution)/shard_map/ppermute | solution.py:186
  11.8 8.6 %collective-permute-start.3 = (bf16[4,2,40,768]{3,2,1,0:T(8,128)(2,1)S(1)}, bf16[4,2,40,768]{3,2,1,0:T(8,128)(2,1)S(1)}, u32[]{:S(2)}, u32[]{:S(2)}) collective-permute-start(bf16[4,2,40,768]{3,2,1,0:T(8,128)(2,1)S(1)} %pad_maximum_fusion.refs_1_), channel_id=1, source_target_pairs={{0,32},{32,0},{1,33},{33,1},{2,34},{34,2},{3,35},{35,3},{4,36},{36... | collective-permute-start | bytes 1474568 | tf_op jit(solution)/shard_map/ppermute | solution.py:190
  13.7 20.4 %collective-permute-start.7 = (bf16[4,2,40,768]{3,2,1,0:T(8,128)(2,1)S(1)}, bf16[4,2,40,768]{3,2,1,0:T(8,128)(2,1)S(1)}, u32[]{:S(2)}, u32[]{:S(2)}) collective-permute-start(bf16[4,2,40,768]{3,2,1,0:T(8,128)(2,1)S(1)} %pad_maximum_fusion.refs_1_), channel_id=1, source_target_pairs={{0,1},{1,0},{2,3},{3,2},{4,5},{5,4},{6,7},{7,6},{8,9},{9,8},{10,11... | collective-permute-start | bytes 1474568 | tf_op jit(solution)/shard_map/ppermute | solution.py:190
  26.0 13.8 %collective-permute-start.4 = (bf16[2,80,1536]{2,1,0:T(8,128)(2,1)S(1)}, bf16[2,80,1536]{2,1,0:T(8,128)(2,1)S(1)}, u32[]{:S(2)}, u32[]{:S(2)}) collective-permute-start(bf16[2,80,1536]{2,1,0:T(8,128)(2,1)S(1)} %get-tuple-element.69), channel_id=1, source_target_pairs={{0,2},{2,4},{4,6},{6,0},{1,3},{3,5},{5,7},{7,1},{8,10},{10,12},{12... | collective-permute-start | bytes 1474568 | tf_op jit(solution)/shard_map/ppermute | solution.py:186
  27.3 24.0 %collective-permute-start.5 = (bf16[2,80,1536]{2,1,0:T(8,128)(2,1)S(1)}, bf16[2,80,1536]{2,1,0:T(8,128)(2,1)S(1)}, u32[]{:S(2)}, u32[]{:S(2)}) collective-permute-start(bf16[2,80,1536]{2,1,0:T(8,128)(2,1)S(1)} %get-tuple-element.70), channel_id=1, source_target_pairs={{0,4},{2,6},{4,0},{6,2},{1,5},{3,7},{5,1},{7,3},{8,12},{10,14},{12... | collective-permute-start | bytes 1474568 | tf_op jit(solution)/shard_map/ppermute | solution.py:186
  29.7 22.8 %collective-permute-start.6 = (bf16[2,80,1536]{2,1,0:T(8,128)(2,1)S(1)}, bf16[2,80,1536]{2,1,0:T(8,128)(2,1)S(1)}, u32[]{:S(2)}, u32[]{:S(2)}) collective-permute-start(bf16[2,80,1536]{2,1,0:T(8,128)(2,1)S(1)} %get-tuple-element.71), channel_id=1, source_target_pairs={{0,6},{2,0},{4,2},{6,4},{1,7},{3,1},{5,3},{7,5},{8,14},{10,8},{12,... | collective-permute-start | bytes 1474568 | tf_op jit(solution)/shard_map/ppermute | solution.py:186
  56.3 24.3 %collective-permute-start.15 = (bf16[2,80,1536]{2,1,0:T(8,128)(2,1)S(1)}, bf16[2,80,1536]{2,1,0:T(8,128)(2,1)S(1)}, u32[]{:S(2)}, u32[]{:S(2)}) collective-permute-start(bf16[2,80,1536]{2,1,0:T(8,128)(2,1)S(1)} %get-tuple-element.83), channel_id=1, source_target_pairs={{0,2},{2,4},{4,6},{6,0},{1,3},{3,5},{5,7},{7,1},{8,10},{10,12},{12... | collective-permute-start | bytes 1474568 | tf_op jit(solution)/shard_map/ppermute | solution.py:186
  56.4 25.8 %collective-permute-start.16 = (bf16[2,80,1536]{2,1,0:T(8,128)(2,1)S(1)}, bf16[2,80,1536]{2,1,0:T(8,128)(2,1)S(1)}, u32[]{:S(2)}, u32[]{:S(2)}) collective-permute-start(bf16[2,80,1536]{2,1,0:T(8,128)(2,1)S(1)} %get-tuple-element.84), channel_id=1, source_target_pairs={{0,4},{2,6},{4,0},{6,2},{1,5},{3,7},{5,1},{7,3},{8,12},{10,14},{12... | collective-permute-start | bytes 1474568 | tf_op jit(solution)/shard_map/ppermute | solution.py:186
  57.4 24.8 %collective-permute-start.17 = (bf16[2,80,1536]{2,1,0:T(8,128)(2,1)S(1)}, bf16[2,80,1536]{2,1,0:T(8,128)(2,1)S(1)}, u32[]{:S(2)}, u32[]{:S(2)}) collective-permute-start(bf16[2,80,1536]{2,1,0:T(8,128)(2,1)S(1)} %get-tuple-element.85), channel_id=1, source_target_pairs={{0,6},{2,0},{4,2},{6,4},{1,7},{3,1},{5,3},{7,5},{8,14},{10,8},{12,... | collective-permute-start | bytes 1474568 | tf_op jit(solution)/shard_map/ppermute | solution.py:186
  59.9 5.7 %collective-permute-start.9 = (bf16[2,80,384]{2,1,0:T(8,128)(2,1)S(1)}, bf16[2,80,384]{2,1,0:T(8,128)(2,1)S(1)}, u32[]{:S(2)}, u32[]{:S(2)}) collective-permute-start(bf16[2,80,384]{2,1,0:T(8,128)(2,1)S(1)} %get-tuple-element.77), channel_id=1, source_target_pairs={{0,8},{8,16},{16,24},{24,0},{1,9},{9,17},{17,25},{25,1},{2,10},{10... | collective-permute-start | bytes 368648 | tf_op jit(solution)/shard_map/ppermute | solution.py:186
  60.7 11.2 %collective-permute-start.10 = (bf16[2,80,384]{2,1,0:T(8,128)(2,1)S(1)}, bf16[2,80,384]{2,1,0:T(8,128)(2,1)S(1)}, u32[]{:S(2)}, u32[]{:S(2)}) collective-permute-start(bf16[2,80,384]{2,1,0:T(8,128)(2,1)S(1)} %get-tuple-element.78), channel_id=1, source_target_pairs={{0,16},{8,24},{16,0},{24,8},{1,17},{9,25},{17,1},{25,9},{2,18},{10... | collective-permute-start | bytes 368648 | tf_op jit(solution)/shard_map/ppermute | solution.py:186
  65.6 6.4 %collective-permute-start.11 = (bf16[2,80,384]{2,1,0:T(8,128)(2,1)S(1)}, bf16[2,80,384]{2,1,0:T(8,128)(2,1)S(1)}, u32[]{:S(2)}, u32[]{:S(2)}) collective-permute-start(bf16[2,80,384]{2,1,0:T(8,128)(2,1)S(1)} %get-tuple-element.79), channel_id=1, source_target_pairs={{0,24},{8,0},{16,8},{24,16},{1,25},{9,1},{17,9},{25,17},{2,26},{10... | collective-permute-start | bytes 368648 | tf_op jit(solution)/shard_map/ppermute | solution.py:186
  72.1 11.0 %collective-permute-start.12 = (bf16[2,80,384]{2,1,0:T(8,128)(2,1)S(1)}, bf16[2,80,384]{2,1,0:T(8,128)(2,1)S(1)}, u32[]{:S(2)}, u32[]{:S(2)}) collective-permute-start(bf16[2,80,384]{2,1,0:T(8,128)(2,1)S(1)} %get-tuple-element.81.refs_1_), channel_id=1, source_target_pairs={{0,8},{8,16},{16,24},{24,0},{1,9},{9,17},{17,25},{25,1},{2,10},{10... | collective-permute-start | bytes 368648 | tf_op jit(solution)/shard_map/ppermute | solution.py:186
  74.0 10.4 %collective-permute-start.13 = (bf16[2,80,384]{2,1,0:T(8,128)(2,1)S(1)}, bf16[2,80,384]{2,1,0:T(8,128)(2,1)S(1)}, u32[]{:S(2)}, u32[]{:S(2)}) collective-permute-start(bf16[2,80,384]{2,1,0:T(8,128)(2,1)S(1)} %get-tuple-element.81.refs_1_), channel_id=1, source_target_pairs={{0,16},{8,24},{16,0},{24,8},{1,17},{9,25},{17,1},{25,9},{2,18},{10... | collective-permute-start | bytes 368648 | tf_op jit(solution)/shard_map/ppermute | solution.py:186
  80.5 6.2 %collective-permute-start.14 = (bf16[2,80,384]{2,1,0:T(8,128)(2,1)S(1)}, bf16[2,80,384]{2,1,0:T(8,128)(2,1)S(1)}, u32[]{:S(2)}, u32[]{:S(2)}) collective-permute-start(bf16[2,80,384]{2,1,0:T(8,128)(2,1)S(1)} %get-tuple-element.81.refs_1_), channel_id=1, source_target_pairs={{0,24},{8,0},{16,8},{24,16},{1,25},{9,1},{17,9},{25,17},{2,26},{10... | collective-permute-start | bytes 368648 | tf_op jit(solution)/shard_map/ppermute | solution.py:186
  83.0 10.6 %collective-permute-start.21 = (bf16[2,80,384]{2,1,0:T(8,128)(2,1)S(1)}, bf16[2,80,384]{2,1,0:T(8,128)(2,1)S(1)}, u32[]{:S(2)}, u32[]{:S(2)}) collective-permute-start(bf16[2,80,384]{2,1,0:T(8,128)(2,1)S(1)} %get-tuple-element.90), channel_id=1, source_target_pairs={{0,8},{8,16},{16,24},{24,0},{1,9},{9,17},{17,25},{25,1},{2,10},{10... | collective-permute-start | bytes 368648 | tf_op jit(solution)/shard_map/ppermute | solution.py:186
  87.4 25.6 %collective-permute-start.18 = (bf16[2,80,1536]{2,1,0:T(8,128)(2,1)S(1)}, bf16[2,80,1536]{2,1,0:T(8,128)(2,1)S(1)}, u32[]{:S(2)}, u32[]{:S(2)}) collective-permute-start(bf16[2,80,1536]{2,1,0:T(8,128)(2,1)S(1)} %get-tuple-element.88.refs_1_), channel_id=1, source_target_pairs={{0,2},{2,4},{4,6},{6,0},{1,3},{3,5},{5,7},{7,1},{8,10},{10,12},{12... | collective-permute-start | bytes 1474568 | tf_op jit(solution)/shard_map/ppermute | solution.py:186
  87.5 25.5 %collective-permute-start.19 = (bf16[2,80,1536]{2,1,0:T(8,128)(2,1)S(1)}, bf16[2,80,1536]{2,1,0:T(8,128)(2,1)S(1)}, u32[]{:S(2)}, u32[]{:S(2)}) collective-permute-start(bf16[2,80,1536]{2,1,0:T(8,128)(2,1)S(1)} %get-tuple-element.88.refs_1_), channel_id=1, source_target_pairs={{0,4},{2,6},{4,0},{6,2},{1,5},{3,7},{5,1},{7,3},{8,12},{10,14},{12... | collective-permute-start | bytes 1474568 | tf_op jit(solution)/shard_map/ppermute | solution.py:186
  87.7 25.3 %collective-permute-start.20 = (bf16[2,80,1536]{2,1,0:T(8,128)(2,1)S(1)}, bf16[2,80,1536]{2,1,0:T(8,128)(2,1)S(1)}, u32[]{:S(2)}, u32[]{:S(2)}) collective-permute-start(bf16[2,80,1536]{2,1,0:T(8,128)(2,1)S(1)} %get-tuple-element.88.refs_1_), channel_id=1, source_target_pairs={{0,6},{2,0},{4,2},{6,4},{1,7},{3,1},{5,3},{7,5},{8,14},{10,8},{12,... | collective-permute-start | bytes 1474568 | tf_op jit(solution)/shard_map/ppermute | solution.py:186
  90.1 6.6 %collective-permute-start.22 = (bf16[2,80,384]{2,1,0:T(8,128)(2,1)S(1)}, bf16[2,80,384]{2,1,0:T(8,128)(2,1)S(1)}, u32[]{:S(2)}, u32[]{:S(2)}) collective-permute-start(bf16[2,80,384]{2,1,0:T(8,128)(2,1)S(1)} %get-tuple-element.91), channel_id=1, source_target_pairs={{0,16},{8,24},{16,0},{24,8},{1,17},{9,25},{17,1},{25,9},{2,18},{10... | collective-permute-start | bytes 368648 | tf_op jit(solution)/shard_map/ppermute | solution.py:186
  99.3 7.2 %collective-permute-start.24 = (bf16[2,80,384]{2,1,0:T(8,128)(2,1)S(1)}, bf16[2,80,384]{2,1,0:T(8,128)(2,1)S(1)}, u32[]{:S(2)}, u32[]{:S(2)}) collective-permute-start(bf16[2,80,384]{2,1,0:T(8,128)(2,1)S(1)} %get-tuple-element.94.refs_1_), channel_id=1, source_target_pairs={{0,8},{8,16},{16,24},{24,0},{1,9},{9,17},{17,25},{25,1},{2,10},{10... | collective-permute-start | bytes 368648 | tf_op jit(solution)/shard_map/ppermute | solution.py:186
  102.8 10.1 %collective-permute-start.25 = (bf16[2,80,384]{2,1,0:T(8,128)(2,1)S(1)}, bf16[2,80,384]{2,1,0:T(8,128)(2,1)S(1)}, u32[]{:S(2)}, u32[]{:S(2)}) collective-permute-start(bf16[2,80,384]{2,1,0:T(8,128)(2,1)S(1)} %get-tuple-element.94.refs_1_), channel_id=1, source_target_pairs={{0,16},{8,24},{16,0},{24,8},{1,17},{9,25},{17,1},{25,9},{2,18},{10... | collective-permute-start | bytes 368648 | tf_op jit(solution)/shard_map/ppermute | solution.py:186
  106.5 6.5 %collective-permute-start.26 = (bf16[2,80,384]{2,1,0:T(8,128)(2,1)S(1)}, bf16[2,80,384]{2,1,0:T(8,128)(2,1)S(1)}, u32[]{:S(2)}, u32[]{:S(2)}) collective-permute-start(bf16[2,80,384]{2,1,0:T(8,128)(2,1)S(1)} %get-tuple-element.94.refs_1_), channel_id=1, source_target_pairs={{0,24},{8,0},{16,8},{24,16},{1,25},{9,1},{17,9},{25,17},{2,26},{10... | collective-permute-start | bytes 368648 | tf_op jit(solution)/shard_map/ppermute | solution.py:186
  115.9 7.7 %collective-permute-start.27 = (bf16[4,2,40,768]{3,2,1,0:T(8,128)(2,1)S(1)}, bf16[4,2,40,768]{3,2,1,0:T(8,128)(2,1)S(1)}, u32[]{:S(2)}, u32[]{:S(2)}) collective-permute-start(bf16[4,2,40,768]{3,2,1,0:T(8,128)(2,1)S(1)} %get-tuple-element.98), channel_id=1, source_target_pairs={{0,32},{32,0},{1,33},{33,1},{2,34},{34,2},{3,35},{35,3},{4,36},{36... | collective-permute-start | bytes 1474568 | tf_op jit(solution)/shard_map/ppermute | solution.py:190
  117.8 15.5 %collective-permute-start.31 = (bf16[2,80,1536]{2,1,0:T(8,128)(2,1)S(1)}, bf16[2,80,1536]{2,1,0:T(8,128)(2,1)S(1)}, u32[]{:S(2)}, u32[]{:S(2)}) collective-permute-start(bf16[2,80,1536]{2,1,0:T(8,128)(2,1)S(1)} %get-tuple-element.110.refs_1_), channel_id=1, source_target_pairs={{0,2},{2,4},{4,6},{6,0},{1,3},{3,5},{5,7},{7,1},{8,10},{10,12},{12... | collective-permute-start | bytes 1474568 | tf_op jit(solution)/shard_map/ppermute | solution.py:186
  117.8 24.8 %collective-permute-start.32 = (bf16[2,80,1536]{2,1,0:T(8,128)(2,1)S(1)}, bf16[2,80,1536]{2,1,0:T(8,128)(2,1)S(1)}, u32[]{:S(2)}, u32[]{:S(2)}) collective-permute-start(bf16[2,80,1536]{2,1,0:T(8,128)(2,1)S(1)} %get-tuple-element.110.refs_1_), channel_id=1, source_target_pairs={{0,4},{2,6},{4,0},{6,2},{1,5},{3,7},{5,1},{7,3},{8,12},{10,14},{12... | collective-permute-start | bytes 1474568 | tf_op jit(solution)/shard_map/ppermute | solution.py:186
  120.7 21.9 %collective-permute-start.33 = (bf16[2,80,1536]{2,1,0:T(8,128)(2,1)S(1)}, bf16[2,80,1536]{2,1,0:T(8,128)(2,1)S(1)}, u32[]{:S(2)}, u32[]{:S(2)}) collective-permute-start(bf16[2,80,1536]{2,1,0:T(8,128)(2,1)S(1)} %get-tuple-element.110.refs_1_), channel_id=1, source_target_pairs={{0,6},{2,0},{4,2},{6,4},{1,7},{3,1},{5,3},{7,5},{8,14},{10,8},{12,... | collective-permute-start | bytes 1474568 | tf_op jit(solution)/shard_map/ppermute | solution.py:186
  124.8 7.5 %collective-permute-start.29 = (bf16[2,40,768]{2,1,0:T(8,128)(2,1)S(1)}, bf16[2,40,768]{2,1,0:T(8,128)(2,1)S(1)}, u32[]{:S(2)}, u32[]{:S(2)}) collective-permute-start(bf16[2,40,768]{2,1,0:T(8,128)(2,1)S(1)} %get-tuple-element.106), channel_id=1, source_target_pairs={{0,128},{64,192},{128,0},{192,64},{1,129},{65,193},{129,1},{193,65... | collective-permute-start | bytes 368648 | tf_op jit(solution)/shard_map/ppermute | solution.py:186
  147.7 7.3 %collective-permute-start.35 = (bf16[2,40,768]{2,1,0:T(8,128)(2,1)S(1)}, bf16[2,40,768]{2,1,0:T(8,128)(2,1)S(1)}, u32[]{:S(2)}, u32[]{:S(2)}) collective-permute-start(bf16[2,40,768]{2,1,0:T(8,128)(2,1)S(1)} %get-tuple-element.116), channel_id=1, source_target_pairs={{0,64},{64,128},{128,192},{192,0},{1,65},{65,129},{129,193},{193,1... | collective-permute-start | bytes 368648 | tf_op jit(solution)/shard_map/ppermute | solution.py:186
  148.8 7.8 %collective-permute-start.36 = (bf16[2,40,768]{2,1,0:T(8,128)(2,1)S(1)}, bf16[2,40,768]{2,1,0:T(8,128)(2,1)S(1)}, u32[]{:S(2)}, u32[]{:S(2)}) collective-permute-start(bf16[2,40,768]{2,1,0:T(8,128)(2,1)S(1)} %get-tuple-element.117), channel_id=1, source_target_pairs={{0,128},{64,192},{128,0},{192,64},{1,129},{65,193},{129,1},{193,65... | collective-permute-start | bytes 368648 | tf_op jit(solution)/shard_map/ppermute | solution.py:186
  156.7 10.1 %collective-permute-start.38 = (bf16[2,40,768]{2,1,0:T(8,128)(2,1)S(1)}, bf16[2,40,768]{2,1,0:T(8,128)(2,1)S(1)}, u32[]{:S(2)}, u32[]{:S(2)}) collective-permute-start(bf16[2,40,768]{2,1,0:T(8,128)(2,1)S(1)} %get-tuple-element.124), channel_id=1, source_target_pairs={{0,1},{1,0},{2,3},{3,2},{4,5},{5,4},{6,7},{7,6},{8,9},{9,8},{10,11... | collective-permute-start | bytes 368648 | tf_op jit(solution)/shard_map/ppermute | solution.py:190
  (13 other events, 117.8 us)
